TPU v7x, 32 devices: a whole 2x2x4 slice. The times are simulated.
32 devices in a mesh: leaf: 4 (over y, x), rows: 8 (over z, core).
Axes of the slice: x: 2, y: 2, z: 4, core: 2. Of those that a mesh axis runs over, the one named last changes fastest.
Arguments:
- rhs_top: float32 [1, 4096, 128], P(None, 'rows'), may hold values from -6 to 6
- rhs_one: float32 [2, 2048, 128], P(None, 'rows'), may hold values from -6 to 6
- rhs_two: float32 [4, 2048, 128], P(None, 'rows'), may hold values from -6 to 6
- rhs_three: float32 [8, 1024, 128], P(None, 'rows'), may hold values from -6 to 6
- inv_top: float32 [4096, 4096], P('rows', 'leaf')
- inv_one: float32 [2048, 4096], P('rows', 'leaf')
- inv_two: float32 [2048, 8192], P('rows', 'leaf')
- inv_three: float32 [1024, 8192], P('rows', 'leaf')
- panel_one: float32 [4096, 2048], P('leaf', 'rows'), may hold values from -0.0625 to 0.0625
- panel_two: float32 [8192, 4096], P('leaf', 'rows'), may hold values from -0.0625 to 0.0625
- panel_three: float32 [8192, 4096], P('leaf', 'rows'), may hold values from -0.09375 to 0.09375
- rows_one: int32 [2, 16], P(None, 'rows'), may hold values from 0 to 31, as said below
- rows_two: int32 [4, 32], P(None, 'rows'), may hold values from 0 to 47, as said below
- rows_three: int32 [8, 32], P(None, 'rows'), may hold values from 0 to 63, as said below
Outputs:
- solution_top: float32 [1, 4096, 128], P(None, 'rows')
- solution_one: float32 [2, 2048, 128], P(None, 'rows')
- solution_two: float32 [4, 2048, 128], P(None, 'rows')
- solution_three: float32 [8, 1024, 128], P(None, 'rows')
Inputs may be any that keep to these rules, and one draw needn't show every extreme that they name: `rows_one`: each row lists 16 different blocks of a chain of 32 blocks, the chain's first and last among them. `rows_two`: each row lists 32 different blocks of a chain of 48 blocks, the chain's first and last among them. `rows_three`: each row lists 32 different blocks of a chain of 64 blocks, the chain's first and last among them.
All inputs are finite; a program needn't handle non-finite values.
Results may differ from a plain program's by a relative error of at most 0.0001.
Values sent between devices are 32-bit elements; how exact they have to be, the bound alone decides.
No kernel may reach another device: no remote copies, remote signals or barrier semaphores. Data moves between devices by JAX's collectives and lax.ppermute only.
A program may use at most 128 MiB of HBM per device.

v0:
```python
import jax
import jax.numpy as jnp
from jax import lax
from jax.sharding import PartitionSpec as P

SEP0 = 4096
SEP1 = 2048
SEP2 = 2048
SEP3 = 1024
BLOCK = 128


def layout(sep_count, sep_size):
    span_rows = sep_count * sep_size // lax.axis_size("leaf")
    held_count = max(1, span_rows // sep_size)
    part_rows = min(span_rows, sep_size)
    first_sep = lax.axis_index("leaf") * span_rows // sep_size
    return (held_count, part_rows, first_sep)


def forward_solve(inverse, source, sep_count, sep_size):
    held_count, part_rows, first_sep = layout(sep_count, sep_size)
    picked = lax.dynamic_slice_in_dim(source, first_sep, held_count, 0)
    blocks = inverse.reshape(inverse.shape[0], held_count, part_rows)
    partial_y = jnp.einsum("csr,scn->srn", blocks, picked, precision=lax.Precision.HIGHEST)
    return lax.psum(partial_y, "rows")


def chain_matches(index_rows, first_sep, held_count, chain_count, listed):
    picked_rows = lax.dynamic_slice_in_dim(index_rows, first_sep, held_count, 0)
    column_ids = lax.broadcasted_iota(jnp.int32, (held_count, chain_count, listed), 1)
    return (column_ids == picked_rows[:, None, :]).astype(jnp.float32)


def ancestor_terms(panel, index_rows, solved_rows, sep_sizes, sep_counts, level_at):
    held_count, part_rows, first_sep = layout(sep_counts[level_at], sep_sizes[level_at])
    width_rhs = solved_rows.shape[2]
    listed = panel.shape[1] // BLOCK
    chain_count = sum(sep_sizes[:level_at]) // BLOCK
    panel_cut = panel.reshape(held_count, part_rows, listed * BLOCK)
    updates = jnp.einsum("sra,srn->san", panel_cut, solved_rows, precision=lax.Precision.HIGHEST)
    matches = chain_matches(index_rows, first_sep, held_count, chain_count, listed)
    spread = jnp.einsum(
        "sck,skbn->scbn",
        matches,
        updates.reshape(held_count, listed, BLOCK, width_rhs),
        precision=lax.Precision.HIGHEST,
    )
    owners = first_sep + jnp.arange(held_count, dtype=jnp.int32)
    results = []
    offset = 0
    for upper in range(level_at):
        blocks_up = sep_sizes[upper] // BLOCK
        segment = spread[:, offset : offset + blocks_up].reshape(
            held_count, sep_sizes[upper], width_rhs
        )
        target_ids = lax.broadcasted_iota(jnp.int32, (held_count, sep_counts[upper]), 1)
        target = (target_ids == (owners >> level_at - upper)[:, None]).astype(jnp.float32)
        results.append(jnp.einsum("sq,srn->qrn", target, segment, precision=lax.Precision.HIGHEST))
        offset = offset + blocks_up
    return results


def reduce_dense(parts):
    column_parts = lax.psum_scatter(parts, "rows", scatter_dimension=1, tiled=True)
    return lax.psum(column_parts, "leaf")


def backward_panel(panel, index_rows, gathered, solved_rows, sep_sizes, sep_counts, level_at):
    held_count, part_rows, first_sep = layout(sep_counts[level_at], sep_sizes[level_at])
    width_rhs = solved_rows.shape[2]
    listed = panel.shape[1] // BLOCK
    chain_count = sum(sep_sizes[:level_at]) // BLOCK
    owners = first_sep + jnp.arange(held_count, dtype=jnp.int32)
    pieces = []
    for upper in range(level_at):
        target_ids = lax.broadcasted_iota(jnp.int32, (held_count, sep_counts[upper]), 1)
        target = (target_ids == (owners >> level_at - upper)[:, None]).astype(jnp.float32)
        pieces.append(
            jnp.einsum("sq,qrn->srn", target, gathered[upper], precision=lax.Precision.HIGHEST)
        )
    chain_x = jnp.concatenate(pieces, axis=1).reshape(held_count, chain_count, BLOCK, width_rhs)
    matches = chain_matches(index_rows, first_sep, held_count, chain_count, listed)
    chosen = jnp.einsum("sck,scbn->skbn", matches, chain_x, precision=lax.Precision.HIGHEST)
    panel_cut = panel.reshape(held_count, part_rows, listed * BLOCK)
    partial_g = jnp.einsum(
        "sra,san->srn",
        panel_cut,
        chosen.reshape(held_count, listed * BLOCK, width_rhs),
        precision=lax.Precision.HIGHEST,
    )
    return solved_rows - lax.psum(partial_g, "rows")


def backward_solve(inverse, residue, sep_count, sep_size):
    held_count, part_rows, first_sep = layout(sep_count, sep_size)
    blocks = inverse.reshape(inverse.shape[0], held_count, part_rows)
    partial_x = jnp.einsum("csr,srn->scn", blocks, residue, precision=lax.Precision.HIGHEST)
    owners = first_sep + jnp.arange(held_count, dtype=jnp.int32)
    place_ids = lax.broadcasted_iota(jnp.int32, (held_count, sep_count), 1)
    placing = (place_ids == owners[:, None]).astype(jnp.float32)
    dense = jnp.einsum("sq,scn->qcn", placing, partial_x, precision=lax.Precision.HIGHEST)
    return lax.psum(dense, "leaf")


def body(
    rhs_top,
    rhs_one,
    rhs_two,
    rhs_three,
    inv_top,
    inv_one,
    inv_two,
    inv_three,
    panel_one,
    panel_two,
    panel_three,
    rows_one,
    rows_two,
    rows_three,
):
    sep_sizes = [SEP0, SEP1, SEP2, SEP3]
    sep_counts = [1, 2, 4, 8]
    right_sides = [rhs_top, rhs_one, rhs_two, rhs_three]
    inverses = [inv_top, inv_one, inv_two, inv_three]
    panels = [None, panel_one, panel_two, panel_three]
    indices = [None, rows_one, rows_two, rows_three]
    solved = [None, None, None, None]
    owed_rows = [jnp.zeros(item.shape, jnp.float32) for item in right_sides]
    for level_at in (3, 2, 1, 0):
        source = right_sides[level_at] - owed_rows[level_at]
        solved[level_at] = forward_solve(
            inverses[level_at], source, sep_counts[level_at], sep_sizes[level_at]
        )
        if level_at > 0:
            fresh = ancestor_terms(
                panels[level_at],
                indices[level_at],
                solved[level_at],
                sep_sizes,
                sep_counts,
                level_at,
            )
            reduced = reduce_dense(tuple(fresh))
            for upper in range(level_at):
                owed_rows[upper] = owed_rows[upper] + reduced[upper]
    gathered = []
    results = []
    for level_at in range(4):
        residue = solved[level_at]
        if level_at > 0:
            residue = backward_panel(
                panels[level_at],
                indices[level_at],
                gathered,
                solved[level_at],
                sep_sizes,
                sep_counts,
                level_at,
            )
        solution_cols = backward_solve(
            inverses[level_at], residue, sep_counts[level_at], sep_sizes[level_at]
        )
        results.append(solution_cols)
        if level_at < 3:
            gathered.append(lax.all_gather(solution_cols, "rows", axis=1, tiled=True))
    return (results[0], results[1], results[2], results[3])


def solution(mesh):
    return jax.shard_map(
        body,
        mesh=mesh,
        in_specs=(
            P(None, "rows", None),
            P(None, "rows", None),
            P(None, "rows", None),
            P(None, "rows", None),
            P("rows", "leaf"),
            P("rows", "leaf"),
            P("rows", "leaf"),
            P("rows", "leaf"),
            P("leaf", "rows"),
            P("leaf", "rows"),
            P("leaf", "rows"),
            P(None, "rows"),
            P(None, "rows"),
            P(None, "rows"),
        ),
        out_specs=(
            P(None, "rows", None),
            P(None, "rows", None),
            P(None, "rows", None),
            P(None, "rows", None),
        ),
        check_vma=False,
    )
```

profile of v0, /device:TPU:0, one launch (start us, length us, event | category | flops | bytes accessed | tf_op | source)
XLA Modules:
  0.0 1188.2 jit_solution(17033452079673094226)
XLA Ops:
  11.0 61.4 %all-reduce.19.cloned.1.call-done = f32[2,1024,128]{1,2,0:T(8,128)} async-done(((f32[2,1024,128]{1,2,0:T(8,128)}), f32[2,1024,128]{1,2,0:T(8,128)}) %all-reduce.19.cloned.1.call-update) | async-done | bytes 1048592 | tf_op jit(solution)/shard_map/psum | solution.py:26
  72.4 5.0 convolution_bitcast_fusion.8
  85.9 12.6 %fusion.4 = f32[4,2048,128]{2,0,1:T(4,128)} fusion(f32[2,2048,128]{2,1,0:T(8,128)S(1)} %bitcast.179, s32[2]{0:T(128)S(1)} %broadcast_shift-right-arithmetic_fusion.1), kind=kOutput, calls=%fused_computation.11 | convolution fusion | flops 25165832 | bytes 6291464 | tf_op jit(solution)/shard_map/sq,srn->qrn/dot_general | solution.py:59
  100.4 93.7 %all-reduce.47.cloned.1.call-done = f32[4,2048,128]{2,0,1:T(4,128)} async-done(((f32[4,2048,128]{2,0,1:T(4,128)}), f32[4,2048,128]{2,0,1:T(4,128)}) %all-reduce.47.cloned.1.call-update) | async-done | bytes 4194320
  197.0 46.1 %all-reduce.21.cloned.1.call-done = f32[4,256,128]{2,0,1:T(4,128)} async-done(((f32[4,256,128]{2,0,1:T(4,128)}), f32[4,256,128]{2,0,1:T(4,128)}) %all-reduce.21.cloned.1.call-update) | async-done | bytes 524304 | tf_op jit(solution)/shard_map/psum | solution.py:66
  251.2 54.4 %all-reduce.23.cloned.1.call-done = f32[1,2048,128]{1,2,0:T(8,128)} async-done(((f32[1,2048,128]{1,2,0:T(8,128)}), f32[1,2048,128]{1,2,0:T(8,128)}) %all-reduce.23.cloned.1.call-update) | async-done | bytes 1048592 | tf_op jit(solution)/shard_map/psum | solution.py:26
  305.5 4.9 convolution_bitcast_fusion.9
  315.0 12.8 %multiply_add_fusion = f32[2,2048,128]{2,0,1:T(2,128)} fusion(f32[2,2048,128]{2,1,0:T(8,128)S(1)} %bitcast.190, f32[2048,128]{1,0:T(8,128)S(1)} %bitcast.193, f32[2]{0:T(128)S(1)} %fusion.54, s32[2]{0:T(128)S(1)} %broadcast_shift-right-arithmetic_fusion), kind=kOutput, calls=%fused_computation.16 | convolution fusion | flops 13631492 | bytes 5242896 | tf_op jit(solution)/shard_map/sq,srn->qrn/dot_general | solution.py:59
  332.7 4.4 copy.72
  337.1 54.7 %all-reduce.49.cloned.1.call-done = f32[2,2048,128]{2,0,1:T(2,128)} async-done(((f32[2,2048,128]{2,0,1:T(2,128)}), f32[2,2048,128]{2,0,1:T(2,128)}) %all-reduce.49.cloned.1.call-update) | async-done | bytes 2097168
  393.6 20.2 %fusion.2 = f32[1,4096,128]{2,0,1:T(1,128)} fusion(f32[2,4096,128]{2,1,0:T(8,128)} %bitcast.187, s32[]{:T(128)S(6)} %select_n.41), kind=kOutput, calls=%fused_computation.3 | convolution fusion | flops 12582918 | bytes 6291460 | tf_op jit(solution)/shard_map/sq,srn->qrn/dot_general | solution.py:59
  413.8 24.0 %all-reduce.43.cloned.1.call-done = f32[2,256,128]{2,0,1:T(2,128)} async-done(((f32[2,256,128]{2,0,1:T(2,128)}), f32[2,256,128]{2,0,1:T(2,128)}) %all-reduce.43.cloned.1.call-update) | async-done | bytes 262160 | tf_op jit(solution)/shard_map/psum | solution.py:66
  446.6 51.5 %all-reduce.25.cloned.1.call-done = f32[1,1024,128]{1,2,0:T(8,128)} async-done(((f32[1,1024,128]{1,2,0:T(8,128)}), f32[1,1024,128]{1,2,0:T(8,128)}) %all-reduce.25.cloned.1.call-update) | async-done | bytes 524304 | tf_op jit(solution)/shard_map/psum | solution.py:26
  505.8 34.8 %reduce-scatter.2.cloned.1.call-done = f32[1,512,128]{2,1,0:T(8,128)} async-done(((f32[1,4096,128]{2,1,0:T(8,128)}), f32[1,512,128]{2,1,0:T(8,128)}) %reduce-scatter.2.cloned.1.call-update) | async-done | bytes 262160 | tf_op jit(solution)/shard_map/reduce_scatter | solution.py:65
  540.7 44.4 %all-reduce.45.cloned.1.call-done = f32[1,512,128]{2,1,0:T(8,128)} async-done(((f32[1,512,128]{2,1,0:T(8,128)}), f32[1,512,128]{2,1,0:T(8,128)}) %all-reduce.45.cloned.1.call-update) | async-done | bytes 262160 | tf_op jit(solution)/shard_map/psum | solution.py:66
  589.0 56.3 %all-reduce.27.cloned.1.call-done = f32[1024,128]{0,1:T(8,128)} async-done(((f32[1024,128]{0,1:T(8,128)}), f32[1024,128]{0,1:T(8,128)}) %all-reduce.27.cloned.1.call-update) | async-done | bytes 524304 | tf_op jit(solution)/shard_map/psum | solution.py:26
  645.3 4.7 fusion.10
  650.1 42.0 %all-reduce.29.cloned.1.call-done = f32[1,512,128]{1,2,0:T(8,128)} async-done(((f32[1,512,128]{1,2,0:T(8,128)}), f32[1,512,128]{1,2,0:T(8,128)}) %all-reduce.29.cloned.1.call-update) | async-done | bytes 262160 | tf_op jit(solution)/shard_map/psum | solution.py:103
  692.2 30.6 %all-gather.4.cloned.1.call-done = f32[1,4096,128]{1,2,0:T(8,128)} async-done(((f32[1,512,128]{1,2,0:T(8,128)}), f32[1,4096,128]{1,2,0:T(8,128)}) %all-gather.4.cloned.1.call-update) | async-done | bytes 2097168 | tf_op jit(solution)/shard_map/all_gather | solution.py:166
  734.3 55.6 %all-reduce.31.cloned.1.call-done = f32[1,1024,128]{1,2,0:T(8,128)} async-done(((f32[1,1024,128]{1,2,0:T(8,128)}), f32[1,1024,128]{1,2,0:T(8,128)}) %all-reduce.31.cloned.1.call-update) | async-done | bytes 524304 | tf_op jit(solution)/shard_map/psum | solution.py:92
  793.6 42.0 %all-reduce.33.cloned.1.call-done = f32[2,256,128]{2,0,1:T(2,128)} async-done(((f32[2,256,128]{2,0,1:T(2,128)}), f32[2,256,128]{2,0,1:T(2,128)}) %all-reduce.33.cloned.1.call-update) | async-done | bytes 262160 | tf_op jit(solution)/shard_map/psum | solution.py:103
  838.9 27.5 %all-gather.6.cloned.1.call-done = f32[2,2048,128]{2,0,1:T(2,128)} async-done(((f32[2,256,128]{2,0,1:T(2,128)}), f32[2,2048,128]{2,0,1:T(2,128)}) %all-gather.6.cloned.1.call-update) | async-done | bytes 2097168 | tf_op jit(solution)/shard_map/all_gather | solution.py:166
  866.3 6.7 fusion.48
  886.0 7.8 convolution_bitcast_fusion
  894.1 58.3 %all-reduce.35.cloned.1.call-done = f32[1,2048,128]{1,2,0:T(8,128)} async-done(((f32[1,2048,128]{1,2,0:T(8,128)}), f32[1,2048,128]{1,2,0:T(8,128)}) %all-reduce.35.cloned.1.call-update) | async-done | bytes 1048592 | tf_op jit(solution)/shard_map/psum | solution.py:92
  956.9 44.4 %all-reduce.37.cloned.1.call-done = f32[4,256,128]{2,0,1:T(4,128)} async-done(((f32[4,256,128]{2,0,1:T(4,128)}), f32[4,256,128]{2,0,1:T(4,128)}) %all-reduce.37.cloned.1.call-update) | async-done | bytes 524304 | tf_op jit(solution)/shard_map/psum | solution.py:103
  1014.1 35.9 %all-gather.8.cloned.1.call-done = f32[4,2048,128]{2,0,1:T(4,128)} async-done(((f32[4,256,128]{2,0,1:T(4,128)}), f32[4,2048,128]{2,0,1:T(4,128)}) %all-gather.8.cloned.1.call-update) | async-done | bytes 4194320 | tf_op jit(solution)/shard_map/all_gather | solution.py:166
  1050.0 6.4 fusion.44
  1059.5 7.7 fusion
  1067.2 5.6 convolution_bitcast_fusion.3
  1072.9 57.6 %all-reduce.39.cloned.1.call-done = f32[2,1024,128]{1,2,0:T(8,128)} async-done(((f32[2,1024,128]{1,2,0:T(8,128)}), f32[2,1024,128]{1,2,0:T(8,128)}) %all-reduce.39.cloned.1.call-update) | async-done | bytes 1048592 | tf_op jit(solution)/shard_map/psum | solution.py:92
  1137.0 42.1 %all-reduce.41.cloned.1.call-done = f32[8,128,128]{2,0,1:T(8,128)} async-done(((f32[8,128,128]{2,0,1:T(8,128)}), f32[8,128,128]{2,0,1:T(8,128)}) %all-reduce.41.cloned.1.call-update) | async-done | bytes 524304 | tf_op jit(solution)/shard_map/psum | solution.py:103
  (162 shorter events, 116.3 us)
Async XLA Ops:
  7.2 237.2 %copy-start = (f32[256,2048]{1,0:T(8,128)S(1)}, f32[256,2048]{1,0:T(8,128)}, u32[]{:S(2)}) copy-start(f32[256,2048]{1,0:T(8,128)} %param.20) | copy-start | bytes 6291460
  7.2 3.6 copy-start.18
  7.2 65.2 %all-reduce.19.cloned.1.call-start = ((), (), s32[]{:S(2)}) async-start(), calls=%async_computation.1 | async-start | bytes 2097152 | tf_op jit(solution)/shard_map/psum | solution.py:26
  10.7 183.4 %all-reduce.47.cloned.1.call-start = ((), (), s32[]{:S(2)}) async-start(), calls=%async_computation.19 | async-start | bytes 8388608
  81.4 3.9 copy-start.1
  98.5 144.6 %all-reduce.21.cloned.1.call-start = ((), (), s32[]{:S(2)}) async-start(), calls=%async_computation.2 | async-start | bytes 1048576 | tf_op jit(solution)/shard_map/psum | solution.py:66
  196.0 109.5 %all-reduce.23.cloned.1.call-start = ((), (), s32[]{:S(2)}) async-start(), calls=%async_computation.3 | async-start | bytes 2097152 | tf_op jit(solution)/shard_map/psum | solution.py:26
  246.6 145.2 %all-reduce.49.cloned.1.call-start = ((), (), s32[]{:S(2)}) async-start(), calls=%async_computation.20 | async-start | bytes 4194304
  246.8 67.1 %copy-start.19 = (s32[2]{0:T(128)}, s32[2]{0:T(128)S(1)}, u32[]{:S(2)}) copy-start(s32[2]{0:T(128)S(1)} %broadcast_shift-right-arithmetic_fusion) | copy-start | bytes 28
  327.9 110.0 %all-reduce.43.cloned.1.call-start = ((), (), s32[]{:S(2)}) async-start(), calls=%async_computation.16 | async-start | bytes 524288 | tf_op jit(solution)/shard_map/psum | solution.py:66
  393.5 104.5 %all-reduce.25.cloned.1.call-start = ((), (), s32[]{:S(2)}) async-start(), calls=%async_computation.4 | async-start | bytes 1048576 | tf_op jit(solution)/shard_map/psum | solution.py:26
  441.7 99.0 %reduce-scatter.2.cloned.1.call-start = ((), (), s32[]{:S(2)}) async-start(), calls=%async_computation.18 | async-start | bytes 2359296 | tf_op jit(solution)/shard_map/reduce_scatter | solution.py:65
  505.8 79.4 %copy-start.16 = (f32[1,512,128]{2,1,0:T(8,128)S(1)}, f32[1,512,128]{2,1,0:T(8,128)}, u32[]{:S(2)}) copy-start(f32[1,512,128]{2,1,0:T(8,128)} %param.14) | copy-start | bytes 786436
  505.8 79.4 %all-reduce.45.cloned.1.call-start = ((), (), s32[]{:S(2)}) async-start(), calls=%async_computation.17 | async-start | bytes 524288 | tf_op jit(solution)/shard_map/psum | solution.py:66
  540.7 104.6 %all-reduce.27.cloned.1.call-start = ((), (), s32[]{:S(2)}) async-start(), calls=%async_computation.5 | async-start | bytes 1048576 | tf_op jit(solution)/shard_map/psum | solution.py:26
  589.0 103.1 %all-reduce.29.cloned.1.call-start = ((), (), s32[]{:S(2)}) async-start(), calls=%async_computation.6 | async-start | bytes 524288 | tf_op jit(solution)/shard_map/psum | solution.py:103
  650.0 72.7 %all-gather.4.cloned.1.call-start = ((), (), s32[]{:S(2)}) async-start(), calls=%async_computation.7 | async-start | bytes 2359296 | tf_op jit(solution)/shard_map/all_gather | solution.py:166
  692.1 97.8 %all-reduce.31.cloned.1.call-start = ((), (), s32[]{:S(2)}) async-start(), calls=%async_computation.8 | async-start | bytes 1048576 | tf_op jit(solution)/shard_map/psum | solution.py:92
  734.1 101.5 %all-reduce.33.cloned.1.call-start = ((), (), s32[]{:S(2)}) async-start(), calls=%async_computation.9 | async-start | bytes 524288 | tf_op jit(solution)/shard_map/psum | solution.py:103
  793.6 72.7 %all-gather.6.cloned.1.call-start = ((), (), s32[]{:S(2)}) async-start(), calls=%async_computation.10 | async-start | bytes 2359296 | tf_op jit(solution)/shard_map/all_gather | solution.py:166
  835.7 116.7 %all-reduce.35.cloned.1.call-start = ((), (), s32[]{:S(2)}) async-start(), calls=%async_computation.11 | async-start | bytes 2097152 | tf_op jit(solution)/shard_map/psum | solution.py:92
  886.0 66.4 %copy-start.9 = (f32[1,2048,128]{1,2,0:T(8,128)S(1)}, f32[1,2048,128]{1,2,0:T(8,128)}, u32[]{:S(2)}) copy-start(f32[1,2048,128]{1,2,0:T(8,128)} %all-reduce.23.cloned.1.call-done) | copy-start | bytes 3145732
  893.8 107.5 %all-reduce.37.cloned.1.call-start = ((), (), s32[]{:S(2)}) async-start(), calls=%async_computation.12 | async-start | bytes 1048576 | tf_op jit(solution)/shard_map/psum | solution.py:103
  956.8 93.2 %all-gather.8.cloned.1.call-start = ((), (), s32[]{:S(2)}) async-start(), calls=%async_computation.13 | async-start | bytes 4718592 | tf_op jit(solution)/shard_map/all_gather | solution.py:166
  1001.3 129.1 %all-reduce.39.cloned.1.call-start = ((), (), s32[]{:S(2)}) async-start(), calls=%async_computation.14 | async-start | bytes 2097152 | tf_op jit(solution)/shard_map/psum | solution.py:92
  1004.3 4.1 copy-start.10
  1004.3 4.1 copy-start.20
  1050.0 6.6 copy-start.6
  1059.5 7.7 copy-start.2
  1067.2 63.2 %copy-start.7 = (f32[128,2048]{1,0:T(8,128)S(1)}, f32[128,2048]{1,0:T(8,128)}, u32[]{:S(2)}) copy-start(f32[128,2048]{1,0:T(8,128)} %param.21) | copy-start | bytes 3145732
  1072.8 106.2 %all-reduce.41.cloned.1.call-start = ((), (), s32[]{:S(2)}) async-start(), calls=%async_computation.15 | async-start | bytes 1048576 | tf_op jit(solution)/shard_map/psum | solution.py:103
  1072.9 61.7 %copy-start.14 = (f32[1,512,128]{1,2,0:T(8,128)S(1)}, f32[1,512,128]{1,2,0:T(8,128)}, u32[]{:S(2)}) copy-start(f32[1,512,128]{1,2,0:T(8,128)} %all-reduce.29.cloned.1.call-done) | copy-start | bytes 786436
  (12 other events, 25.0 us)
Sparse Core Ops, SparseCore 0:
  10.9 61.4 all-reduce.18
  98.6 95.4 all-reduce.46
  197.7 45.3 all-reduce.20
  246.7 58.7 all-reduce.22
  328.0 63.8 all-reduce.48
  395.2 42.5 all-reduce.42
  441.8 56.1 all-reduce.24
  505.9 34.7 reduce-scatter.1
  543.6 41.5 all-reduce.44
  589.1 56.1 all-reduce.26
  650.2 41.8 all-reduce.28
  693.6 29.0 all-gather.3
  734.2 55.6 all-reduce.30
  793.7 41.8 all-reduce.32
  837.2 29.0 all-gather.5
  893.9 58.3 all-reduce.34
  957.0 44.2 all-reduce.36
  1002.8 47.1 all-gather.7
  1072.9 57.4 all-reduce.38
  1134.7 44.2 all-reduce.40
where the time goes:
time: 1200 us; the launch traced here: 1190 us
  waiting for transfers between devices  958 us (80%)
  matrix products  137 us (11%)
  local copies, waits for them, and re-layouts  56.4 us (5%)
  other arithmetic  19.3 us (2%)
  between operations  16 us (1%)
    psum x4, waiting for transfers between devices, forward_solve(): return lax.psum(partial_y, 'rows')  224 us
    psum x3, waiting for transfers between devices, backward_panel(): return solved_rows - lax.psum(partial_g, 'rows')  171 us
    psum x4, waiting for transfers between devices, backward_solve(): return lax.psum(dense, 'leaf')  170 us
    unnamed x22, waiting for transfers between devices  149 us
    psum x3, waiting for transfers between devices, reduce_dense(): return lax.psum(column_parts, 'leaf')  115 us
    all_gather x3, waiting for transfers between devices, body(): gathered.append(lax.all_gather(solution_cols, 'rows', axis=1, tiled=True))  93.9 us
    dot_general x3, matrix products, ancestor_terms(): jnp.einsum('sq,srn->qrn', target, segment, precision=lax.Precision.HIGHEST)  45.6 us
    reduce_scatter x1, waiting for transfers between devices, reduce_dense(): lax.psum_scatter(parts, 'rows', scatter_dimension=1, tiled=True)  34.8 us
  transfers between devices with their start and end apart: 20, of which 20 were waited for; matrix products, arithmetic and copies ran while one was open for 5% of the time, Pallas kernels for 0%

commit v1 on v0

v1 whole, which is shorter than its diff:
```python
import functools

import jax
import jax.numpy as jnp
from jax import lax
from jax.experimental import pallas as pl
from jax.experimental.pallas import tpu as pltpu
from jax.sharding import PartitionSpec as P

BLOCK = 128
F32 = jnp.float32
BF16 = jnp.bfloat16
VMEM = pl.BlockSpec(memory_space=pltpu.VMEM)
SMEM = pl.BlockSpec(memory_space=pltpu.SMEM)
LIMIT = 40 * 1024 * 1024


def cut(x):
    high = x.astype(BF16)
    return high, (x - high.astype(F32)).astype(BF16)


def wide(x):
    return jnp.concatenate(cut(x), axis=1)


def product(dims, a, xw):
    n = xw.shape[1] // 2
    high, low = cut(a)
    first = lax.dot_general(high, xw, (dims, ((), ())), preferred_element_type=F32)
    second = lax.dot_general(low, xw[:, :n], (dims, ((), ())), preferred_element_type=F32)
    return first[:, :n] + (first[:, n:] + second)


times = functools.partial(product, ((1,), (0,)))
transposed_times = functools.partial(product, ((0,), (0,)))


def tile_of(rows, largest=512):
    return min(rows, largest)


def spread_parts(meta, full, own, other, offset=0):
    rows = own[0].shape[0]
    for k in range(len(own)):
        chunk = 2 * jnp.bitwise_xor(meta[0], k)
        full[pl.ds(pl.multiple_of(offset + (chunk + meta[1]) * rows, 8), rows), :] = own[k][...]
        full[pl.ds(pl.multiple_of(offset + (chunk + 1 - meta[1]) * rows, 8), rows), :] = other[k][...]


def split_cores(meta, full, offset, keep, send):
    count, rows = keep.shape[0], keep.shape[1]
    for k in range(count):
        keep[k] = full[pl.ds(pl.multiple_of(offset + (2 * k + meta[1]) * rows, 8), rows), :]
        send[k] = full[pl.ds(pl.multiple_of(offset + (2 * k + 1 - meta[1]) * rows, 8), rows), :]


def forward_inv_kernel(owed_count, meta, rhs, *refs):
    owed, (inv, keep, send, full) = refs[:owed_count], refs[owed_count:]
    held = rhs.shape[0]
    part = inv.shape[1] // held
    tile = tile_of(part)
    for h in range(held):
        source = rhs[h]
        for item in owed:
            source = source - item[...]
        source = wide(source)
        for start in range(h * part, (h + 1) * part, tile):
            full[start : start + tile, :] = transposed_times(inv[:, start : start + tile], source)
    split_cores(meta, full, 0, keep, send)


def forward_panel_kernel(nz, has_before, cut_at, meta, rows, *refs):
    own, other, refs = refs[:nz], refs[nz : 2 * nz], refs[2 * nz :]
    if has_before:
        before, refs = refs[0], refs[1:]
    panel, keep, send, chain, full = refs
    held, listed = rows.shape
    part = panel.shape[0] // held
    tile = tile_of(part)
    spread_parts(meta, full, own, other)
    if has_before:
        chain[...] = before[: chain.shape[0], :]
    else:
        chain[...] = jnp.zeros_like(chain)
    for h in range(held):
        update = None
        for start in range(h * part, (h + 1) * part, tile):
            term = transposed_times(panel[start : start + tile, :], wide(full[start : start + tile, :]))
            update = term if update is None else update + term
        for k in range(listed):
            place = pl.ds(pl.multiple_of(rows[h, k] * BLOCK, BLOCK), BLOCK)
            chain[place, :] = chain[place, :] + update[k * BLOCK : (k + 1) * BLOCK]
    split_cores(meta, chain, cut_at, keep, send)


def backward_panel_kernel(nz, has_before, meta, rows, *refs):
    own, other, refs = refs[:nz], refs[nz : 2 * nz], refs[2 * nz :]
    offset = 0
    if has_before:
        before, refs = refs[0], refs[1:]
        offset = before.shape[0]
    panel, keep, send, chain, chosen, full = refs
    held, listed = rows.shape
    part = panel.shape[0] // held
    tile = tile_of(part)
    if has_before:
        chain[:offset, :] = before[...]
    spread_parts(meta, chain, own, other, offset)
    for h in range(held):
        for k in range(listed):
            place = pl.ds(pl.multiple_of(rows[h, k] * BLOCK, BLOCK), BLOCK)
            chosen[k * BLOCK : (k + 1) * BLOCK, :] = wide(chain[place, :])
        for start in range(h * part, (h + 1) * part, tile):
            full[start : start + tile, :] = times(panel[start : start + tile, :], chosen[...])
    split_cores(meta, full, 0, keep, send)


def backward_inv_kernel(nz, meta, *refs):
    own, other, (inv, solved, full) = refs[:nz], refs[nz : 2 * nz], refs[2 * nz :]
    held = solved.shape[0]
    part = inv.shape[1] // held
    tile = tile_of(part)
    spread_parts(meta, full, own, other)
    for h in range(held):
        total = None
        for start in range(h * part, (h + 1) * part, tile):
            term = times(inv[:, start : start + tile], wide(full[start : start + tile, :]))
            total = term if total is None else total + term
        solved[h] = total


def call(kernel, name, out_shapes, scratch, flops, smem_count, *operands):
    single = not isinstance(out_shapes, (list, tuple))
    outs = [out_shapes] if single else list(out_shapes)
    moved = sum(item.size * 4 for item in operands) + sum(item.size * 4 for item in outs)
    result = pl.pallas_call(
        kernel,
        out_shape=outs,
        in_specs=[SMEM] * smem_count + [VMEM] * (len(operands) - smem_count),
        out_specs=[VMEM] * len(outs),
        scratch_shapes=scratch,
        compiler_params=pltpu.CompilerParams(vmem_limit_bytes=LIMIT),
        cost_estimate=pl.CostEstimate(flops=flops, bytes_accessed=moved, transcendentals=0),
        name=name,
    )(*operands)
    return result[0] if single else result


def shaped(*dims):
    return jax.ShapeDtypeStruct(dims, F32)


def body(*arguments):
    rhs, inv = arguments[0:4], arguments[4:8]
    panel, index_rows = (None,) + arguments[8:11], (None,) + arguments[11:14]
    leaves, devices = lax.axis_size("leaf"), lax.axis_size("rows")
    leaf, device = lax.axis_index("leaf"), lax.axis_index("rows")
    nz = devices // 2
    z, core = device // 2, device % 2
    meta = jnp.stack([z, core]).astype(jnp.int32)
    width = rhs[0].shape[2]
    counts = [item.shape[0] for item in rhs]
    owned = [item.shape[1] for item in rhs]
    sizes = [item * devices for item in owned]
    spans = [item.shape[1] for item in inv]
    helds = [max(1, spans[l] // sizes[l]) for l in range(4)]
    groups = [max(1, sizes[l] // spans[l]) for l in range(4)]
    chunks = [item // devices for item in spans]
    offsets = [sum(sizes[:l]) for l in range(5)]

    def to_core(x):
        return lax.ppermute(x, "rows", [(r, r ^ 1) for r in range(devices)])

    def to_chip(x, k):
        return lax.ppermute(x, "rows", [(r, r ^ (2 * k)) for r in range(devices)])

    def to_leaf(x, k):
        return lax.ppermute(x, "leaf", [(i, i ^ k) for i in range(leaves)])

    def scatter_sum(keep, send):
        received = to_core(send)
        pick = lambda k: lax.dynamic_index_in_dim(keep, z ^ k, 0, False) + lax.dynamic_index_in_dim(
            received, z ^ k, 0, False
        )
        return [to_chip(pick(k), k) for k in range(nz - 1, 0, -1)] + [pick(0)]

    def gather(x):
        own = [x] + [to_chip(x, k) for k in range(1, nz)]
        return own + [to_core(item) for item in own]

    def leaf_sum(x, group):
        step = 1
        while step < group:
            x = x + to_leaf(x, step)
            step = step * 2
        return x

    def leaf_rows(x, l):
        return lax.dynamic_slice_in_dim(x, leaf * helds[l] // groups[l], helds[l], 0)

    def place(x, l):
        group, held = groups[l], helds[l]
        if leaves == group:
            return x
        out = jnp.zeros(rhs[l].shape, F32)
        for k in range(leaves // group):
            item = x if k == 0 else to_leaf(x, k * group)
            out = lax.dynamic_update_slice_in_dim(out, item, (leaf // group ^ k) * held, 0)
        return out

    def halves(rows):
        return [shaped(nz, rows, width), shaped(nz, rows, width)]

    solved = [None] * 4
    chain, owed = None, []
    for l in (3, 2, 1, 0):
        keep, send = call(
            functools.partial(forward_inv_kernel, len(owed)),
            f"forward_inv_{l}",
            halves(chunks[l]),
            [pltpu.VMEM((spans[l], width), F32)],
            6 * inv[l].size * width,
            1,
            meta,
            leaf_rows(rhs[l], l),
            *owed,
            inv[l],
        )
        solved[l] = sum(scatter_sum(keep, send)[::-1])
        if l == 0:
            break
        parts = gather(solved[l])
        before = [] if chain is None else [chain]
        keep, send, chain = call(
            functools.partial(forward_panel_kernel, nz, bool(before), offsets[l - 1]),
            f"forward_panel_{l}",
            halves(owned[l - 1]) + [shaped(offsets[l], width)],
            [pltpu.VMEM((spans[l], width), F32)],
            6 * panel[l].size * width,
            2,
            meta,
            leaf_rows(index_rows[l], l),
            *parts,
            *before,
            panel[l],
        )
        owed = scatter_sum(keep, send)
        if groups[l - 1] > 1:
            owed = [leaf_sum(sum(owed[::-1]), groups[l - 1])]
    results = []
    chain, parts = None, None
    for l in range(4):
        residue = solved[l]
        if l > 0:
            before = [] if chain is None else [chain]
            keep, send, chain = call(
                functools.partial(backward_panel_kernel, nz, bool(before)),
                f"backward_panel_{l}",
                halves(chunks[l]) + [shaped(offsets[l], width)],
                [
                    pltpu.VMEM((panel[l].shape[1], 2 * width), BF16),
                    pltpu.VMEM((spans[l], width), F32),
                ],
                6 * panel[l].size * width,
                2,
                meta,
                leaf_rows(index_rows[l], l),
                *parts,
                *before,
                panel[l],
            )
            residue = residue - sum(scatter_sum(keep, send)[::-1])
        x = call(
            functools.partial(backward_inv_kernel, nz),
            f"backward_inv_{l}",
            shaped(helds[l], owned[l], width),
            [pltpu.VMEM((spans[l], width), F32)],
            6 * inv[l].size * width,
            1,
            meta,
            *gather(residue),
            inv[l],
        )
        x = leaf_sum(x, groups[l])
        if l < 3:
            parts = gather(x[0])
        results.append(place(x, l))
    return tuple(results)


def solution(mesh):
    across = P(None, "rows", None)
    return jax.shard_map(
        body,
        mesh=mesh,
        in_specs=(across,) * 4 + (P("rows", "leaf"),) * 4 + (P("leaf", "rows"),) * 3 + (P(None, "rows"),) * 3,
        out_specs=(across,) * 4,
        check_vma=False,
    )
```

time: 1200 us -> 411 us (0.34)
  waiting for transfers between devices: 958 us -> 239 us
  matrix products: 137 us -> 0 us
  starting transfers between devices: 1.99 us -> 125 us
  local copies, waits for them, and re-layouts: 56.4 us -> 17.2 us
  Pallas kernels: 0 us -> 23.8 us
  other arithmetic: 19.3 us -> 4.27 us
  between operations: 16 us -> 1.29 us
    psum x14 -> x0, waiting for transfers between devices: 680 us -> none  [the longest x4 224 us: forward_solve(): return lax.psum(partial_y, 'rows')]
    ppermute x0 -> x123, waiting for transfers between devices: none -> 239 us  [the longest x60 177 us: to_chip(): return lax.ppermute(x, 'rows', [(r, r ^ 2 * k) for r in range(devices)])]
    unnamed x22 -> x0, waiting for transfers between devices: 149 us -> none
    dot_general x27 -> x0, matrix products: 137 us -> none  [the longest x3 45.6 us: ancestor_terms(): jnp.einsum('sq,srn->qrn', target, segment, precision=lax.Precision.HIGHEST)]
    ppermute x0 -> x123, starting transfers between devices: none -> 125 us  [the longest x60 96.9 us: to_chip(): return lax.ppermute(x, 'rows', [(r, r ^ 2 * k) for r in range(devices)])]
    all_gather x3 -> x0, waiting for transfers between devices: 93.9 us -> none  [body(): gathered.append(lax.all_gather(solution_cols, 'rows', axis=1, tiled=True))]
    reduce_scatter x1 -> x0, waiting for transfers between devices: 34.8 us -> none  [reduce_dense(): lax.psum_scatter(parts, 'rows', scatter_dimension=1, tiled=True)]
    pallas_call x0 -> x14, Pallas kernels: none -> 23.8 us  [call(): pl.pallas_call(kernel, out_shape=outs, in_specs=[SMEM] * smem_count + [VM...]
  transfers between devices with their start and end apart: 20 -> 123, of which waited for: 20 -> 72; matrix products, arithmetic and copies ran while one was open for 5% -> 1% of each run, Pallas kernels for 0% -> 0%
where the time goes in v1:
time: 411 us
  waiting for transfers between devices  239 us (58%)
  starting transfers between devices  125 us (30%)
  Pallas kernels  23.8 us (6%)
  local copies, waits for them, and re-layouts  17.2 us (4%)
  other arithmetic  4.27 us (1%)
    ppermute x60, waiting for transfers between devices, to_chip(): return lax.ppermute(x, 'rows', [(r, r ^ 2 * k) for r in range(devices)])  177 us
    ppermute x60, starting transfers between devices, to_chip(): return lax.ppermute(x, 'rows', [(r, r ^ 2 * k) for r in range(devices)])  96.9 us
    ppermute x13, waiting for transfers between devices, to_leaf(): return lax.ppermute(x, 'leaf', [(i, i ^ k) for i in range(leaves)])  37.2 us
    ppermute x50, waiting for transfers between devices, to_core(): return lax.ppermute(x, 'rows', [(r, r ^ 1) for r in range(devices)])  25.3 us
    pallas_call x14, Pallas kernels, call(): pl.pallas_call(kernel, out_shape=outs, in_specs=[SMEM] * smem_count + [VM...  23.8 us
    ppermute x13, starting transfers between devices, to_leaf(): return lax.ppermute(x, 'leaf', [(i, i ^ k) for i in range(leaves)])  19.9 us
    unnamed x53, local copies, waits for them, and re-layouts  14.3 us
    ppermute x50, starting transfers between devices, to_core(): return lax.ppermute(x, 'rows', [(r, r ^ 1) for r in range(devices)])  8.39 us
  transfers between devices with their start and end apart: 123, of which 72 were waited for; matrix products, arithmetic and copies ran while one was open for 1% of the time, Pallas kernels for 0%

profile of v1, /device:TPU:0, one launch (start us, length us, event | category | flops | bytes accessed | tf_op | source)
XLA Modules:
  0.0 410.9 jit_solution(7674891471506988450)
XLA Ops:
  14.9 7.2 %collective-permute-done.2 = f32[256,128]{1,0:T(8,128)S(1)} collective-permute-done((f32[256,128]{1,0:T(8,128)S(1)}, f32[256,128]{1,0:T(8,128)S(1)}, u32[]{:S(2)}, u32[]{:S(2)}) %collective-permute-start.2) | collective-permute-done | bytes 131104 | tf_op jit(solution)/shard_map/ppermute | solution.py:176
  26.7 3.7 collective-permute-done.6.refs_3_
  31.0 4.9 %collective-permute-done.5.refs_2_ = f32[256,128]{1,0:T(8,128)S(1)} collective-permute-done((f32[256,128]{1,0:T(8,128)S(1)}, f32[256,128]{1,0:T(8,128)S(1)}, u32[]{:S(2)}, u32[]{:S(2)}) %collective-permute-start.5) | collective-permute-done | bytes 131104 | tf_op jit(solution)/shard_map/ppermute | solution.py:176
  55.0 4.7 %collective-permute-done.13.refs_1_ = f32[256,128]{1,0:T(8,128)S(1)} collective-permute-done((f32[256,128]{1,0:T(8,128)S(1)}, f32[256,128]{1,0:T(8,128)S(1)}, u32[]{:S(2)}, u32[]{:S(2)}) %collective-permute-start.13) | collective-permute-done | bytes 131104 | tf_op jit(solution)/shard_map/ppermute | solution.py:176
  70.8 5.9 %collective-permute-done.17 = f32[256,128]{1,0:T(8,128)S(1)} collective-permute-done((f32[256,128]{1,0:T(8,128)S(1)}, f32[256,128]{1,0:T(8,128)S(1)}, u32[]{:S(2)}, u32[]{:S(2)}) %collective-permute-start.17) | collective-permute-done | bytes 131104 | tf_op jit(solution)/shard_map/ppermute | solution.py:176
  83.5 7.8 %collective-permute-done.20.refs_2_ = f32[256,128]{1,0:T(8,128)S(1)} collective-permute-done((f32[256,128]{1,0:T(8,128)S(1)}, f32[256,128]{1,0:T(8,128)S(1)}, u32[]{:S(2)}, u32[]{:S(2)}) %collective-permute-start.20) | collective-permute-done | bytes 131104 | tf_op jit(solution)/shard_map/ppermute | solution.py:176
  105.2 3.3 collective-permute-done.27
  108.4 7.0 %collective-permute-done.28 = f32[256,128]{1,0:T(8,128)S(1)} collective-permute-done((f32[256,128]{1,0:T(8,128)S(1)}, f32[256,128]{1,0:T(8,128)S(1)}, u32[]{:S(2)}, u32[]{:S(2)}) %collective-permute-start.28) | collective-permute-done | bytes 131104 | tf_op jit(solution)/shard_map/ppermute | solution.py:176
  130.3 5.8 %collective-permute-done.33 = f32[128,128]{1,0:T(8,128)S(1)} collective-permute-done((f32[128,128]{1,0:T(8,128)S(1)}, f32[128,128]{1,0:T(8,128)S(1)}, u32[]{:S(2)}, u32[]{:S(2)}) %collective-permute-start.33) | collective-permute-done | bytes 65568 | tf_op jit(solution)/shard_map/ppermute | solution.py:176
  141.1 4.1 collective-permute-done.36.refs_2_
  158.2 9.1 %collective-permute-done.43 = f32[512,128]{1,0:T(8,128)S(1)} collective-permute-done((f32[512,128]{1,0:T(8,128)S(1)}, f32[512,128]{1,0:T(8,128)S(1)}, u32[]{:S(2)}, u32[]{:S(2)}) %collective-permute-start.43) | collective-permute-done | bytes 262176 | tf_op jit(solution)/shard_map/ppermute | solution.py:176
  167.3 9.0 %collective-permute-done.44 = f32[512,128]{1,0:T(8,128)S(1)} collective-permute-done((f32[512,128]{1,0:T(8,128)S(1)}, f32[512,128]{1,0:T(8,128)S(1)}, u32[]{:S(2)}, u32[]{:S(2)}) %collective-permute-start.44) | collective-permute-done | bytes 262176 | tf_op jit(solution)/shard_map/ppermute | solution.py:176
  177.8 4.9 %collective-permute-done.46 = f32[512,128]{1,0:T(8,128)S(1)} collective-permute-done((f32[512,128]{1,0:T(8,128)S(1)}, f32[512,128]{1,0:T(8,128)S(1)}, u32[]{:S(2)}, u32[]{:S(2)}) %collective-permute-start.46) | collective-permute-done | bytes 262176 | tf_op jit(solution)/shard_map/ppermute | solution.py:179
  184.3 4.9 %collective-permute-done.47 = f32[512,128]{1,0:T(8,128)S(1)} collective-permute-done((f32[512,128]{1,0:T(8,128)S(1)}, f32[512,128]{1,0:T(8,128)S(1)}, u32[]{:S(2)}, u32[]{:S(2)}) %collective-permute-start.47) | collective-permute-done | bytes 262176 | tf_op jit(solution)/shard_map/ppermute | solution.py:179
  192.2 6.1 %collective-permute-start.49 = (f32[128,128]{1,0:T(8,128)S(1)}, f32[128,128]{1,0:T(8,128)S(1)}, u32[]{:S(2)}, u32[]{:S(2)}) collective-permute-start(f32[128,128]{1,0:T(8,128)S(1)} %get-tuple-element.79), channel_id=1, source_target_pairs={{0,2},{1,3},{2,0},{3,1},{4,6},{5,7},{6,4},{7,5},{8,10},{9,11},{10,... | collective-permute-start | bytes 196616 | tf_op jit(solution)/shard_map/ppermute | solution.py:176
  200.8 5.7 %collective-permute-done.50 = f32[128,128]{1,0:T(8,128)S(1)} collective-permute-done((f32[128,128]{1,0:T(8,128)S(1)}, f32[128,128]{1,0:T(8,128)S(1)}, u32[]{:S(2)}, u32[]{:S(2)}) %collective-permute-start.50) | collective-permute-done | bytes 65568 | tf_op jit(solution)/shard_map/ppermute | solution.py:176
  211.5 4.0 collective-permute-done.53.refs_2_
  219.8 7.1 %collective-permute-done.59 = f32[1,512,128]{2,1,0:T(8,128)S(1)} collective-permute-done((f32[1,512,128]{2,1,0:T(8,128)S(1)}, f32[1,512,128]{2,1,0:T(8,128)S(1)}, u32[]{:S(2)}, u32[]{:S(2)}) %collective-permute-start.59) | collective-permute-done | bytes 262176 | tf_op jit(solution)/shard_map/ppermute | solution.py:179
  228.5 6.3 %collective-permute-done.60 = f32[1,512,128]{2,1,0:T(8,128)S(1)} collective-permute-done((f32[1,512,128]{2,1,0:T(8,128)S(1)}, f32[1,512,128]{2,1,0:T(8,128)S(1)}, u32[]{:S(2)}, u32[]{:S(2)}) %collective-permute-start.60) | collective-permute-done | bytes 262176 | tf_op jit(solution)/shard_map/ppermute | solution.py:179
  239.3 6.9 %collective-permute-done.61.refs_1_ = f32[512,128]{1,0:T(8,128)S(1)} collective-permute-done((f32[512,128]{1,0:T(8,128)S(1)}, f32[512,128]{1,0:T(8,128)S(1)}, u32[]{:S(2)}, u32[]{:S(2)}) %collective-permute-start.61) | collective-permute-done | bytes 262176 | tf_op jit(solution)/shard_map/ppermute | solution.py:176
  246.2 10.6 %collective-permute-done.62.refs_2_ = f32[512,128]{1,0:T(8,128)S(1)} collective-permute-done((f32[512,128]{1,0:T(8,128)S(1)}, f32[512,128]{1,0:T(8,128)S(1)}, u32[]{:S(2)}, u32[]{:S(2)}) %collective-permute-start.62) | collective-permute-done | bytes 262176 | tf_op jit(solution)/shard_map/ppermute | solution.py:176
  267.1 5.7 %collective-permute-done.70 = f32[128,128]{1,0:T(8,128)S(1)} collective-permute-done((f32[128,128]{1,0:T(8,128)S(1)}, f32[128,128]{1,0:T(8,128)S(1)}, u32[]{:S(2)}, u32[]{:S(2)}) %collective-permute-start.70) | collective-permute-done | bytes 65568 | tf_op jit(solution)/shard_map/ppermute | solution.py:176
  277.8 4.1 collective-permute-done.73.refs_2_
  285.8 4.3 %collective-permute-done.79 = f32[1,256,128]{2,1,0:T(8,128)S(1)} collective-permute-done((f32[1,256,128]{2,1,0:T(8,128)S(1)}, f32[1,256,128]{2,1,0:T(8,128)S(1)}, u32[]{:S(2)}, u32[]{:S(2)}) %collective-permute-start.79) | collective-permute-done | bytes 131104 | tf_op jit(solution)/shard_map/ppermute | solution.py:179
  296.9 6.6 %collective-permute-done.82.refs_2_ = f32[256,128]{1,0:T(8,128)S(1)} collective-permute-done((f32[256,128]{1,0:T(8,128)S(1)}, f32[256,128]{1,0:T(8,128)S(1)}, u32[]{:S(2)}, u32[]{:S(2)}) %collective-permute-start.82) | collective-permute-done | bytes 131104 | tf_op jit(solution)/shard_map/ppermute | solution.py:176
  316.7 7.3 %collective-permute-done.90 = f32[256,128]{1,0:T(8,128)S(1)} collective-permute-done((f32[256,128]{1,0:T(8,128)S(1)}, f32[256,128]{1,0:T(8,128)S(1)}, u32[]{:S(2)}, u32[]{:S(2)}) %collective-permute-start.90) | collective-permute-done | bytes 131104 | tf_op jit(solution)/shard_map/ppermute | solution.py:176
  330.4 7.9 %collective-permute-done.93.refs_2_ = f32[256,128]{1,0:T(8,128)S(1)} collective-permute-done((f32[256,128]{1,0:T(8,128)S(1)}, f32[256,128]{1,0:T(8,128)S(1)}, u32[]{:S(2)}, u32[]{:S(2)}) %collective-permute-start.93) | collective-permute-done | bytes 131104 | tf_op jit(solution)/shard_map/ppermute | solution.py:176
  348.6 7.5 %collective-permute-done.103.refs_2_ = f32[256,128]{1,0:T(8,128)S(1)} collective-permute-done((f32[256,128]{1,0:T(8,128)S(1)}, f32[256,128]{1,0:T(8,128)S(1)}, u32[]{:S(2)}, u32[]{:S(2)}) %collective-permute-start.103) | collective-permute-done | bytes 131104 | tf_op jit(solution)/shard_map/ppermute | solution.py:176
  357.7 4.0 backward_panel_3.1
  372.0 7.6 %collective-permute-done.111 = f32[256,128]{1,0:T(8,128)} collective-permute-done((f32[256,128]{1,0:T(8,128)}, f32[256,128]{1,0:T(8,128)}, u32[]{:S(2)}, u32[]{:S(2)}) %collective-permute-start.111) | collective-permute-done | bytes 131104 | tf_op jit(solution)/shard_map/ppermute | solution.py:176
  387.7 7.2 %collective-permute-done.114.refs_2_ = f32[256,128]{1,0:T(8,128)S(1)} collective-permute-done((f32[256,128]{1,0:T(8,128)S(1)}, f32[256,128]{1,0:T(8,128)S(1)}, u32[]{:S(2)}, u32[]{:S(2)}) %collective-permute-start.114) | collective-permute-done | bytes 131104 | tf_op jit(solution)/shard_map/ppermute | solution.py:176
  405.5 4.5 %collective-permute-done.121 = f32[2,128,128]{2,1,0:T(8,128)S(1)} collective-permute-done((f32[2,128,128]{2,1,0:T(8,128)S(1)}, f32[2,128,128]{2,1,0:T(8,128)S(1)}, u32[]{:S(2)}, u32[]{:S(2)}) %collective-permute-start.121) | collective-permute-done | bytes 131104 | tf_op jit(solution)/shard_map/ppermute | solution.py:179
  (325 shorter events, 213.9 us)
Async XLA Ops:
  9.3 12.9 %collective-permute-start.2 = (f32[256,128]{1,0:T(8,128)S(1)}, f32[256,128]{1,0:T(8,128)S(1)}, u32[]{:S(2)}, u32[]{:S(2)}) collective-permute-start(f32[256,128]{1,0:T(8,128)S(1)} %get-tuple-element.75), channel_id=1, source_target_pairs={{0,4},{1,5},{2,6},{3,7},{4,0},{5,1},{6,2},{7,3},{8,12},{9,13},{10,... | collective-permute-start | bytes 393224 | tf_op jit(solution)/shard_map/ppermute | solution.py:176
  48.9 10.8 %collective-permute-start.13 = (f32[256,128]{1,0:T(8,128)S(1)}, f32[256,128]{1,0:T(8,128)S(1)}, u32[]{:S(2)}, u32[]{:S(2)}) collective-permute-start(f32[256,128]{1,0:T(8,128)S(1)} %get-tuple-element.71), channel_id=1, source_target_pairs={{0,4},{1,5},{2,6},{3,7},{4,0},{5,1},{6,2},{7,3},{8,12},{9,13},{10,... | collective-permute-start | bytes 393224 | tf_op jit(solution)/shard_map/ppermute | solution.py:176
  48.9 10.8 %collective-permute-start.14 = (f32[256,128]{1,0:T(8,128)S(1)}, f32[256,128]{1,0:T(8,128)S(1)}, u32[]{:S(2)}, u32[]{:S(2)}) collective-permute-start(f32[256,128]{1,0:T(8,128)S(1)} %get-tuple-element.70), channel_id=1, source_target_pairs={{0,2},{1,3},{2,0},{3,1},{4,6},{5,7},{6,4},{7,5},{8,10},{9,11},{10,... | collective-permute-start | bytes 393224 | tf_op jit(solution)/shard_map/ppermute | solution.py:176
  63.8 12.9 %collective-permute-start.17 = (f32[256,128]{1,0:T(8,128)S(1)}, f32[256,128]{1,0:T(8,128)S(1)}, u32[]{:S(2)}, u32[]{:S(2)}) collective-permute-start(f32[256,128]{1,0:T(8,128)S(1)} %get-tuple-element.68), channel_id=1, source_target_pairs={{0,4},{1,5},{2,6},{3,7},{4,0},{5,1},{6,2},{7,3},{8,12},{9,13},{10,... | collective-permute-start | bytes 393224 | tf_op jit(solution)/shard_map/ppermute | solution.py:176
  79.1 12.1 %collective-permute-start.20 = (f32[256,128]{1,0:T(8,128)S(1)}, f32[256,128]{1,0:T(8,128)S(1)}, u32[]{:S(2)}, u32[]{:S(2)}) collective-permute-start(f32[256,128]{1,0:T(8,128)S(1)} %fusion.11.refs_0_), channel_id=1, source_target_pairs={{0,4},{1,5},{2,6},{3,7},{4,0},{5,1},{6,2},{7,3},{8,12},{9,13},{10,... | collective-permute-start | bytes 393224 | tf_op jit(solution)/shard_map/ppermute | solution.py:176
  80.0 11.2 %collective-permute-start.21 = (f32[256,128]{1,0:T(8,128)S(1)}, f32[256,128]{1,0:T(8,128)S(1)}, u32[]{:S(2)}, u32[]{:S(2)}) collective-permute-start(f32[256,128]{1,0:T(8,128)S(1)} %fusion.11.refs_0_), channel_id=1, source_target_pairs={{0,6},{1,7},{2,4},{3,5},{4,2},{5,3},{6,0},{7,1},{8,14},{9,15},{10,... | collective-permute-start | bytes 393224 | tf_op jit(solution)/shard_map/ppermute | solution.py:176
  81.6 10.9 %collective-permute-start.22 = (f32[256,128]{1,0:T(8,128)S(1)}, f32[256,128]{1,0:T(8,128)S(1)}, u32[]{:S(2)}, u32[]{:S(2)}) collective-permute-start(f32[256,128]{1,0:T(8,128)S(1)} %fusion.11.refs_0_), channel_id=1, source_target_pairs={{0,1},{1,0},{2,3},{3,2},{4,5},{5,4},{6,7},{7,6},{8,9},{9,8},{10,11... | collective-permute-start | bytes 393224 | tf_op jit(solution)/shard_map/ppermute | solution.py:173
  102.5 12.9 %collective-permute-start.28 = (f32[256,128]{1,0:T(8,128)S(1)}, f32[256,128]{1,0:T(8,128)S(1)}, u32[]{:S(2)}, u32[]{:S(2)}) collective-permute-start(f32[256,128]{1,0:T(8,128)S(1)} %get-tuple-element.65), channel_id=1, source_target_pairs={{0,4},{1,5},{2,6},{3,7},{4,0},{5,1},{6,2},{7,3},{8,12},{9,13},{10,... | collective-permute-start | bytes 393224 | tf_op jit(solution)/shard_map/ppermute | solution.py:176
  103.7 11.8 %collective-permute-start.29 = (f32[256,128]{1,0:T(8,128)S(1)}, f32[256,128]{1,0:T(8,128)S(1)}, u32[]{:S(2)}, u32[]{:S(2)}) collective-permute-start(f32[256,128]{1,0:T(8,128)S(1)} %get-tuple-element.64), channel_id=1, source_target_pairs={{0,6},{1,7},{2,4},{3,5},{4,2},{5,3},{6,0},{7,1},{8,14},{9,15},{10,... | collective-permute-start | bytes 393224 | tf_op jit(solution)/shard_map/ppermute | solution.py:176
  153.7 13.5 %collective-permute-start.43 = (f32[512,128]{1,0:T(8,128)S(1)}, f32[512,128]{1,0:T(8,128)S(1)}, u32[]{:S(2)}, u32[]{:S(2)}) collective-permute-start(f32[512,128]{1,0:T(8,128)S(1)} %get-tuple-element.54), channel_id=1, source_target_pairs={{0,2},{1,3},{2,0},{3,1},{4,6},{5,7},{6,4},{7,5},{8,10},{9,11},{10,... | collective-permute-start | bytes 786440 | tf_op jit(solution)/shard_map/ppermute | solution.py:176
  154.9 21.3 %collective-permute-start.44 = (f32[512,128]{1,0:T(8,128)S(1)}, f32[512,128]{1,0:T(8,128)S(1)}, u32[]{:S(2)}, u32[]{:S(2)}) collective-permute-start(f32[512,128]{1,0:T(8,128)S(1)} %get-tuple-element.56), channel_id=1, source_target_pairs={{0,4},{1,5},{2,6},{3,7},{4,0},{5,1},{6,2},{7,3},{8,12},{9,13},{10,... | collective-permute-start | bytes 786440 | tf_op jit(solution)/shard_map/ppermute | solution.py:176
  156.6 19.6 %collective-permute-start.45 = (f32[512,128]{1,0:T(8,128)S(1)}, f32[512,128]{1,0:T(8,128)S(1)}, u32[]{:S(2)}, u32[]{:S(2)}) collective-permute-start(f32[512,128]{1,0:T(8,128)S(1)} %get-tuple-element.55), channel_id=1, source_target_pairs={{0,6},{1,7},{2,4},{3,5},{4,2},{5,3},{6,0},{7,1},{8,14},{9,15},{10,... | collective-permute-start | bytes 786440 | tf_op jit(solution)/shard_map/ppermute | solution.py:176
  234.8 11.4 %collective-permute-start.61 = (f32[512,128]{1,0:T(8,128)S(1)}, f32[512,128]{1,0:T(8,128)S(1)}, u32[]{:S(2)}, u32[]{:S(2)}) collective-permute-start(f32[512,128]{1,0:T(8,128)S(1)} %bitcast.132), channel_id=1, source_target_pairs={{0,2},{1,3},{2,0},{3,1},{4,6},{5,7},{6,4},{7,5},{8,10},{9,11},{10,... | collective-permute-start | bytes 786440 | tf_op jit(solution)/shard_map/ppermute | solution.py:176
  235.6 21.2 %collective-permute-start.62 = (f32[512,128]{1,0:T(8,128)S(1)}, f32[512,128]{1,0:T(8,128)S(1)}, u32[]{:S(2)}, u32[]{:S(2)}) collective-permute-start(f32[512,128]{1,0:T(8,128)S(1)} %bitcast.133), channel_id=1, source_target_pairs={{0,4},{1,5},{2,6},{3,7},{4,0},{5,1},{6,2},{7,3},{8,12},{9,13},{10,... | collective-permute-start | bytes 786440 | tf_op jit(solution)/shard_map/ppermute | solution.py:176
  237.6 19.2 %collective-permute-start.63 = (f32[512,128]{1,0:T(8,128)S(1)}, f32[512,128]{1,0:T(8,128)S(1)}, u32[]{:S(2)}, u32[]{:S(2)}) collective-permute-start(f32[512,128]{1,0:T(8,128)S(1)} %bitcast.134), channel_id=1, source_target_pairs={{0,6},{1,7},{2,4},{3,5},{4,2},{5,3},{6,0},{7,1},{8,14},{9,15},{10,... | collective-permute-start | bytes 786440 | tf_op jit(solution)/shard_map/ppermute | solution.py:176
  239.3 18.0 %collective-permute-start.64 = (f32[512,128]{1,0:T(8,128)S(1)}, f32[512,128]{1,0:T(8,128)S(1)}, u32[]{:S(2)}, u32[]{:S(2)}) collective-permute-start(f32[512,128]{1,0:T(8,128)S(1)} %bitcast.135), channel_id=1, source_target_pairs={{0,1},{1,0},{2,3},{3,2},{4,5},{5,4},{6,7},{7,6},{8,9},{9,8},{10,11... | collective-permute-start | bytes 786440 | tf_op jit(solution)/shard_map/ppermute | solution.py:173
  246.2 11.1 %collective-permute-start.65 = (f32[512,128]{1,0:T(8,128)S(1)}, f32[512,128]{1,0:T(8,128)S(1)}, u32[]{:S(2)}, u32[]{:S(2)}) collective-permute-start(f32[512,128]{1,0:T(8,128)S(1)} %collective-permute-done.61.refs_1_), channel_id=1, source_target_pairs={{0,1},{1,0},{2,3},{3,2},{4,5},{5,4},{6,7},{7,6},{8,9},{9,8},{10,11... | collective-permute-start | bytes 786440 | tf_op jit(solution)/shard_map/ppermute | solution.py:173
  291.2 12.3 %collective-permute-start.82 = (f32[256,128]{1,0:T(8,128)S(1)}, f32[256,128]{1,0:T(8,128)S(1)}, u32[]{:S(2)}, u32[]{:S(2)}) collective-permute-start(f32[256,128]{1,0:T(8,128)S(1)} %bitcast.138), channel_id=1, source_target_pairs={{0,4},{1,5},{2,6},{3,7},{4,0},{5,1},{6,2},{7,3},{8,12},{9,13},{10,... | collective-permute-start | bytes 393224 | tf_op jit(solution)/shard_map/ppermute | solution.py:176
  311.1 12.9 %collective-permute-start.90 = (f32[256,128]{1,0:T(8,128)S(1)}, f32[256,128]{1,0:T(8,128)S(1)}, u32[]{:S(2)}, u32[]{:S(2)}) collective-permute-start(f32[256,128]{1,0:T(8,128)S(1)} %get-tuple-element.62), channel_id=1, source_target_pairs={{0,4},{1,5},{2,6},{3,7},{4,0},{5,1},{6,2},{7,3},{8,12},{9,13},{10,... | collective-permute-start | bytes 393224 | tf_op jit(solution)/shard_map/ppermute | solution.py:176
  311.7 12.3 %collective-permute-start.91 = (f32[256,128]{1,0:T(8,128)S(1)}, f32[256,128]{1,0:T(8,128)S(1)}, u32[]{:S(2)}, u32[]{:S(2)}) collective-permute-start(f32[256,128]{1,0:T(8,128)S(1)} %get-tuple-element.61), channel_id=1, source_target_pairs={{0,6},{1,7},{2,4},{3,5},{4,2},{5,3},{6,0},{7,1},{8,14},{9,15},{10,... | collective-permute-start | bytes 393224 | tf_op jit(solution)/shard_map/ppermute | solution.py:176
  326.4 11.9 %collective-permute-start.93 = (f32[256,128]{1,0:T(8,128)S(1)}, f32[256,128]{1,0:T(8,128)S(1)}, u32[]{:S(2)}, u32[]{:S(2)}) collective-permute-start(f32[256,128]{1,0:T(8,128)S(1)} %fusion.7.refs_0_), channel_id=1, source_target_pairs={{0,4},{1,5},{2,6},{3,7},{4,0},{5,1},{6,2},{7,3},{8,12},{9,13},{10,... | collective-permute-start | bytes 393224 | tf_op jit(solution)/shard_map/ppermute | solution.py:176
  326.9 11.4 %collective-permute-start.94 = (f32[256,128]{1,0:T(8,128)S(1)}, f32[256,128]{1,0:T(8,128)S(1)}, u32[]{:S(2)}, u32[]{:S(2)}) collective-permute-start(f32[256,128]{1,0:T(8,128)S(1)} %fusion.7.refs_0_), channel_id=1, source_target_pairs={{0,6},{1,7},{2,4},{3,5},{4,2},{5,3},{6,0},{7,1},{8,14},{9,15},{10,... | collective-permute-start | bytes 393224 | tf_op jit(solution)/shard_map/ppermute | solution.py:176
  343.2 12.9 %collective-permute-start.103 = (f32[256,128]{1,0:T(8,128)S(1)}, f32[256,128]{1,0:T(8,128)S(1)}, u32[]{:S(2)}, u32[]{:S(2)}) collective-permute-start(f32[256,128]{1,0:T(8,128)S(1)} %bitcast.128), channel_id=1, source_target_pairs={{0,4},{1,5},{2,6},{3,7},{4,0},{5,1},{6,2},{7,3},{8,12},{9,13},{10,... | collective-permute-start | bytes 393224 | tf_op jit(solution)/shard_map/ppermute | solution.py:176
  343.7 12.4 %collective-permute-start.104 = (f32[256,128]{1,0:T(8,128)S(1)}, f32[256,128]{1,0:T(8,128)S(1)}, u32[]{:S(2)}, u32[]{:S(2)}) collective-permute-start(f32[256,128]{1,0:T(8,128)S(1)} %bitcast.129), channel_id=1, source_target_pairs={{0,6},{1,7},{2,4},{3,5},{4,2},{5,3},{6,0},{7,1},{8,14},{9,15},{10,... | collective-permute-start | bytes 393224 | tf_op jit(solution)/shard_map/ppermute | solution.py:176
  345.7 11.0 %collective-permute-start.105 = (f32[256,128]{1,0:T(8,128)S(1)}, f32[256,128]{1,0:T(8,128)S(1)}, u32[]{:S(2)}, u32[]{:S(2)}) collective-permute-start(f32[256,128]{1,0:T(8,128)S(1)} %bitcast.130), channel_id=1, source_target_pairs={{0,1},{1,0},{2,3},{3,2},{4,5},{5,4},{6,7},{7,6},{8,9},{9,8},{10,11... | collective-permute-start | bytes 393224 | tf_op jit(solution)/shard_map/ppermute | solution.py:173
  366.4 13.2 %collective-permute-start.111 = (f32[256,128]{1,0:T(8,128)}, f32[256,128]{1,0:T(8,128)}, u32[]{:S(2)}, u32[]{:S(2)}) collective-permute-start(f32[256,128]{1,0:T(8,128)} %get-tuple-element.59), channel_id=1, source_target_pairs={{0,4},{1,5},{2,6},{3,7},{4,0},{5,1},{6,2},{7,3},{8,12},{9,13},{10,... | collective-permute-start | bytes 393224 | tf_op jit(solution)/shard_map/ppermute | solution.py:176
  366.8 12.8 %collective-permute-start.112 = (f32[256,128]{1,0:T(8,128)S(1)}, f32[256,128]{1,0:T(8,128)}, u32[]{:S(2)}, u32[]{:S(2)}) collective-permute-start(f32[256,128]{1,0:T(8,128)S(1)} %get-tuple-element.58), channel_id=1, source_target_pairs={{0,6},{1,7},{2,4},{3,5},{4,2},{5,3},{6,0},{7,1},{8,14},{9,15},{10,... | collective-permute-start | bytes 393224 | tf_op jit(solution)/shard_map/ppermute | solution.py:176
  368.8 16.7 %collective-permute-start.80 = (f32[1,256,128]{2,1,0:T(8,128)S(1)}, f32[1,256,128]{2,1,0:T(8,128)S(1)}, u32[]{:S(2)}, u32[]{:S(2)}) collective-permute-start(f32[1,256,128]{2,1,0:T(8,128)S(1)} %get-tuple-element.53), channel_id=1, source_target_pairs={{0,16},{8,24},{16,0},{24,8},{1,17},{9,25},{17,1},{25,9},{2,18},{10... | collective-permute-start | bytes 393224 | tf_op jit(solution)/shard_map/ppermute | solution.py:179
  370.3 16.8 %collective-permute-start.99 = (f32[1,256,128]{2,1,0:T(8,128)S(1)}, f32[1,256,128]{2,1,0:T(8,128)S(1)}, u32[]{:S(2)}, u32[]{:S(2)}) collective-permute-start(f32[1,256,128]{2,1,0:T(8,128)S(1)} %backward_inv_2.1), channel_id=1, source_target_pairs={{0,8},{8,0},{16,24},{24,16},{1,9},{9,1},{17,25},{25,17},{2,10},{10... | collective-permute-start | bytes 393224 | tf_op jit(solution)/shard_map/ppermute | solution.py:179
  383.0 11.9 %collective-permute-start.114 = (f32[256,128]{1,0:T(8,128)S(1)}, f32[256,128]{1,0:T(8,128)S(1)}, u32[]{:S(2)}, u32[]{:S(2)}) collective-permute-start(f32[256,128]{1,0:T(8,128)S(1)} %fusion.4.refs_0_), channel_id=1, source_target_pairs={{0,4},{1,5},{2,6},{3,7},{4,0},{5,1},{6,2},{7,3},{8,12},{9,13},{10,... | collective-permute-start | bytes 393224 | tf_op jit(solution)/shard_map/ppermute | solution.py:176
  383.5 11.4 %collective-permute-start.115 = (f32[256,128]{1,0:T(8,128)S(1)}, f32[256,128]{1,0:T(8,128)S(1)}, u32[]{:S(2)}, u32[]{:S(2)}) collective-permute-start(f32[256,128]{1,0:T(8,128)S(1)} %fusion.4.refs_0_), channel_id=1, source_target_pairs={{0,6},{1,7},{2,4},{3,5},{4,2},{5,3},{6,0},{7,1},{8,14},{9,15},{10,... | collective-permute-start | bytes 393224 | tf_op jit(solution)/shard_map/ppermute | solution.py:176
  387.1 10.8 %collective-permute-start.116 = (f32[256,128]{1,0:T(8,128)S(1)}, f32[256,128]{1,0:T(8,128)S(1)}, u32[]{:S(2)}, u32[]{:S(2)}) collective-permute-start(f32[256,128]{1,0:T(8,128)S(1)} %fusion.4.refs_0_), channel_id=1, source_target_pairs={{0,1},{1,0},{2,3},{3,2},{4,5},{5,4},{6,7},{7,6},{8,9},{9,8},{10,11... | collective-permute-start | bytes 393224 | tf_op jit(solution)/shard_map/ppermute | solution.py:173
  (117 other events, 1168.4 us)

commit v2 on v1

v2 whole, which is shorter than its diff:
```python
import functools

import jax
import jax.numpy as jnp
from jax import lax
from jax.experimental import pallas as pl
from jax.experimental.pallas import tpu as pltpu
from jax.sharding import PartitionSpec as P

BLOCK = 128
F32 = jnp.float32
BF16 = jnp.bfloat16
VMEM = pl.BlockSpec(memory_space=pltpu.VMEM)
SMEM = pl.BlockSpec(memory_space=pltpu.SMEM)
LIMIT = 14 * 1024 * 1024


def cut(x):
    high = x.astype(BF16)
    return high, (x - high.astype(F32)).astype(BF16)


def wide(x):
    return jnp.concatenate(cut(x), axis=1)


def product(dims, a, xw):
    n = xw.shape[1] // 2
    high, low = cut(a)
    first = lax.dot_general(high, xw, (dims, ((), ())), preferred_element_type=F32)
    second = lax.dot_general(low, xw[:, :n], (dims, ((), ())), preferred_element_type=F32)
    return first[:, :n] + (first[:, n:] + second)


times = functools.partial(product, ((1,), (0,)))
transposed_times = functools.partial(product, ((0,), (0,)))


def tile_of(rows, largest=512):
    return min(rows, largest)


def spread_parts(meta, full, own, other, offset=0):
    rows = own[0].shape[0]
    for k in range(len(own)):
        chunk = 2 * jnp.bitwise_xor(meta[0], k)
        full[pl.ds(pl.multiple_of(offset + (chunk + meta[1]) * rows, 8), rows), :] = own[k][...]
        full[pl.ds(pl.multiple_of(offset + (chunk + 1 - meta[1]) * rows, 8), rows), :] = other[k][...]


def split_cores(meta, full, offset, keep, send):
    count, rows = keep.shape[0], keep.shape[1]
    for k in range(count):
        keep[k] = full[pl.ds(pl.multiple_of(offset + (2 * k + meta[1]) * rows, 8), rows), :]
        send[k] = full[pl.ds(pl.multiple_of(offset + (2 * k + 1 - meta[1]) * rows, 8), rows), :]


def forward_inv_kernel(owed_count, meta, rhs, *refs):
    owed, (inv, keep, send, full) = refs[:owed_count], refs[owed_count:]
    held = rhs.shape[0]
    part = inv.shape[1] // held
    tile = tile_of(part)
    for h in range(held):
        source = rhs[h]
        for item in owed:
            source = source - item[...]
        source = wide(source)
        for start in range(h * part, (h + 1) * part, tile):
            full[start : start + tile, :] = transposed_times(inv[:, start : start + tile], source)
    split_cores(meta, full, 0, keep, send)


def forward_top_kernel(leaves, group, meta, rhs, *refs):
    owed, (inv, keep, send, source, full) = refs[:leaves], refs[leaves:]
    rows = BLOCK // group
    source[...] = rhs[0]
    for d in range(leaves):
        place = lax.rem(jnp.bitwise_xor(meta[2], d), group) * rows
        for b in range(rhs.shape[1] // BLOCK):
            at = pl.ds(pl.multiple_of(b * BLOCK + place, 8), rows)
            source[at, :] = source[at, :] - owed[d][b * rows : (b + 1) * rows, :]
    factor = wide(source[...])
    tile = tile_of(inv.shape[1])
    for start in range(0, inv.shape[1], tile):
        full[start : start + tile, :] = transposed_times(inv[:, start : start + tile], factor)
    split_cores(meta, full, 0, keep, send)


def panel_update(panel, full, h, held):
    part = panel.shape[0] // held
    tile = tile_of(part)
    update = None
    for start in range(h * part, (h + 1) * part, tile):
        term = transposed_times(panel[start : start + tile, :], wide(full[start : start + tile, :]))
        update = term if update is None else update + term
    return update


def forward_panel_kernel(nz, before_count, cut_at, meta, rows, *refs):
    own, other, refs = refs[:nz], refs[nz : 2 * nz], refs[2 * nz :]
    before, (panel, keep, send), refs = refs[:before_count], refs[before_count : before_count + 3], refs[before_count + 3 :]
    (deferred, (chain, full)) = (refs[:-2], refs[-2:])
    held, listed = rows.shape
    spread_parts(meta, full, own, other)
    if before:
        chain[...] = before[0][...]
    else:
        chain[...] = jnp.zeros_like(chain)
    for h in range(held):
        update = panel_update(panel, full, h, held)
        for k in range(listed):
            place = pl.ds(pl.multiple_of(rows[h, k] * BLOCK, BLOCK), BLOCK)
            chain[place, :] = chain[place, :] + update[k * BLOCK : (k + 1) * BLOCK]
    split_cores(meta, chain, cut_at, keep, send)
    if len(deferred) == 2:
        split_cores(meta, chain, 0, *deferred)
    elif deferred:
        deferred[0][...] = chain[: deferred[0].shape[0], :]


def forward_last_kernel(nz, group, meta, rows, *refs):
    own, other, refs = refs[:nz], refs[nz : 2 * nz], refs[2 * nz :]
    panel, pieces, (full, update) = refs[0], refs[1:-2], refs[-2:]
    spread_parts(meta, full, own, other)
    update[...] = panel_update(panel, full, 0, 1)
    listed = rows.shape[1]
    height = BLOCK // group
    for d in range(group):
        place = jnp.bitwise_xor(lax.rem(meta[2], group), d) * height
        for k in range(listed):
            at = pl.ds(pl.multiple_of(k * BLOCK + place, 8), height)
            pieces[d][k * height : (k + 1) * height, :] = update[at, :]
        tail = pieces[d].shape[0] - listed * height
        numbers = jnp.zeros((tail, update.shape[1]), F32)
        if d == 0:
            line = lax.broadcasted_iota(jnp.int32, numbers.shape, 0)
            for k in range(listed):
                numbers = jnp.where(line == k, rows[0, k].astype(F32), numbers)
        pieces[d][listed * height :, :] = numbers


def owed_top_kernel(nz, group, listed, meta, *refs):
    parts, (deferred, owed) = refs[: 2 * nz], refs[2 * nz :]
    height = BLOCK // group
    blocks = owed.shape[0] // height
    first = (2 * meta[0] + meta[1]) * blocks
    for b in range(blocks):
        wanted = (first + b).astype(F32)
        total = jnp.zeros((height, owed.shape[1]), F32)
        for item in parts:
            for k in range(listed):
                number = item[listed * height + k : listed * height + k + 1, :]
                total = total + jnp.where(number == wanted, item[k * height : (k + 1) * height, :], 0.0)
        owed[b * height : (b + 1) * height, :] = total
    count = deferred.shape[0]
    at = pl.ds(pl.multiple_of((meta[2] // group) * count, 8), count)
    owed[at, :] = owed[at, :] + deferred[...]


def pick_kernel(nz, leaves, levels, meta, *refs):
    lists, refs = refs[: len(levels)], refs[len(levels) :]
    own, other, picks, full = refs[:nz], refs[nz : 2 * nz], refs[2 * nz : 2 * nz + leaves], refs[2 * nz + leaves]
    height = BLOCK // leaves
    last = full.shape[0] // height - 1
    spread_parts(meta, full, own, other)
    for d in range(leaves):
        at = 0
        for (held, group), rows in zip(levels, lists):
            first = jnp.bitwise_xor(meta[2], d) * held // group
            for h in range(held):
                for k in range(rows.shape[1]):
                    block = jnp.minimum(rows[first + h, k], last)
                    picks[d][at : at + height, :] = full[pl.ds(pl.multiple_of(block * height, 8), height), :]
                    at += height


def backward_panel_kernel(nz, leaves, top, skip, before_count, meta, rows, *refs):
    picks, refs = refs[:leaves], refs[leaves:]
    own, other, refs = refs[:nz], refs[nz : 2 * nz], refs[2 * nz :]
    before, refs = refs[:before_count], refs[before_count:]
    panel, keep, send, *chain, chosen, factor, full = refs
    held, listed = rows.shape
    height = BLOCK // leaves
    part = panel.shape[0] // held
    tile = tile_of(part)
    if chain:
        chain = chain[0]
        offset = 0
        if before:
            offset = before[0].shape[0]
            chain[:offset, :] = before[0][...]
        spread_parts(meta, chain, own, other, offset)
    for h in range(held):
        for k in range(listed):
            for d in range(leaves):
                at = pl.ds(pl.multiple_of(k * BLOCK + jnp.bitwise_xor(meta[2], d) * height, 8), height)
                line = skip + (h * listed + k) * height
                chosen[at, :] = picks[d][line : line + height, :]
            if own:

                @pl.when(rows[h, k] >= top)
                def _(h=h, k=k):
                    place = pl.ds(pl.multiple_of((rows[h, k] - top) * BLOCK, BLOCK), BLOCK)
                    chosen[k * BLOCK : (k + 1) * BLOCK, :] = chain[place, :]

        for k in range(listed):
            factor[k * BLOCK : (k + 1) * BLOCK, :] = wide(chosen[k * BLOCK : (k + 1) * BLOCK, :])
        for start in range(h * part, (h + 1) * part, tile):
            full[start : start + tile, :] = times(panel[start : start + tile, :], factor[...])
    split_cores(meta, full, 0, keep, send)


def backward_sum(inv, full, h, held):
    part = inv.shape[1] // held
    tile = tile_of(part)
    total = None
    for start in range(h * part, (h + 1) * part, tile):
        term = times(inv[:, start : start + tile], wide(full[start : start + tile, :]))
        total = term if total is None else total + term
    return total


def backward_inv_kernel(nz, meta, *refs):
    own, other, (inv, solved, full) = refs[:nz], refs[nz : 2 * nz], refs[2 * nz :]
    spread_parts(meta, full, own, other)
    for h in range(solved.shape[0]):
        solved[h] = backward_sum(inv, full, h, solved.shape[0])


def backward_top_kernel(nz, leaves, meta, *refs):
    own, other, refs = refs[:nz], refs[nz : 2 * nz], refs[2 * nz :]
    inv, pieces, (full, solved) = refs[0], refs[1:-2], refs[-2:]
    spread_parts(meta, full, own, other)
    solved[...] = backward_sum(inv, full, 0, 1)
    height = BLOCK // leaves
    for d in range(leaves):
        place = jnp.bitwise_xor(meta[2], d) * height
        for b in range(solved.shape[0] // BLOCK):
            at = pl.ds(pl.multiple_of(b * BLOCK + place, 8), height)
            pieces[d][b * height : (b + 1) * height, :] = solved[at, :]


def call(kernel, name, out_shapes, scratch, flops, smem_count, *operands):
    single = not isinstance(out_shapes, (list, tuple))
    outs = [out_shapes] if single else list(out_shapes)
    moved = sum(item.size * 4 for item in operands) + sum(item.size * 4 for item in outs)
    result = pl.pallas_call(
        kernel,
        out_shape=outs,
        in_specs=[SMEM] * smem_count + [VMEM] * (len(operands) - smem_count),
        out_specs=[VMEM] * len(outs),
        scratch_shapes=scratch,
        compiler_params=pltpu.CompilerParams(vmem_limit_bytes=LIMIT),
        cost_estimate=pl.CostEstimate(flops=flops, bytes_accessed=moved, transcendentals=0),
        name=name,
    )(*operands)
    return result[0] if single else result


def shaped(*dims):
    return jax.ShapeDtypeStruct(dims, F32)


def body(*arguments):
    rhs, inv = arguments[0:4], arguments[4:8]
    panel, index_rows = (None,) + arguments[8:11], (None,) + arguments[11:14]
    leaves, devices = lax.axis_size("leaf"), lax.axis_size("rows")
    leaf, device = lax.axis_index("leaf"), lax.axis_index("rows")
    nz = devices // 2
    z, core = device // 2, device % 2
    meta = jnp.stack([z, core, leaf]).astype(jnp.int32)
    width = rhs[0].shape[2]
    counts = [item.shape[0] for item in rhs]
    owned = [item.shape[1] for item in rhs]
    sizes = [item * devices for item in owned]
    spans = [item.shape[1] for item in inv]
    helds = [max(1, spans[l] // sizes[l]) for l in range(4)]
    groups = [max(1, sizes[l] // spans[l]) for l in range(4)]
    chunks = [item // devices for item in spans]
    offsets = [sum(sizes[:l]) for l in range(5)]
    listed = [0] + [item.shape[1] // BLOCK for item in panel[1:]]

    def to_core(x):
        return lax.ppermute(x, "rows", [(r, r ^ 1) for r in range(devices)])

    def to_chip(x, k):
        return lax.ppermute(x, "rows", [(r, r ^ (2 * k)) for r in range(devices)])

    def to_leaf(x, k):
        return x if k == 0 else lax.ppermute(x, "leaf", [(i, i ^ k) for i in range(leaves)])

    def to_leaves(pieces):
        far_first = {d: to_leaf(pieces[d], d) for d in reversed(range(len(pieces)))}
        return [far_first[d] for d in range(len(pieces))]

    def scatter_chips(chunk):
        return [to_chip(chunk(k), k) for k in range(nz - 1, 0, -1)] + [chunk(0)]

    def scatter_sum(keep, send):
        received = to_core(send)
        return scatter_chips(
            lambda k: lax.dynamic_index_in_dim(keep, z ^ k, 0, False)
            + lax.dynamic_index_in_dim(received, z ^ k, 0, False)
        )

    def gather(x):
        far_first = {k: to_chip(x, k) for k in range(nz - 1, 0, -1)}
        own = [x] + [far_first[k] for k in range(1, nz)]
        return own + [to_core(item) for item in own]

    def leaf_sum(x, group):
        step = 1
        while step < group:
            x = x + to_leaf(x, step)
            step = step * 2
        return x

    def leaf_rows(x, l):
        return lax.dynamic_slice_in_dim(x, leaf * helds[l] // groups[l], helds[l], 0)

    def place(x, l):
        group, held = groups[l], helds[l]
        if leaves == group:
            return x
        out = jnp.zeros(rhs[l].shape, F32)
        for k in range(leaves // group):
            out = lax.dynamic_update_slice_in_dim(out, to_leaf(x, k * group), (leaf // group ^ k) * held, 0)
        return out

    def halves(rows):
        return [shaped(nz, rows, width), shaped(nz, rows, width)]

    def room(*dims):
        return pltpu.VMEM(dims, F32)

    solved = [None] * 4
    chain, owed = [], []
    for l in (3, 2, 1):
        keep, send = call(
            functools.partial(forward_inv_kernel, len(owed)),
            f"forward_inv_{l}",
            halves(chunks[l]),
            [room(spans[l], width)],
            6 * inv[l].size * width,
            1,
            meta,
            leaf_rows(rhs[l], l),
            *owed,
            inv[l],
        )
        solved[l] = sum(scatter_sum(keep, send)[::-1])
        parts = gather(solved[l])
        if l == 1:
            break
        keep, send, *chain = call(
            functools.partial(forward_panel_kernel, nz, len(chain), offsets[l - 1]),
            f"forward_panel_{l}",
            halves(owned[l - 1]) + ([shaped(offsets[l - 1], width)] if l > 2 else halves(owned[0])),
            [room(offsets[l], width), room(spans[l], width)],
            6 * panel[l].size * width,
            2,
            meta,
            leaf_rows(index_rows[l], l),
            *parts,
            *chain,
            panel[l],
        )
        owed = scatter_sum(keep, send)
        if groups[l - 1] > 1:
            owed = [leaf_sum(sum(owed[::-1]), groups[l - 1])]

    group, seps = groups[1], leaves // groups[1]
    height = BLOCK // group
    blocks = owned[0] // BLOCK
    deferred_keep, deferred_send = chain
    deferred_received = to_core(deferred_send)

    def leaf_cut(x, i):
        x = x.reshape(nz, seps, blocks // seps, group, height, width)
        x = lax.dynamic_slice(x, (0, i // group, 0, i % group, 0, 0), (nz, 1, blocks // seps, 1, height, width))
        return x.reshape(nz, blocks // seps * height, width)

    deferred = to_leaves([leaf_cut(deferred_keep, leaf ^ d) + leaf_cut(deferred_received, leaf ^ d) for d in range(leaves)])
    deferred = sum(deferred)
    deferred = sum(scatter_chips(lambda k: lax.dynamic_index_in_dim(deferred, z ^ k, 0, False))[::-1])

    pieces = call(
        functools.partial(forward_last_kernel, nz, group),
        "forward_panel_1",
        [shaped(listed[1] * height + 8, width)] * group,
        [room(spans[1], width), room(panel[1].shape[1], width)],
        6 * panel[1].size * width,
        2,
        meta,
        leaf_rows(index_rows[1], 1),
        *parts,
        panel[1],
    )
    piece = sum(to_leaves(pieces))
    owed = call(
        functools.partial(owed_top_kernel, nz, group, listed[1]),
        "owed_top",
        shaped(blocks * height, width),
        [],
        0,
        1,
        meta,
        *gather(piece),
        deferred,
    )
    keep, send = call(
        functools.partial(forward_top_kernel, leaves, group),
        "forward_inv_0",
        halves(chunks[0]),
        [room(owned[0], width), room(spans[0], width)],
        6 * inv[0].size * width,
        1,
        meta,
        rhs[0],
        *to_leaves([owed] * leaves),
        inv[0],
    )
    solved[0] = sum(scatter_sum(keep, send)[::-1])

    pieces = call(
        functools.partial(backward_top_kernel, nz, leaves),
        "backward_inv_0",
        [shaped(owned[0] // leaves, width)] * leaves,
        [room(spans[0], width), room(owned[0], width)],
        6 * inv[0].size * width,
        1,
        meta,
        *gather(solved[0]),
        inv[0],
    )
    piece = sum(to_leaves(pieces))
    cuts = gather(piece)
    thin = BLOCK // leaves
    top = jnp.zeros((blocks, leaves, thin, width), F32)
    for d, item in enumerate(to_leaves([piece] * leaves)):
        top = lax.dynamic_update_slice(top, item.reshape(blocks, 1, thin, width), (0, leaf ^ d, 0, 0))
    results = [top.reshape(rhs[0].shape)]

    def picked(levels, name):
        picks = call(
            functools.partial(pick_kernel, nz, leaves, [(helds[l], groups[l]) for l in levels]),
            name,
            [shaped(sum(helds[l] * listed[l] for l in levels) * thin, width)] * leaves,
            [room(sizes[0] // leaves, width)],
            0,
            1 + len(levels),
            meta,
            *[index_rows[l] for l in levels],
            *cuts,
        )
        return to_leaves(picks)

    first_picks = picked([1], "pick_1")
    later_picks = picked([2, 3], "pick_2_3")
    chain, parts = [], []
    for l in (1, 2, 3):
        above = sum(sizes[1:l])
        keep, send, *chain = call(
            functools.partial(
                backward_panel_kernel,
                nz if l > 1 else 0,
                leaves,
                sizes[0] // BLOCK,
                helds[2] * listed[2] * thin if l == 3 else 0,
                len(chain),
            ),
            f"backward_panel_{l}",
            halves(chunks[l]) + ([shaped(above, width)] if l > 1 else []),
            [
                room(panel[l].shape[1], width),
                pltpu.VMEM((panel[l].shape[1], 2 * width), BF16),
                room(spans[l], width),
            ],
            6 * panel[l].size * width,
            2,
            meta,
            leaf_rows(index_rows[l], l),
            *(first_picks if l == 1 else later_picks),
            *parts,
            *chain,
            panel[l],
        )
        residue = solved[l] - sum(scatter_sum(keep, send)[::-1])
        x = call(
            functools.partial(backward_inv_kernel, nz),
            f"backward_inv_{l}",
            shaped(helds[l], owned[l], width),
            [room(spans[l], width)],
            6 * inv[l].size * width,
            1,
            meta,
            *gather(residue),
            inv[l],
        )
        x = leaf_sum(x, groups[l])
        if l < 3:
            parts = gather(x[0])
        results.append(place(x, l))
    return tuple(results)


def solution(mesh):
    across = P(None, "rows", None)
    return jax.shard_map(
        body,
        mesh=mesh,
        in_specs=(across,) * 4 + (P("rows", "leaf"),) * 4 + (P("leaf", "rows"),) * 3 + (P(None, "rows"),) * 3,
        out_specs=(across,) * 4,
        check_vma=False,
    )
```

time: 411 us -> 385 us (0.937)
  waiting for transfers between devices: 239 us -> 199 us
  starting transfers between devices: 125 us -> 135 us
    ppermute x60 -> x63, waiting for transfers between devices: 177 us -> 142 us  [to_chip(): return lax.ppermute(x, 'rows', [(r, r ^ 2 * k) for r in range(devices)])]
    ppermute x13 -> x28, starting transfers between devices: 19.9 us -> 32.1 us  [to_leaf(): lax.ppermute(x, 'leaf', [(i, i ^ k) for i in range(leaves)])]
    ppermute x13 -> x28, waiting for transfers between devices: 37.2 us -> 32 us  [to_leaf(): lax.ppermute(x, 'leaf', [(i, i ^ k) for i in range(leaves)])]
    pallas_call x14 -> x17, Pallas kernels: 23.8 us -> 25.4 us  [call(): pl.pallas_call(kernel, out_shape=outs, in_specs=[SMEM] * smem_count + [VM...]
    unnamed x53 -> x55, local copies, waits for them, and re-layouts: 14.3 us -> 12.7 us
    ppermute x50 -> x54, starting transfers between devices: 8.39 us -> 6.94 us  [to_core(): return lax.ppermute(x, 'rows', [(r, r ^ 1) for r in range(devices)])]
    ppermute x60 -> x63, starting transfers between devices: 96.9 us -> 96 us  [to_chip(): return lax.ppermute(x, 'rows', [(r, r ^ 2 * k) for r in range(devices)])]
    ppermute x50 -> x54, waiting for transfers between devices: 25.3 us -> 25.1 us  [to_core(): return lax.ppermute(x, 'rows', [(r, r ^ 1) for r in range(devices)])]
  transfers between devices with their start and end apart: 123 -> 145, of which waited for: 72 -> 87; matrix products, arithmetic and copies ran while one was open for 1% -> 2% of each run, Pallas kernels for 0% -> 1%
where the time goes in v2:
time: 385 us; the launch traced here: 384 us
  waiting for transfers between devices  199 us (52%)
  starting transfers between devices  135 us (35%)
  Pallas kernels  25.4 us (7%)
  local copies, waits for them, and re-layouts  15 us (4%)
  other arithmetic  7.74 us (2%)
    ppermute x63, waiting for transfers between devices, to_chip(): return lax.ppermute(x, 'rows', [(r, r ^ 2 * k) for r in range(devices)])  142 us
    ppermute x63, starting transfers between devices, to_chip(): return lax.ppermute(x, 'rows', [(r, r ^ 2 * k) for r in range(devices)])  96 us
    ppermute x28, starting transfers between devices, to_leaf(): lax.ppermute(x, 'leaf', [(i, i ^ k) for i in range(leaves)])  32.1 us
    ppermute x28, waiting for transfers between devices, to_leaf(): lax.ppermute(x, 'leaf', [(i, i ^ k) for i in range(leaves)])  32 us
    pallas_call x17, Pallas kernels, call(): pl.pallas_call(kernel, out_shape=outs, in_specs=[SMEM] * smem_count + [VM...  25.4 us
    ppermute x54, waiting for transfers between devices, to_core(): return lax.ppermute(x, 'rows', [(r, r ^ 1) for r in range(devices)])  25.1 us
    unnamed x55, local copies, waits for them, and re-layouts  12.7 us
  transfers between devices with their start and end apart: 145, of which 87 were waited for; matrix products, arithmetic and copies ran while one was open for 2% of the time, Pallas kernels for 1%

profile of v2, /device:TPU:0, one launch (start us, length us, event | category | flops | bytes accessed | tf_op | source)
XLA Modules:
  0.0 384.0 jit_solution(9056565075942069401)
XLA Ops:
  6.3 3.0 collective-permute-start.1
  9.3 2.6 collective-permute-start.2
  11.9 3.1 collective-permute-done.1
  15.0 7.2 %collective-permute-done.2 = f32[256,128]{1,0:T(8,128)S(1)} collective-permute-done((f32[256,128]{1,0:T(8,128)S(1)}, f32[256,128]{1,0:T(8,128)S(1)}, u32[]{:S(2)}, u32[]{:S(2)}) %collective-permute-start.2) | collective-permute-done | bytes 131104 | tf_op jit(solution)/shard_map/ppermute | solution.py:287
  26.7 3.7 collective-permute-done.6.refs_3_
  31.1 4.9 %collective-permute-done.5.refs_2_ = f32[256,128]{1,0:T(8,128)S(1)} collective-permute-done((f32[256,128]{1,0:T(8,128)S(1)}, f32[256,128]{1,0:T(8,128)S(1)}, u32[]{:S(2)}, u32[]{:S(2)}) %collective-permute-start.5) | collective-permute-done | bytes 131104 | tf_op jit(solution)/shard_map/ppermute | solution.py:287
  53.4 3.0 collective-permute-done.12.refs_0_
  56.5 4.8 %collective-permute-done.13.refs_1_ = f32[256,128]{1,0:T(8,128)S(1)} collective-permute-done((f32[256,128]{1,0:T(8,128)}, f32[256,128]{1,0:T(8,128)S(1)}, u32[]{:S(2)}, u32[]{:S(2)}) %collective-permute-start.13) | collective-permute-done | bytes 131104 | tf_op jit(solution)/shard_map/ppermute | solution.py:287
  69.1 3.2 collective-permute-done.16
  72.3 5.9 %collective-permute-done.17 = f32[256,128]{1,0:T(8,128)S(1)} collective-permute-done((f32[256,128]{1,0:T(8,128)S(1)}, f32[256,128]{1,0:T(8,128)S(1)}, u32[]{:S(2)}, u32[]{:S(2)}) %collective-permute-start.17) | collective-permute-done | bytes 131104 | tf_op jit(solution)/shard_map/ppermute | solution.py:287
  85.0 7.8 %collective-permute-done.20.refs_2_ = f32[256,128]{1,0:T(8,128)S(1)} collective-permute-done((f32[256,128]{1,0:T(8,128)S(1)}, f32[256,128]{1,0:T(8,128)S(1)}, u32[]{:S(2)}, u32[]{:S(2)}) %collective-permute-start.20) | collective-permute-done | bytes 131104 | tf_op jit(solution)/shard_map/ppermute | solution.py:287
  96.2 3.1 forward_panel_2.1
  106.7 3.3 collective-permute-done.27
  110.0 7.0 %collective-permute-done.28 = f32[256,128]{1,0:T(8,128)S(1)} collective-permute-done((f32[256,128]{1,0:T(8,128)S(1)}, f32[256,128]{1,0:T(8,128)S(1)}, u32[]{:S(2)}, u32[]{:S(2)}) %collective-permute-start.28) | collective-permute-done | bytes 131104 | tf_op jit(solution)/shard_map/ppermute | solution.py:287
  132.8 5.5 %collective-permute-done.33 = f32[128,128]{1,0:T(8,128)S(1)} collective-permute-done((f32[128,128]{1,0:T(8,128)S(1)}, f32[128,128]{1,0:T(8,128)S(1)}, u32[]{:S(2)}, u32[]{:S(2)}) %collective-permute-start.33) | collective-permute-done | bytes 65568 | tf_op jit(solution)/shard_map/ppermute | solution.py:287
  155.0 2.9 collective-permute-done.52
  167.5 6.0 %collective-permute-done.55 = f32[128,128]{1,0:T(8,128)S(1)} collective-permute-done((f32[128,128]{1,0:T(8,128)S(1)}, f32[128,128]{1,0:T(8,128)S(1)}, u32[]{:S(2)}, u32[]{:S(2)}) %collective-permute-start.55) | collective-permute-done | bytes 65568 | tf_op jit(solution)/shard_map/ppermute | solution.py:287
  179.9 2.6 collective-permute-done.57.refs_1_
  182.5 3.7 collective-permute-done.58.refs_2_
  194.6 3.6 collective-permute-done.62
  203.3 2.6 collective-permute-done.65.refs_2_
  242.2 3.4 collective-permute-done.89
  250.7 3.2 collective-permute-done.92.refs_2_
  270.8 5.1 %collective-permute-done.104.refs_6_ = f32[256,128]{1,0:T(8,128)S(1)} collective-permute-done((f32[256,128]{1,0:T(8,128)S(1)}, f32[256,128]{1,0:T(8,128)S(1)}, u32[]{:S(2)}, u32[]{:S(2)}) %collective-permute-start.104) | collective-permute-done | bytes 131104 | tf_op jit(solution)/shard_map/ppermute | solution.py:287
  288.7 7.7 %collective-permute-done.112 = f32[256,128]{1,0:T(8,128)S(1)} collective-permute-done((f32[256,128]{1,0:T(8,128)S(1)}, f32[256,128]{1,0:T(8,128)S(1)}, u32[]{:S(2)}, u32[]{:S(2)}) %collective-permute-start.112) | collective-permute-done | bytes 131104 | tf_op jit(solution)/shard_map/ppermute | solution.py:287
  302.9 7.7 %collective-permute-done.115.refs_2_ = f32[256,128]{1,0:T(8,128)S(1)} collective-permute-done((f32[256,128]{1,0:T(8,128)S(1)}, f32[256,128]{1,0:T(8,128)S(1)}, u32[]{:S(2)}, u32[]{:S(2)}) %collective-permute-start.115) | collective-permute-done | bytes 131104 | tf_op jit(solution)/shard_map/ppermute | solution.py:287
  320.9 7.7 %collective-permute-done.125.refs_6_ = f32[256,128]{1,0:T(8,128)S(1)} collective-permute-done((f32[256,128]{1,0:T(8,128)S(1)}, f32[256,128]{1,0:T(8,128)S(1)}, u32[]{:S(2)}, u32[]{:S(2)}) %collective-permute-start.125) | collective-permute-done | bytes 131104 | tf_op jit(solution)/shard_map/ppermute | solution.py:287
  330.2 3.7 backward_panel_3.1
  346.0 8.0 %collective-permute-done.133 = f32[256,128]{1,0:T(8,128)S(1)} collective-permute-done((f32[256,128]{1,0:T(8,128)S(1)}, f32[256,128]{1,0:T(8,128)S(1)}, u32[]{:S(2)}, u32[]{:S(2)}) %collective-permute-start.133) | collective-permute-done | bytes 131104 | tf_op jit(solution)/shard_map/ppermute | solution.py:287
  361.3 7.5 %collective-permute-done.136.refs_2_ = f32[256,128]{1,0:T(8,128)S(1)} collective-permute-done((f32[256,128]{1,0:T(8,128)S(1)}, f32[256,128]{1,0:T(8,128)S(1)}, u32[]{:S(2)}, u32[]{:S(2)}) %collective-permute-start.136) | collective-permute-done | bytes 131104 | tf_op jit(solution)/shard_map/ppermute | solution.py:287
  372.9 3.8 collective-permute-done.123
  378.4 3.4 collective-permute-done.143
  (379 shorter events, 231.8 us)
Async XLA Ops:
  9.3 12.9 %collective-permute-start.2 = (f32[256,128]{1,0:T(8,128)S(1)}, f32[256,128]{1,0:T(8,128)S(1)}, u32[]{:S(2)}, u32[]{:S(2)}) collective-permute-start(f32[256,128]{1,0:T(8,128)S(1)} %get-tuple-element.100), channel_id=1, source_target_pairs={{0,4},{1,5},{2,6},{3,7},{4,0},{5,1},{6,2},{7,3},{8,12},{9,13},{10,... | collective-permute-start | bytes 393224 | tf_op jit(solution)/shard_map/ppermute | solution.py:287
  11.9 10.3 %collective-permute-start.3 = (f32[256,128]{1,0:T(8,128)S(1)}, f32[256,128]{1,0:T(8,128)S(1)}, u32[]{:S(2)}, u32[]{:S(2)}) collective-permute-start(f32[256,128]{1,0:T(8,128)S(1)} %get-tuple-element.99), channel_id=1, source_target_pairs={{0,6},{1,7},{2,4},{3,5},{4,2},{5,3},{6,0},{7,1},{8,14},{9,15},{10,... | collective-permute-start | bytes 393224 | tf_op jit(solution)/shard_map/ppermute | solution.py:287
  50.4 10.8 %collective-permute-start.13 = (f32[256,128]{1,0:T(8,128)}, f32[256,128]{1,0:T(8,128)S(1)}, u32[]{:S(2)}, u32[]{:S(2)}) collective-permute-start(f32[256,128]{1,0:T(8,128)} %get-tuple-element.96), channel_id=1, source_target_pairs={{0,4},{1,5},{2,6},{3,7},{4,0},{5,1},{6,2},{7,3},{8,12},{9,13},{10,... | collective-permute-start | bytes 393224 | tf_op jit(solution)/shard_map/ppermute | solution.py:287
  50.4 10.8 %collective-permute-start.14 = (f32[256,128]{1,0:T(8,128)}, f32[256,128]{1,0:T(8,128)S(1)}, u32[]{:S(2)}, u32[]{:S(2)}) collective-permute-start(f32[256,128]{1,0:T(8,128)} %get-tuple-element.95), channel_id=1, source_target_pairs={{0,2},{1,3},{2,0},{3,1},{4,6},{5,7},{6,4},{7,5},{8,10},{9,11},{10,... | collective-permute-start | bytes 393224 | tf_op jit(solution)/shard_map/ppermute | solution.py:287
  65.3 12.9 %collective-permute-start.17 = (f32[256,128]{1,0:T(8,128)S(1)}, f32[256,128]{1,0:T(8,128)S(1)}, u32[]{:S(2)}, u32[]{:S(2)}) collective-permute-start(f32[256,128]{1,0:T(8,128)S(1)} %get-tuple-element.93), channel_id=1, source_target_pairs={{0,4},{1,5},{2,6},{3,7},{4,0},{5,1},{6,2},{7,3},{8,12},{9,13},{10,... | collective-permute-start | bytes 393224 | tf_op jit(solution)/shard_map/ppermute | solution.py:287
  67.7 10.5 %collective-permute-start.18 = (f32[256,128]{1,0:T(8,128)S(1)}, f32[256,128]{1,0:T(8,128)S(1)}, u32[]{:S(2)}, u32[]{:S(2)}) collective-permute-start(f32[256,128]{1,0:T(8,128)S(1)} %get-tuple-element.92), channel_id=1, source_target_pairs={{0,6},{1,7},{2,4},{3,5},{4,2},{5,3},{6,0},{7,1},{8,14},{9,15},{10,... | collective-permute-start | bytes 393224 | tf_op jit(solution)/shard_map/ppermute | solution.py:287
  80.6 12.1 %collective-permute-start.20 = (f32[256,128]{1,0:T(8,128)S(1)}, f32[256,128]{1,0:T(8,128)S(1)}, u32[]{:S(2)}, u32[]{:S(2)}) collective-permute-start(f32[256,128]{1,0:T(8,128)S(1)} %fusion.11.refs_0_), channel_id=1, source_target_pairs={{0,4},{1,5},{2,6},{3,7},{4,0},{5,1},{6,2},{7,3},{8,12},{9,13},{10,... | collective-permute-start | bytes 393224 | tf_op jit(solution)/shard_map/ppermute | solution.py:287
  81.5 11.3 %collective-permute-start.21 = (f32[256,128]{1,0:T(8,128)S(1)}, f32[256,128]{1,0:T(8,128)S(1)}, u32[]{:S(2)}, u32[]{:S(2)}) collective-permute-start(f32[256,128]{1,0:T(8,128)S(1)} %fusion.11.refs_0_), channel_id=1, source_target_pairs={{0,6},{1,7},{2,4},{3,5},{4,2},{5,3},{6,0},{7,1},{8,14},{9,15},{10,... | collective-permute-start | bytes 393224 | tf_op jit(solution)/shard_map/ppermute | solution.py:287
  83.1 10.2 %collective-permute-start.22 = (f32[256,128]{1,0:T(8,128)S(1)}, f32[256,128]{1,0:T(8,128)S(1)}, u32[]{:S(2)}, u32[]{:S(2)}) collective-permute-start(f32[256,128]{1,0:T(8,128)S(1)} %fusion.11.refs_0_), channel_id=1, source_target_pairs={{0,1},{1,0},{2,3},{3,2},{4,5},{5,4},{6,7},{7,6},{8,9},{9,8},{10,11... | collective-permute-start | bytes 393224 | tf_op jit(solution)/shard_map/ppermute | solution.py:284
  104.1 12.9 %collective-permute-start.28 = (f32[256,128]{1,0:T(8,128)S(1)}, f32[256,128]{1,0:T(8,128)S(1)}, u32[]{:S(2)}, u32[]{:S(2)}) collective-permute-start(f32[256,128]{1,0:T(8,128)S(1)} %get-tuple-element.90), channel_id=1, source_target_pairs={{0,4},{1,5},{2,6},{3,7},{4,0},{5,1},{6,2},{7,3},{8,12},{9,13},{10,... | collective-permute-start | bytes 393224 | tf_op jit(solution)/shard_map/ppermute | solution.py:287
  105.2 11.8 %collective-permute-start.29 = (f32[256,128]{1,0:T(8,128)S(1)}, f32[256,128]{1,0:T(8,128)S(1)}, u32[]{:S(2)}, u32[]{:S(2)}) collective-permute-start(f32[256,128]{1,0:T(8,128)S(1)} %get-tuple-element.89), channel_id=1, source_target_pairs={{0,6},{1,7},{2,4},{3,5},{4,2},{5,3},{6,0},{7,1},{8,14},{9,15},{10,... | collective-permute-start | bytes 393224 | tf_op jit(solution)/shard_map/ppermute | solution.py:287
  106.7 33.9 %collective-permute-start.50 = (f32[4,512,128]{2,1,0:T(8,128)}, f32[4,512,128]{2,1,0:T(8,128)}, u32[]{:S(2)}, u32[]{:S(2)}) collective-permute-start(f32[4,512,128]{2,1,0:T(8,128)} %get-tuple-element.54), channel_id=1, source_target_pairs={{0,1},{1,0},{2,3},{3,2},{4,5},{5,4},{6,7},{7,6},{8,9},{9,8},{10,11... | collective-permute-start | bytes 3145736 | tf_op jit(solution)/shard_map/ppermute | solution.py:284
  147.0 10.9 %collective-permute-start.52 = (f32[4,128,128]{2,1,0:T(8,128)S(1)}, f32[4,128,128]{2,1,0:T(8,128)S(1)}, u32[]{:S(2)}, u32[]{:S(2)}) collective-permute-start(f32[4,128,128]{2,1,0:T(8,128)S(1)} %bitcast.164), channel_id=1, source_target_pairs={{0,16},{8,24},{16,0},{24,8},{1,17},{9,25},{17,1},{25,9},{2,18},{10... | collective-permute-start | bytes 786440 | tf_op jit(solution)/shard_map/ppermute | solution.py:290
  148.6 10.8 %collective-permute-start.53 = (f32[4,128,128]{2,1,0:T(8,128)S(1)}, f32[4,128,128]{2,1,0:T(8,128)S(1)}, u32[]{:S(2)}, u32[]{:S(2)}) collective-permute-start(f32[4,128,128]{2,1,0:T(8,128)S(1)} %bitcast.163), channel_id=1, source_target_pairs={{0,24},{8,16},{16,8},{24,0},{1,25},{9,17},{17,9},{25,1},{2,26},{10... | collective-permute-start | bytes 786440 | tf_op jit(solution)/shard_map/ppermute | solution.py:290
  160.4 13.2 %collective-permute-start.43 = (f32[136,128]{1,0:T(8,128)S(1)}, f32[136,128]{1,0:T(8,128)S(1)}, u32[]{:S(2)}, u32[]{:S(2)}) collective-permute-start(f32[136,128]{1,0:T(8,128)S(1)} %add.594.refs_0_), channel_id=1, source_target_pairs={{0,2},{1,3},{2,0},{3,1},{4,6},{5,7},{6,4},{7,5},{8,10},{9,11},{10,... | collective-permute-start | bytes 208904 | tf_op jit(solution)/shard_map/ppermute | solution.py:287
  161.7 12.4 %collective-permute-start.44 = (f32[136,128]{1,0:T(8,128)S(1)}, f32[136,128]{1,0:T(8,128)S(1)}, u32[]{:S(2)}, u32[]{:S(2)}) collective-permute-start(f32[136,128]{1,0:T(8,128)S(1)} %add.594.refs_0_), channel_id=1, source_target_pairs={{0,4},{1,5},{2,6},{3,7},{4,0},{5,1},{6,2},{7,3},{8,12},{9,13},{10,... | collective-permute-start | bytes 208904 | tf_op jit(solution)/shard_map/ppermute | solution.py:287
  163.1 11.0 %collective-permute-start.45 = (f32[136,128]{1,0:T(8,128)S(1)}, f32[136,128]{1,0:T(8,128)S(1)}, u32[]{:S(2)}, u32[]{:S(2)}) collective-permute-start(f32[136,128]{1,0:T(8,128)S(1)} %add.594.refs_0_), channel_id=1, source_target_pairs={{0,6},{1,7},{2,4},{3,5},{4,2},{5,3},{6,0},{7,1},{8,14},{9,15},{10,... | collective-permute-start | bytes 208904 | tf_op jit(solution)/shard_map/ppermute | solution.py:287
  264.6 11.3 %collective-permute-start.104 = (f32[256,128]{1,0:T(8,128)S(1)}, f32[256,128]{1,0:T(8,128)S(1)}, u32[]{:S(2)}, u32[]{:S(2)}) collective-permute-start(f32[256,128]{1,0:T(8,128)S(1)} %bitcast.159), channel_id=1, source_target_pairs={{0,4},{1,5},{2,6},{3,7},{4,0},{5,1},{6,2},{7,3},{8,12},{9,13},{10,... | collective-permute-start | bytes 393224 | tf_op jit(solution)/shard_map/ppermute | solution.py:287
  265.7 10.2 %collective-permute-start.105 = (f32[256,128]{1,0:T(8,128)S(1)}, f32[256,128]{1,0:T(8,128)S(1)}, u32[]{:S(2)}, u32[]{:S(2)}) collective-permute-start(f32[256,128]{1,0:T(8,128)S(1)} %bitcast.160), channel_id=1, source_target_pairs={{0,6},{1,7},{2,4},{3,5},{4,2},{5,3},{6,0},{7,1},{8,14},{9,15},{10,... | collective-permute-start | bytes 393224 | tf_op jit(solution)/shard_map/ppermute | solution.py:287
  283.7 12.7 %collective-permute-start.112 = (f32[256,128]{1,0:T(8,128)S(1)}, f32[256,128]{1,0:T(8,128)S(1)}, u32[]{:S(2)}, u32[]{:S(2)}) collective-permute-start(f32[256,128]{1,0:T(8,128)S(1)} %get-tuple-element.87), channel_id=1, source_target_pairs={{0,4},{1,5},{2,6},{3,7},{4,0},{5,1},{6,2},{7,3},{8,12},{9,13},{10,... | collective-permute-start | bytes 393224 | tf_op jit(solution)/shard_map/ppermute | solution.py:287
  283.9 12.5 %collective-permute-start.113 = (f32[256,128]{1,0:T(8,128)S(1)}, f32[256,128]{1,0:T(8,128)S(1)}, u32[]{:S(2)}, u32[]{:S(2)}) collective-permute-start(f32[256,128]{1,0:T(8,128)S(1)} %get-tuple-element.86), channel_id=1, source_target_pairs={{0,6},{1,7},{2,4},{3,5},{4,2},{5,3},{6,0},{7,1},{8,14},{9,15},{10,... | collective-permute-start | bytes 393224 | tf_op jit(solution)/shard_map/ppermute | solution.py:287
  299.0 11.6 %collective-permute-start.115 = (f32[256,128]{1,0:T(8,128)S(1)}, f32[256,128]{1,0:T(8,128)S(1)}, u32[]{:S(2)}, u32[]{:S(2)}) collective-permute-start(f32[256,128]{1,0:T(8,128)S(1)} %fusion.7.refs_0_), channel_id=1, source_target_pairs={{0,4},{1,5},{2,6},{3,7},{4,0},{5,1},{6,2},{7,3},{8,12},{9,13},{10,... | collective-permute-start | bytes 393224 | tf_op jit(solution)/shard_map/ppermute | solution.py:287
  299.0 11.6 %collective-permute-start.116 = (f32[256,128]{1,0:T(8,128)S(1)}, f32[256,128]{1,0:T(8,128)S(1)}, u32[]{:S(2)}, u32[]{:S(2)}) collective-permute-start(f32[256,128]{1,0:T(8,128)S(1)} %fusion.7.refs_0_), channel_id=1, source_target_pairs={{0,6},{1,7},{2,4},{3,5},{4,2},{5,3},{6,0},{7,1},{8,14},{9,15},{10,... | collective-permute-start | bytes 393224 | tf_op jit(solution)/shard_map/ppermute | solution.py:287
  315.9 12.7 %collective-permute-start.125 = (f32[256,128]{1,0:T(8,128)S(1)}, f32[256,128]{1,0:T(8,128)S(1)}, u32[]{:S(2)}, u32[]{:S(2)}) collective-permute-start(f32[256,128]{1,0:T(8,128)S(1)} %bitcast.152), channel_id=1, source_target_pairs={{0,4},{1,5},{2,6},{3,7},{4,0},{5,1},{6,2},{7,3},{8,12},{9,13},{10,... | collective-permute-start | bytes 393224 | tf_op jit(solution)/shard_map/ppermute | solution.py:287
  316.0 12.6 %collective-permute-start.126 = (f32[256,128]{1,0:T(8,128)S(1)}, f32[256,128]{1,0:T(8,128)S(1)}, u32[]{:S(2)}, u32[]{:S(2)}) collective-permute-start(f32[256,128]{1,0:T(8,128)S(1)} %bitcast.153), channel_id=1, source_target_pairs={{0,6},{1,7},{2,4},{3,5},{4,2},{5,3},{6,0},{7,1},{8,14},{9,15},{10,... | collective-permute-start | bytes 393224 | tf_op jit(solution)/shard_map/ppermute | solution.py:287
  318.4 10.8 %collective-permute-start.127 = (f32[256,128]{1,0:T(8,128)S(1)}, f32[256,128]{1,0:T(8,128)S(1)}, u32[]{:S(2)}, u32[]{:S(2)}) collective-permute-start(f32[256,128]{1,0:T(8,128)S(1)} %bitcast.154), channel_id=1, source_target_pairs={{0,1},{1,0},{2,3},{3,2},{4,5},{5,4},{6,7},{7,6},{8,9},{9,8},{10,11... | collective-permute-start | bytes 393224 | tf_op jit(solution)/shard_map/ppermute | solution.py:284
  342.0 12.0 %collective-permute-start.133 = (f32[256,128]{1,0:T(8,128)S(1)}, f32[256,128]{1,0:T(8,128)S(1)}, u32[]{:S(2)}, u32[]{:S(2)}) collective-permute-start(f32[256,128]{1,0:T(8,128)S(1)} %get-tuple-element.84), channel_id=1, source_target_pairs={{0,4},{1,5},{2,6},{3,7},{4,0},{5,1},{6,2},{7,3},{8,12},{9,13},{10,... | collective-permute-start | bytes 393224 | tf_op jit(solution)/shard_map/ppermute | solution.py:287
  342.0 12.0 %collective-permute-start.134 = (f32[256,128]{1,0:T(8,128)S(1)}, f32[256,128]{1,0:T(8,128)S(1)}, u32[]{:S(2)}, u32[]{:S(2)}) collective-permute-start(f32[256,128]{1,0:T(8,128)S(1)} %get-tuple-element.83), channel_id=1, source_target_pairs={{0,6},{1,7},{2,4},{3,5},{4,2},{5,3},{6,0},{7,1},{8,14},{9,15},{10,... | collective-permute-start | bytes 393224 | tf_op jit(solution)/shard_map/ppermute | solution.py:287
  344.5 15.3 %collective-permute-start.99 = (f32[1,256,128]{2,1,0:T(8,128)S(1)}, f32[1,256,128]{2,1,0:T(8,128)S(1)}, u32[]{:S(2)}, u32[]{:S(2)}) collective-permute-start(f32[1,256,128]{2,1,0:T(8,128)S(1)} %get-tuple-element.77), channel_id=1, source_target_pairs={{0,16},{8,24},{16,0},{24,8},{1,17},{9,25},{17,1},{25,9},{2,18},{10... | collective-permute-start | bytes 393224 | tf_op jit(solution)/shard_map/ppermute | solution.py:290
  345.0 15.6 %collective-permute-start.121 = (f32[1,256,128]{2,1,0:T(8,128)S(1)}, f32[1,256,128]{2,1,0:T(8,128)S(1)}, u32[]{:S(2)}, u32[]{:S(2)}) collective-permute-start(f32[1,256,128]{2,1,0:T(8,128)S(1)} %backward_inv_2.1), channel_id=1, source_target_pairs={{0,8},{8,0},{16,24},{24,16},{1,9},{9,1},{17,25},{25,17},{2,10},{10... | collective-permute-start | bytes 393224 | tf_op jit(solution)/shard_map/ppermute | solution.py:290
  357.4 11.4 %collective-permute-start.136 = (f32[256,128]{1,0:T(8,128)S(1)}, f32[256,128]{1,0:T(8,128)S(1)}, u32[]{:S(2)}, u32[]{:S(2)}) collective-permute-start(f32[256,128]{1,0:T(8,128)S(1)} %fusion.4.refs_0_), channel_id=1, source_target_pairs={{0,4},{1,5},{2,6},{3,7},{4,0},{5,1},{6,2},{7,3},{8,12},{9,13},{10,... | collective-permute-start | bytes 393224 | tf_op jit(solution)/shard_map/ppermute | solution.py:287
  357.4 11.4 %collective-permute-start.137 = (f32[256,128]{1,0:T(8,128)S(1)}, f32[256,128]{1,0:T(8,128)S(1)}, u32[]{:S(2)}, u32[]{:S(2)}) collective-permute-start(f32[256,128]{1,0:T(8,128)S(1)} %fusion.4.refs_0_), channel_id=1, source_target_pairs={{0,6},{1,7},{2,4},{3,5},{4,2},{5,3},{6,0},{7,1},{8,14},{9,15},{10,... | collective-permute-start | bytes 393224 | tf_op jit(solution)/shard_map/ppermute | solution.py:287
  (140 other events, 1215.1 us)

commit v3 on v2

v3 whole, which is shorter than its diff:
```python
import functools

import jax
import jax.numpy as jnp
from jax import lax
from jax.experimental import pallas as pl
from jax.experimental.pallas import tpu as pltpu
from jax.sharding import PartitionSpec as P

BLOCK = 128
F32 = jnp.float32
BF16 = jnp.bfloat16
VMEM = pl.BlockSpec(memory_space=pltpu.VMEM)
SMEM = pl.BlockSpec(memory_space=pltpu.SMEM)
LIMIT = 14 * 1024 * 1024


def cut(x):
    high = x.astype(BF16)
    return high, (x - high.astype(F32)).astype(BF16)


def wide(x):
    return jnp.concatenate(cut(x), axis=1)


def product(dims, a, xw):
    n = xw.shape[1] // 2
    high, low = cut(a)
    first = lax.dot_general(high, xw, (dims, ((), ())), preferred_element_type=F32)
    second = lax.dot_general(low, xw[:, :n], (dims, ((), ())), preferred_element_type=F32)
    return first[:, :n] + (first[:, n:] + second)


times = functools.partial(product, ((1,), (0,)))
transposed_times = functools.partial(product, ((0,), (0,)))


def tile_of(rows, largest=512):
    return min(rows, largest)


def spread_parts(meta, full, parts, offset=0):
    half = len(parts) // 2
    for k, part in enumerate(parts):
        core = meta[1] if k < half else 1 - meta[1]
        rows = part.shape[0]
        at = offset + (2 * jnp.bitwise_xor(meta[0], k % half) + core) * rows
        full[pl.ds(pl.multiple_of(at, 8), rows), :] = part[...]


def split_cores(meta, full, offset, keep, send):
    count, rows = keep.shape[0], keep.shape[1]
    for k in range(count):
        keep[k] = full[pl.ds(pl.multiple_of(offset + (2 * k + meta[1]) * rows, 8), rows), :]
        send[k] = full[pl.ds(pl.multiple_of(offset + (2 * k + 1 - meta[1]) * rows, 8), rows), :]


def forward_inv_kernel(owed_count, meta, rhs, *refs):
    owed, inv, halves, full = refs[:owed_count], refs[owed_count], refs[owed_count + 1 : -1], refs[-1]
    held = rhs.shape[0]
    part = inv.shape[1] // held
    tile = tile_of(part)
    for h in range(held):
        source = rhs[h]
        for item in owed:
            source = source - item[...]
        source = wide(source)
        for start in range(h * part, (h + 1) * part, tile):
            full[start : start + tile, :] = transposed_times(inv[:, start : start + tile], source)
    split_cores(meta, full, 0, *halves)


def forward_top_kernel(leaves, group, meta, rhs, *refs):
    owed, (inv, keep, send, source, full) = refs[:leaves], refs[leaves:]
    rows = BLOCK // group
    source[...] = rhs[0]
    for d in range(leaves):
        place = lax.rem(jnp.bitwise_xor(meta[2], d), group) * rows
        for b in range(rhs.shape[1] // BLOCK):
            at = pl.ds(pl.multiple_of(b * BLOCK + place, 8), rows)
            source[at, :] = source[at, :] - owed[d][b * rows : (b + 1) * rows, :]
    factor = wide(source[...])
    tile = tile_of(inv.shape[1])
    for start in range(0, inv.shape[1], tile):
        full[start : start + tile, :] = transposed_times(inv[:, start : start + tile], factor)
    split_cores(meta, full, 0, keep, send)


def panel_update(panel, full, h, held):
    part = panel.shape[0] // held
    tile = tile_of(part)
    update = None
    for start in range(h * part, (h + 1) * part, tile):
        term = transposed_times(panel[start : start + tile, :], wide(full[start : start + tile, :]))
        update = term if update is None else update + term
    return update


def add_blocks(chain, rows, updates, first):
    for k in range(rows.shape[0]):

        @pl.when(jnp.logical_and(rows[k] >= first, rows[k] < first + chain.shape[0] // BLOCK))
        def _(k=k):
            place = pl.ds(pl.multiple_of((rows[k] - first) * BLOCK, BLOCK), BLOCK)
            chain[place, :] = chain[place, :] + updates[k * BLOCK : (k + 1) * BLOCK, :]


def forward_panel_kernel(count, held, first, below_count, meta, rows, *refs):
    below_rows, refs = refs[:below_count], refs[below_count:]
    parts, refs = refs[:count], refs[count:]
    below, refs = refs[:below_count], refs[below_count:]
    panel, keep, send, updates, chain, full = refs
    size = updates.shape[0] // held
    spread_parts(meta, full, parts)
    for h in range(held):
        updates[h * size : (h + 1) * size, :] = panel_update(panel, full, h, held)
    chain[...] = jnp.zeros_like(chain)
    add_blocks(chain, rows, updates, first)
    for lower_rows, lower in zip(below_rows, below):
        add_blocks(chain, lower_rows, lower, first)
    split_cores(meta, chain, 0, keep, send)


def deferred_kernel(meta, upper_rows, lower_rows, upper, lower, keep, send, chain):
    chain[...] = jnp.zeros_like(chain)
    add_blocks(chain, upper_rows, upper, 0)
    add_blocks(chain, lower_rows, lower, 0)
    split_cores(meta, chain, 0, keep, send)


def leaf_cuts_kernel(group, meta, keep, received, *cuts):
    count = keep.shape[1] // BLOCK * group // len(cuts)
    height = BLOCK // group
    for d, cut in enumerate(cuts):
        other = jnp.bitwise_xor(meta[2], d)
        for b in range(count):
            row = ((other // group) * count + b) * BLOCK + lax.rem(other, group) * height
            at = pl.ds(pl.multiple_of(row, 8), height)
            for k in range(keep.shape[0]):
                cut[k, b * height : (b + 1) * height, :] = keep[k, at, :] + received[k, at, :]


def forward_last_kernel(count, group, meta, rows, *refs):
    parts, refs = refs[:count], refs[count:]
    panel, pieces, (full, update) = refs[0], refs[1:-2], refs[-2:]
    spread_parts(meta, full, parts)
    update[...] = panel_update(panel, full, 0, 1)
    listed = rows.shape[0]
    height = BLOCK // group
    for d in range(group):
        place = jnp.bitwise_xor(lax.rem(meta[2], group), d) * height
        for k in range(listed):
            at = pl.ds(pl.multiple_of(k * BLOCK + place, 8), height)
            pieces[d][k * height : (k + 1) * height, :] = update[at, :]
        tail = pieces[d].shape[0] - listed * height
        numbers = jnp.zeros((tail, update.shape[1]), F32)
        if d == 0:
            line = lax.broadcasted_iota(jnp.int32, numbers.shape, 0)
            for k in range(listed):
                numbers = jnp.where(line == k, rows[k].astype(F32), numbers)
        pieces[d][listed * height :, :] = numbers


def owed_top_kernel(nz, group, listed, meta, *refs):
    parts, owed = refs[:-1], refs[-1]
    height = BLOCK // group
    blocks = owed.shape[0] // height
    first = (2 * meta[0] + meta[1]) * blocks
    for b in range(blocks):
        wanted = (first + b).astype(F32)
        total = jnp.zeros((height, owed.shape[1]), F32)
        for item in parts:
            for k in range(listed):
                number = item[listed * height + k : listed * height + k + 1, :]
                total = total + jnp.where(number == wanted, item[k * height : (k + 1) * height, :], 0.0)
        owed[b * height : (b + 1) * height, :] = total
    start = parts[nz].shape[0]
    count = parts[0].shape[0] - start
    at = pl.ds(pl.multiple_of((meta[2] // group) * count, 8), count)
    total = owed[at, :]
    for item in parts[:nz]:
        total = total + item[start:, :]
    owed[at, :] = total


def pick_kernel(count, leaves, levels, meta, *refs):
    lists, refs = refs[: len(levels)], refs[len(levels) :]
    parts, picks, full = refs[:count], refs[count:-1], refs[-1]
    height = BLOCK // leaves
    last = full.shape[0] // height - 1
    spread_parts(meta, full, parts)
    for d in range(leaves):
        at = 0
        for (held, group, listed), rows in zip(levels, lists):
            first = jnp.bitwise_xor(meta[2], d) * held // group
            for h in range(held):
                for k in range(listed):
                    block = jnp.minimum(rows[(first + h) * listed + k], last)
                    picks[d][at : at + height, :] = full[pl.ds(pl.multiple_of(block * height, 8), height), :]
                    at += height


def backward_panel_kernel(count, leaves, held, top, skip, before_count, meta, rows, *refs):
    picks, refs = refs[:leaves], refs[leaves:]
    parts, refs = refs[:count], refs[count:]
    before, refs = refs[:before_count], refs[before_count:]
    panel, halves, chain, (chosen, factor, full) = refs[0], refs[1:3], refs[3:-3], refs[-3:]
    listed = rows.shape[0] // held
    height = BLOCK // leaves
    part = panel.shape[0] // held
    tile = tile_of(part)
    if chain:
        chain = chain[0]
        offset = 0
        if before:
            offset = before[0].shape[0]
            chain[:offset, :] = before[0][...]
        spread_parts(meta, chain, parts, offset)
    for h in range(held):
        for k in range(listed):
            for d in range(leaves):
                at = pl.ds(pl.multiple_of(k * BLOCK + jnp.bitwise_xor(meta[2], d) * height, 8), height)
                line = skip + (h * listed + k) * height
                chosen[at, :] = picks[d][line : line + height, :]
            if parts:

                @pl.when(rows[h * listed + k] >= top)
                def _(h=h, k=k):
                    place = pl.ds(pl.multiple_of((rows[h * listed + k] - top) * BLOCK, BLOCK), BLOCK)
                    chosen[k * BLOCK : (k + 1) * BLOCK, :] = chain[place, :]

        for k in range(listed):
            factor[k * BLOCK : (k + 1) * BLOCK, :] = wide(chosen[k * BLOCK : (k + 1) * BLOCK, :])
        for start in range(h * part, (h + 1) * part, tile):
            full[start : start + tile, :] = times(panel[start : start + tile, :], factor[...])
    split_cores(meta, full, 0, *halves)


def backward_sum(inv, full, h, held):
    part = inv.shape[1] // held
    tile = tile_of(part)
    total = None
    for start in range(h * part, (h + 1) * part, tile):
        term = times(inv[:, start : start + tile], wide(full[start : start + tile, :]))
        total = term if total is None else total + term
    return total


def backward_inv_kernel(meta, *refs):
    parts, (inv, solved, full) = refs[:-3], refs[-3:]
    spread_parts(meta, full, parts)
    for h in range(solved.shape[0]):
        solved[h] = backward_sum(inv, full, h, solved.shape[0])


def backward_top_kernel(count, leaves, meta, *refs):
    parts, refs = refs[:count], refs[count:]
    inv, pieces, (full, solved) = refs[0], refs[1:-2], refs[-2:]
    spread_parts(meta, full, parts)
    solved[...] = backward_sum(inv, full, 0, 1)
    height = BLOCK // leaves
    for d in range(leaves):
        place = jnp.bitwise_xor(meta[2], d) * height
        for b in range(solved.shape[0] // BLOCK):
            at = pl.ds(pl.multiple_of(b * BLOCK + place, 8), height)
            pieces[d][b * height : (b + 1) * height, :] = solved[at, :]


def call(kernel, name, out_shapes, scratch, flops, smem_count, *operands):
    single = not isinstance(out_shapes, (list, tuple))
    outs = [out_shapes] if single else list(out_shapes)
    moved = sum(item.size * 4 for item in operands) + sum(item.size * 4 for item in outs)
    result = pl.pallas_call(
        kernel,
        out_shape=outs,
        in_specs=[SMEM] * smem_count + [VMEM] * (len(operands) - smem_count),
        out_specs=[VMEM] * len(outs),
        scratch_shapes=scratch,
        compiler_params=pltpu.CompilerParams(vmem_limit_bytes=LIMIT),
        cost_estimate=pl.CostEstimate(flops=flops, bytes_accessed=moved, transcendentals=0),
        name=name,
    )(*operands)
    return result[0] if single else result


def spacer_kernel(x, dependency, out):
    out[...] = x[...]


BESIDE = 40_000_000_000


def beside(x, dependency):
    return pl.pallas_call(
        spacer_kernel,
        out_shape=jax.ShapeDtypeStruct(x.shape, x.dtype),
        in_specs=[VMEM, pl.BlockSpec(memory_space=pl.ANY)],
        out_specs=VMEM,
        compiler_params=pltpu.CompilerParams(vmem_limit_bytes=1024 * 1024),
        cost_estimate=pl.CostEstimate(flops=BESIDE, bytes_accessed=2 * x.size * 4, transcendentals=0),
        name="beside",
    )(x, dependency)


def shaped(*dims):
    return jax.ShapeDtypeStruct(dims, F32)


def after(x, *others):
    return lax.optimization_barrier((x, others))[0]


def body(*arguments):
    rhs, inv = arguments[0:4], arguments[4:8]
    panel, index_rows = (None,) + arguments[8:11], (None,) + arguments[11:14]
    leaves, devices = lax.axis_size("leaf"), lax.axis_size("rows")
    leaf, device = lax.axis_index("leaf"), lax.axis_index("rows")
    nz = devices // 2
    z, core = device // 2, device % 2
    meta = jnp.stack([z, core, leaf]).astype(jnp.int32)
    width = rhs[0].shape[2]
    owned = [item.shape[1] for item in rhs]
    sizes = [item * devices for item in owned]
    spans = [item.shape[1] for item in inv]
    helds = [max(1, spans[l] // sizes[l]) for l in range(4)]
    groups = [max(1, sizes[l] // spans[l]) for l in range(4)]
    chunks = [item // devices for item in spans]
    listed = [0] + [item.shape[1] // BLOCK for item in panel[1:]]

    def to_core(x):
        return lax.ppermute(x, "rows", [(r, r ^ 1) for r in range(devices)])

    def to_chip(x, k):
        return lax.ppermute(x, "rows", [(r, r ^ (2 * k)) for r in range(devices)])

    def to_leaf(x, k):
        return x if k == 0 else lax.ppermute(x, "leaf", [(i, i ^ k) for i in range(leaves)])

    def to_leaves(pieces):
        far_first = {d: to_leaf(pieces[d], d) for d in reversed(range(len(pieces)))}
        return [far_first[d] for d in range(len(pieces))]

    def scatter_chips(chunk):
        far_first = {k: to_chip(chunk(k), k) for k in range(nz - 1, 0, -1)}
        return [chunk(0)] + [far_first[k] for k in range(1, nz)]

    def scatter_parts(keep, send):
        received = to_core(send)
        return scatter_chips(
            lambda k: lax.dynamic_index_in_dim(keep, z ^ k, 0, False)
            + lax.dynamic_index_in_dim(received, z ^ k, 0, False)
        )

    def scatter_sum(keep, send):
        return sum(scatter_parts(keep, send))

    def gather(x):
        far_first = {k: to_chip(x, k) for k in range(nz - 1, 0, -1)}
        own = [x] + [far_first[k] for k in range(1, nz)]
        return own + [to_core(item) for item in own]

    def leaf_sum(x, group):
        step = 1
        while step < group:
            x = x + to_leaf(x, step)
            step = step * 2
        return x

    def leaf_rows(x, l):
        return lax.dynamic_slice_in_dim(x, leaf * helds[l] // groups[l], helds[l], 0)

    def flat_rows(l, first, count):
        width_rows = index_rows[l].shape[1]
        at = lax.iota(jnp.int32, count * width_rows)[:, None, None]
        seps = lax.broadcasted_iota(jnp.int32, (1,) + index_rows[l].shape, 1)
        line = lax.broadcasted_iota(jnp.int32, (1,) + index_rows[l].shape, 2)
        wanted = (seps - first) * width_rows + line == at
        return jnp.sum(jnp.where(wanted, index_rows[l][None], 0), axis=(1, 2))

    all_rows = [None] + [flat_rows(l, 0, index_rows[l].shape[0]) for l in (1, 2, 3)]
    own_rows = [None] + [flat_rows(l, leaf * helds[l] // groups[l], helds[l]) for l in (1, 2, 3)]

    def other_groups(x, l):
        return [x] + [to_leaf(x, k * groups[l]) for k in range(1, leaves // groups[l])]

    def place(parts, l):
        out = jnp.zeros(rhs[l].shape, F32)
        for k, item in enumerate(parts):
            out = lax.dynamic_update_slice_in_dim(out, item, (leaf // groups[l] ^ k) * helds[l], 0)
        return out

    def halves(rows):
        return [shaped(nz, rows, width)] * 2

    def room(*dims):
        return pltpu.VMEM(dims, F32)

    def forward_inv(l, owed):
        return call(
            functools.partial(forward_inv_kernel, len(owed)),
            f"forward_inv_{l}",
            halves(chunks[l]),
            [room(spans[l], width)],
            6 * inv[l].size * width,
            1,
            meta,
            leaf_rows(rhs[l], l),
            *owed,
            inv[l],
        )

    solved = [None] * 4

    solved[3] = scatter_sum(*forward_inv(3, []))
    def forward_panel(l, below):
        parts = gather(solved[l])
        return call(
            functools.partial(forward_panel_kernel, len(parts), helds[l], sum(sizes[: l - 1]) // BLOCK, len(below)),
            f"forward_panel_{l}",
            halves(owned[l - 1]) + [shaped(helds[l] * listed[l] * BLOCK, width)],
            [room(sizes[l - 1], width), room(spans[l], width)],
            6 * panel[l].size * width,
            2 + len(below),
            meta,
            own_rows[l],
            *[own_rows[item] for item in below],
            *parts,
            *[updates[item] for item in below],
            panel[l],
        )

    updates = [None] * 4
    keep, send, updates[3] = forward_panel(3, [])

    def owed_parts(parts, l):
        return parts if groups[l] == 1 else [leaf_sum(sum(parts), groups[l])]

    solved[2] = scatter_sum(*forward_inv(2, owed_parts(scatter_parts(keep, send), 2)))
    keep, send, updates[2] = forward_panel(2, [3])
    parts = scatter_parts(keep, send)

    group, seps = groups[1], leaves // groups[1]
    height = BLOCK // group
    blocks = owned[0] // BLOCK
    parts = scatter_parts(*forward_inv(1, owed_parts(parts, 1)))
    top_keep, top_send = call(
        deferred_kernel,
        "deferred",
        halves(owned[0]),
        [room(sizes[0], width)],
        BESIDE,
        3,
        meta,
        own_rows[2],
        own_rows[3],
        after(updates[2], parts[0]),
        updates[3],
    )
    leaf_cuts = call(
        functools.partial(leaf_cuts_kernel, group),
        "leaf_cuts",
        [shaped(nz, owned[0] // leaves, width)] * leaves,
        [],
        0,
        1,
        meta,
        top_keep,
        to_core(top_send),
    )
    parts, leaf_cuts = lax.optimization_barrier((parts, leaf_cuts))
    deferred = to_leaves(leaf_cuts)
    solved[1] = sum(parts)

    parts = gather(solved[1])
    pieces = call(
        functools.partial(forward_last_kernel, len(parts), group),
        "forward_panel_1",
        [shaped(listed[1] * height + 8, width)] * group,
        [room(spans[1], width), room(panel[1].shape[1], width)],
        6 * panel[1].size * width,
        2,
        meta,
        own_rows[1],
        *parts,
        panel[1],
    )
    piece, deferred = sum(to_leaves(pieces)), sum(deferred)
    own = scatter_chips(
        lambda k: jnp.concatenate([piece, lax.dynamic_index_in_dim(deferred, z ^ k, 0, False)], axis=0)
    )
    owed = call(
        functools.partial(owed_top_kernel, nz, group, listed[1]),
        "owed_top",
        shaped(blocks * height, width),
        [],
        0,
        1,
        meta,
        *own,
        *[to_core(item[: piece.shape[0]]) for item in own],
    )
    keep, send = call(
        functools.partial(forward_top_kernel, leaves, group),
        "forward_inv_0",
        halves(chunks[0]),
        [room(owned[0], width), room(spans[0], width)],
        6 * inv[0].size * width,
        1,
        meta,
        rhs[0],
        *to_leaves([owed] * leaves),
        inv[0],
    )
    solved[0] = scatter_sum(keep, send)

    parts = gather(solved[0])
    pieces = call(
        functools.partial(backward_top_kernel, len(parts), leaves),
        "backward_inv_0",
        [shaped(owned[0] // leaves, width)] * leaves,
        [room(spans[0], width), room(owned[0], width)],
        6 * inv[0].size * width,
        1,
        meta,
        *parts,
        inv[0],
    )
    piece = sum(to_leaves(pieces))
    quarters = gather(piece)
    top_parts = to_leaves([beside(piece, piece)] * leaves)

    def picked(levels, name, quarters, cost):
        picks = call(
            functools.partial(pick_kernel, len(quarters), leaves, [(helds[l], groups[l], listed[l]) for l in levels]),
            name,
            [shaped(sum(helds[l] * listed[l] for l in levels) * (BLOCK // leaves), width)] * leaves,
            [room(sizes[0] // leaves, width)],
            cost,
            1 + len(levels),
            meta,
            *[all_rows[l] for l in levels],
            *quarters,
        )
        return to_leaves(picks)

    thin = BLOCK // leaves
    quarters, top_parts = lax.optimization_barrier((quarters, top_parts))
    top = jnp.zeros((blocks, leaves, thin, width), F32)
    for d, item in enumerate(top_parts):
        top = lax.dynamic_update_slice(top, item.reshape(blocks, 1, thin, width), (0, leaf ^ d, 0, 0))
    results = [top.reshape(rhs[0].shape)]
    picks = picked([1], "pick_1", quarters, 0)
    chain, parts = [], []
    for l in (1, 2, 3):
        above = sum(sizes[1:l])
        keep, send, *chain = call(
            functools.partial(
                backward_panel_kernel,
                len(parts),
                leaves,
                helds[l],
                sizes[0] // BLOCK,
                helds[2] * listed[2] * thin if l == 3 else 0,
                len(chain),
            ),
            f"backward_panel_{l}",
            halves(chunks[l]) + ([shaped(above, width)] if l > 1 else []),
            [
                room(panel[l].shape[1], width),
                pltpu.VMEM((panel[l].shape[1], 2 * width), BF16),
                room(spans[l], width),
            ],
            6 * panel[l].size * width,
            2,
            meta,
            own_rows[l],
            *picks,
            *parts,
            *chain,
            panel[l],
        )
        residue = solved[l] - scatter_sum(keep, send)
        if l == 1:
            picks = picked([2, 3], "pick_2_3", after(quarters, residue), BESIDE)
        x = call(
            backward_inv_kernel,
            f"backward_inv_{l}",
            shaped(helds[l], owned[l], width),
            [room(spans[l], width)],
            6 * inv[l].size * width,
            1,
            meta,
            *gather(residue),
            inv[l],
        )
        if l == 1:
            x, picks = lax.optimization_barrier((x, picks))
        x = leaf_sum(x, groups[l])
        if l < 3:
            parts = gather(x[0])
            placed = [x] + other_groups(beside(x, x), l)[1:]
            parts, placed = lax.optimization_barrier((parts, placed))
            results.append(place(placed, l))
    results.append(place(other_groups(x, 3), 3))
    return tuple(results)


def solution(mesh):
    across = P(None, "rows", None)
    return jax.shard_map(
        body,
        mesh=mesh,
        in_specs=(across,) * 4 + (P("rows", "leaf"),) * 4 + (P("leaf", "rows"),) * 3 + (P(None, "rows"),) * 3,
        out_specs=(across,) * 4,
        check_vma=False,
    )
```

time: 385 us -> 378 us (0.982)
  local copies, waits for them, and re-layouts: 15 us -> 8.73 us
    unnamed x55 -> x66, local copies, waits for them, and re-layouts: 12.7 us -> 6.56 us
    ppermute x28, waiting for transfers between devices: 32 us -> 36.7 us  [to_leaf(): lax.ppermute(x, 'leaf', [(i, i ^ k) for i in range(leaves)])]
    add x17 -> x22, other arithmetic: 6.55 us -> 2.26 us  [the longest x9 1.1 us: scatter_parts(): lax.dynamic_index_in_dim(keep, z ^ k, 0, False)]
    ppermute x63 -> x60, starting transfers between devices: 96 us -> 92.4 us  [to_chip(): return lax.ppermute(x, 'rows', [(r, r ^ 2 * k) for r in range(devices)])]
    ppermute x63 -> x60, waiting for transfers between devices: 142 us -> 139 us  [to_chip(): return lax.ppermute(x, 'rows', [(r, r ^ 2 * k) for r in range(devices)])]
    pallas_call x17 -> x19, Pallas kernels: 25.4 us -> 26.3 us  [call(): pl.pallas_call(kernel, out_shape=outs, in_specs=[SMEM] * smem_count + [VM...]
  transfers between devices with their start and end apart: 145 -> 142, of which waited for: 87 -> 83; matrix products, arithmetic and copies ran while one was open for 2% -> 1% of each run, Pallas kernels for 1% -> 1%
where the time goes in v3:
time: 378 us
  waiting for transfers between devices  201 us (53%)
  starting transfers between devices  136 us (36%)
  Pallas kernels  26.3 us (7%)
  local copies, waits for them, and re-layouts  8.73 us (2%)
  other arithmetic  4.22 us (1%)
    ppermute x60, waiting for transfers between devices, to_chip(): return lax.ppermute(x, 'rows', [(r, r ^ 2 * k) for r in range(devices)])  139 us
    ppermute x60, starting transfers between devices, to_chip(): return lax.ppermute(x, 'rows', [(r, r ^ 2 * k) for r in range(devices)])  92.4 us
    ppermute x28, waiting for transfers between devices, to_leaf(): lax.ppermute(x, 'leaf', [(i, i ^ k) for i in range(leaves)])  36.7 us
    ppermute x28, starting transfers between devices, to_leaf(): lax.ppermute(x, 'leaf', [(i, i ^ k) for i in range(leaves)])  33.9 us
    pallas_call x19, Pallas kernels, call(): pl.pallas_call(kernel, out_shape=outs, in_specs=[SMEM] * smem_count + [VM...  26.3 us
    ppermute x54, waiting for transfers between devices, to_core(): return lax.ppermute(x, 'rows', [(r, r ^ 1) for r in range(devices)])  25.3 us
    ppermute x54, starting transfers between devices, to_core(): return lax.ppermute(x, 'rows', [(r, r ^ 1) for r in range(devices)])  9.21 us
  transfers between devices with their start and end apart: 142, of which 83 were waited for; matrix products, arithmetic and copies ran while one was open for 1% of the time, Pallas kernels for 1%

profile of v3, /device:TPU:0, one launch (start us, length us, event | category | flops | bytes accessed | tf_op | source)
XLA Modules:
  0.0 377.6 jit_solution(5295496554200497834)
XLA Ops:
  6.3 3.0 collective-permute-start.1
  11.9 3.1 collective-permute-done.1
  15.0 7.2 %collective-permute-done.2 = f32[256,128]{1,0:T(8,128)S(1)} collective-permute-done((f32[256,128]{1,0:T(8,128)S(1)}, f32[256,128]{1,0:T(8,128)S(1)}, u32[]{:S(2)}, u32[]{:S(2)}) %collective-permute-start.2) | collective-permute-done | bytes 131104 | tf_op jit(solution)/shard_map/ppermute | solution.py:335
  26.7 3.7 collective-permute-done.6.refs_3_
  31.1 4.9 %collective-permute-done.5.refs_2_ = f32[256,128]{1,0:T(8,128)S(1)} collective-permute-done((f32[256,128]{1,0:T(8,128)S(1)}, f32[256,128]{1,0:T(8,128)S(1)}, u32[]{:S(2)}, u32[]{:S(2)}) %collective-permute-start.5) | collective-permute-done | bytes 131104 | tf_op jit(solution)/shard_map/ppermute | solution.py:335
  44.5 3.0 collective-permute-start.13
  49.8 2.8 collective-permute-done.12.refs_1_
  52.5 5.1 %collective-permute-done.13.refs_2_ = f32[256,128]{1,0:T(8,128)S(1)} collective-permute-done((f32[256,128]{1,0:T(8,128)}, f32[256,128]{1,0:T(8,128)S(1)}, u32[]{:S(2)}, u32[]{:S(2)}) %collective-permute-start.13) | collective-permute-done | bytes 131104 | tf_op jit(solution)/shard_map/ppermute | solution.py:335
  66.8 3.2 collective-permute-done.16
  70.0 7.3 %collective-permute-done.17 = f32[256,128]{1,0:T(8,128)S(1)} collective-permute-done((f32[256,128]{1,0:T(8,128)S(1)}, f32[256,128]{1,0:T(8,128)S(1)}, u32[]{:S(2)}, u32[]{:S(2)}) %collective-permute-start.17) | collective-permute-done | bytes 131104 | tf_op jit(solution)/shard_map/ppermute | solution.py:335
  83.9 7.9 %collective-permute-done.20.refs_3_ = f32[256,128]{1,0:T(8,128)S(1)} collective-permute-done((f32[256,128]{1,0:T(8,128)S(1)}, f32[256,128]{1,0:T(8,128)S(1)}, u32[]{:S(2)}, u32[]{:S(2)}) %collective-permute-start.20) | collective-permute-done | bytes 131104 | tf_op jit(solution)/shard_map/ppermute | solution.py:335
  101.9 3.2 collective-permute-done.27
  105.2 7.0 %collective-permute-done.28 = f32[256,128]{1,0:T(8,128)S(1)} collective-permute-done((f32[256,128]{1,0:T(8,128)S(1)}, f32[256,128]{1,0:T(8,128)S(1)}, u32[]{:S(2)}, u32[]{:S(2)}) %collective-permute-start.28) | collective-permute-done | bytes 131104 | tf_op jit(solution)/shard_map/ppermute | solution.py:335
  115.3 2.9 collective-permute-done.30
  129.9 5.3 %collective-permute-done.33 = f32[128,128]{1,0:T(8,128)S(1)} collective-permute-done((f32[128,128]{1,0:T(8,128)S(1)}, f32[128,128]{1,0:T(8,128)S(1)}, u32[]{:S(2)}, u32[]{:S(2)}) %collective-permute-start.33) | collective-permute-done | bytes 65568 | tf_op jit(solution)/shard_map/ppermute | solution.py:335
  150.9 4.6 %collective-permute-done.43 = f32[136,128]{1,0:T(8,128)S(1)} collective-permute-done((f32[136,128]{1,0:T(8,128)S(1)}, f32[136,128]{1,0:T(8,128)S(1)}, u32[]{:S(2)}, u32[]{:S(2)}) %collective-permute-start.43) | collective-permute-done | bytes 69664 | tf_op jit(solution)/shard_map/ppermute | solution.py:338
  162.9 6.4 %collective-permute-done.48.refs_2_ = f32[264,128]{1,0:T(8,128)S(1)} collective-permute-done((f32[264,128]{1,0:T(8,128)S(1)}, f32[264,128]{1,0:T(8,128)S(1)}, u32[]{:S(2)}, u32[]{:S(2)}) %collective-permute-start.48) | collective-permute-done | bytes 135200 | tf_op jit(solution)/shard_map/ppermute | solution.py:335
  177.7 3.7 collective-permute-done.55.refs_2_
  189.0 5.5 %collective-permute-done.59 = f32[128,128]{1,0:T(8,128)S(1)} collective-permute-done((f32[128,128]{1,0:T(8,128)S(1)}, f32[128,128]{1,0:T(8,128)S(1)}, u32[]{:S(2)}, u32[]{:S(2)}) %collective-permute-start.59) | collective-permute-done | bytes 65568 | tf_op jit(solution)/shard_map/ppermute | solution.py:335
  199.5 4.1 %collective-permute-done.62.refs_2_ = f32[128,128]{1,0:T(8,128)S(1)} collective-permute-done((f32[128,128]{1,0:T(8,128)S(1)}, f32[128,128]{1,0:T(8,128)S(1)}, u32[]{:S(2)}, u32[]{:S(2)}) %collective-permute-start.62) | collective-permute-done | bytes 65568 | tf_op jit(solution)/shard_map/ppermute | solution.py:335
  240.8 3.5 collective-permute-done.86
  260.0 4.4 %collective-permute-done.98 = f32[1,256,128]{2,1,0:T(8,128)S(1)} collective-permute-done((f32[1,256,128]{2,1,0:T(8,128)S(1)}, f32[1,256,128]{2,1,0:T(8,128)S(1)}, u32[]{:S(2)}, u32[]{:S(2)}) %collective-permute-start.98) | collective-permute-done | bytes 131104 | tf_op jit(solution)/shard_map/ppermute | solution.py:338
  270.9 3.7 collective-permute-done.100.refs_6_
  284.8 3.1 collective-permute-done.108
  287.9 7.2 %collective-permute-done.109 = f32[256,128]{1,0:T(8,128)S(1)} collective-permute-done((f32[256,128]{1,0:T(8,128)S(1)}, f32[256,128]{1,0:T(8,128)S(1)}, u32[]{:S(2)}, u32[]{:S(2)}) %collective-permute-start.109) | collective-permute-done | bytes 131104 | tf_op jit(solution)/shard_map/ppermute | solution.py:335
  301.5 8.0 %collective-permute-done.112.refs_2_ = f32[256,128]{1,0:T(8,128)S(1)} collective-permute-done((f32[256,128]{1,0:T(8,128)S(1)}, f32[256,128]{1,0:T(8,128)S(1)}, u32[]{:S(2)}, u32[]{:S(2)}) %collective-permute-start.112) | collective-permute-done | bytes 131104 | tf_op jit(solution)/shard_map/ppermute | solution.py:335
  321.3 6.0 %collective-permute-done.119.refs_6_ = f32[256,128]{1,0:T(8,128)S(1)} collective-permute-done((f32[256,128]{1,0:T(8,128)S(1)}, f32[256,128]{1,0:T(8,128)S(1)}, u32[]{:S(2)}, u32[]{:S(2)}) %collective-permute-start.119) | collective-permute-done | bytes 131104 | tf_op jit(solution)/shard_map/ppermute | solution.py:335
  329.3 3.5 backward_panel_3.1
  339.5 3.0 collective-permute-done.129
  342.5 7.4 %collective-permute-done.130 = f32[256,128]{1,0:T(8,128)S(1)} collective-permute-done((f32[256,128]{1,0:T(8,128)S(1)}, f32[256,128]{1,0:T(8,128)S(1)}, u32[]{:S(2)}, u32[]{:S(2)}) %collective-permute-start.130) | collective-permute-done | bytes 131104 | tf_op jit(solution)/shard_map/ppermute | solution.py:335
  356.3 8.0 %collective-permute-done.133.refs_2_ = f32[256,128]{1,0:T(8,128)S(1)} collective-permute-done((f32[256,128]{1,0:T(8,128)S(1)}, f32[256,128]{1,0:T(8,128)S(1)}, u32[]{:S(2)}, u32[]{:S(2)}) %collective-permute-start.133) | collective-permute-done | bytes 131104 | tf_op jit(solution)/shard_map/ppermute | solution.py:335
  372.9 3.9 %collective-permute-done.140 = f32[2,128,128]{2,1,0:T(8,128)S(1)} collective-permute-done((f32[2,128,128]{2,1,0:T(8,128)S(1)}, f32[2,128,128]{2,1,0:T(8,128)S(1)}, u32[]{:S(2)}, u32[]{:S(2)}) %collective-permute-start.140) | collective-permute-done | bytes 131104 | tf_op jit(solution)/shard_map/ppermute | solution.py:338
  (407 shorter events, 220.7 us)
Async XLA Ops:
  9.3 12.9 %collective-permute-start.2 = (f32[256,128]{1,0:T(8,128)S(1)}, f32[256,128]{1,0:T(8,128)S(1)}, u32[]{:S(2)}, u32[]{:S(2)}) collective-permute-start(f32[256,128]{1,0:T(8,128)S(1)} %get-tuple-element.216), channel_id=1, source_target_pairs={{0,4},{1,5},{2,6},{3,7},{4,0},{5,1},{6,2},{7,3},{8,12},{9,13},{10,... | collective-permute-start | bytes 393224 | tf_op jit(solution)/shard_map/ppermute | solution.py:335
  11.9 10.3 %collective-permute-start.3 = (f32[256,128]{1,0:T(8,128)S(1)}, f32[256,128]{1,0:T(8,128)S(1)}, u32[]{:S(2)}, u32[]{:S(2)}) collective-permute-start(f32[256,128]{1,0:T(8,128)S(1)} %get-tuple-element.215), channel_id=1, source_target_pairs={{0,6},{1,7},{2,4},{3,5},{4,2},{5,3},{6,0},{7,1},{8,14},{9,15},{10,... | collective-permute-start | bytes 393224 | tf_op jit(solution)/shard_map/ppermute | solution.py:335
  26.2 9.9 %collective-permute-start.5 = (f32[256,128]{1,0:T(8,128)S(1)}, f32[256,128]{1,0:T(8,128)S(1)}, u32[]{:S(2)}, u32[]{:S(2)}) collective-permute-start(f32[256,128]{1,0:T(8,128)S(1)} %fusion.11.refs_0_), channel_id=1, source_target_pairs={{0,4},{1,5},{2,6},{3,7},{4,0},{5,1},{6,2},{7,3},{8,12},{9,13},{10,... | collective-permute-start | bytes 393224 | tf_op jit(solution)/shard_map/ppermute | solution.py:335
  44.5 13.1 %collective-permute-start.13 = (f32[256,128]{1,0:T(8,128)}, f32[256,128]{1,0:T(8,128)S(1)}, u32[]{:S(2)}, u32[]{:S(2)}) collective-permute-start(f32[256,128]{1,0:T(8,128)} %get-tuple-element.211), channel_id=1, source_target_pairs={{0,4},{1,5},{2,6},{3,7},{4,0},{5,1},{6,2},{7,3},{8,12},{9,13},{10,... | collective-permute-start | bytes 393224 | tf_op jit(solution)/shard_map/ppermute | solution.py:335
  47.4 10.2 %collective-permute-start.14 = (f32[256,128]{1,0:T(8,128)}, f32[256,128]{1,0:T(8,128)}, u32[]{:S(2)}, u32[]{:S(2)}) collective-permute-start(f32[256,128]{1,0:T(8,128)} %get-tuple-element.210), channel_id=1, source_target_pairs={{0,6},{1,7},{2,4},{3,5},{4,2},{5,3},{6,0},{7,1},{8,14},{9,15},{10,... | collective-permute-start | bytes 393224 | tf_op jit(solution)/shard_map/ppermute | solution.py:335
  64.3 12.9 %collective-permute-start.17 = (f32[256,128]{1,0:T(8,128)S(1)}, f32[256,128]{1,0:T(8,128)S(1)}, u32[]{:S(2)}, u32[]{:S(2)}) collective-permute-start(f32[256,128]{1,0:T(8,128)S(1)} %get-tuple-element.209), channel_id=1, source_target_pairs={{0,4},{1,5},{2,6},{3,7},{4,0},{5,1},{6,2},{7,3},{8,12},{9,13},{10,... | collective-permute-start | bytes 393224 | tf_op jit(solution)/shard_map/ppermute | solution.py:335
  65.3 11.9 %collective-permute-start.18 = (f32[256,128]{1,0:T(8,128)S(1)}, f32[256,128]{1,0:T(8,128)S(1)}, u32[]{:S(2)}, u32[]{:S(2)}) collective-permute-start(f32[256,128]{1,0:T(8,128)S(1)} %get-tuple-element.208), channel_id=1, source_target_pairs={{0,6},{1,7},{2,4},{3,5},{4,2},{5,3},{6,0},{7,1},{8,14},{9,15},{10,... | collective-permute-start | bytes 393224 | tf_op jit(solution)/shard_map/ppermute | solution.py:335
  79.6 12.1 %collective-permute-start.20 = (f32[256,128]{1,0:T(8,128)S(1)}, f32[256,128]{1,0:T(8,128)S(1)}, u32[]{:S(2)}, u32[]{:S(2)}) collective-permute-start(f32[256,128]{1,0:T(8,128)S(1)} %fusion.9.refs_1_), channel_id=1, source_target_pairs={{0,4},{1,5},{2,6},{3,7},{4,0},{5,1},{6,2},{7,3},{8,12},{9,13},{10,... | collective-permute-start | bytes 393224 | tf_op jit(solution)/shard_map/ppermute | solution.py:335
  80.6 11.2 %collective-permute-start.21 = (f32[256,128]{1,0:T(8,128)S(1)}, f32[256,128]{1,0:T(8,128)S(1)}, u32[]{:S(2)}, u32[]{:S(2)}) collective-permute-start(f32[256,128]{1,0:T(8,128)S(1)} %fusion.9.refs_1_), channel_id=1, source_target_pairs={{0,6},{1,7},{2,4},{3,5},{4,2},{5,3},{6,0},{7,1},{8,14},{9,15},{10,... | collective-permute-start | bytes 393224 | tf_op jit(solution)/shard_map/ppermute | solution.py:335
  82.1 10.4 %collective-permute-start.22 = (f32[256,128]{1,0:T(8,128)S(1)}, f32[256,128]{1,0:T(8,128)S(1)}, u32[]{:S(2)}, u32[]{:S(2)}) collective-permute-start(f32[256,128]{1,0:T(8,128)S(1)} %fusion.9.refs_1_), channel_id=1, source_target_pairs={{0,1},{1,0},{2,3},{3,2},{4,5},{5,4},{6,7},{7,6},{8,9},{9,8},{10,11... | collective-permute-start | bytes 393224 | tf_op jit(solution)/shard_map/ppermute | solution.py:332
  99.3 12.9 %collective-permute-start.28 = (f32[256,128]{1,0:T(8,128)S(1)}, f32[256,128]{1,0:T(8,128)S(1)}, u32[]{:S(2)}, u32[]{:S(2)}) collective-permute-start(f32[256,128]{1,0:T(8,128)S(1)} %get-tuple-element.206), channel_id=1, source_target_pairs={{0,4},{1,5},{2,6},{3,7},{4,0},{5,1},{6,2},{7,3},{8,12},{9,13},{10,... | collective-permute-start | bytes 393224 | tf_op jit(solution)/shard_map/ppermute | solution.py:335
  100.3 11.9 %collective-permute-start.29 = (f32[256,128]{1,0:T(8,128)S(1)}, f32[256,128]{1,0:T(8,128)S(1)}, u32[]{:S(2)}, u32[]{:S(2)}) collective-permute-start(f32[256,128]{1,0:T(8,128)S(1)} %get-tuple-element.205), channel_id=1, source_target_pairs={{0,6},{1,7},{2,4},{3,5},{4,2},{5,3},{6,0},{7,1},{8,14},{9,15},{10,... | collective-permute-start | bytes 393224 | tf_op jit(solution)/shard_map/ppermute | solution.py:335
  139.7 15.9 %collective-permute-start.44 = (f32[4,128,128]{2,1,0:T(8,128)S(1)}, f32[4,128,128]{2,1,0:T(8,128)S(1)}, u32[]{:S(2)}, u32[]{:S(2)}) collective-permute-start(f32[4,128,128]{2,1,0:T(8,128)S(1)} %get-tuple-element.127), channel_id=1, source_target_pairs={{0,8},{8,0},{16,24},{24,16},{1,9},{9,1},{17,25},{25,17},{2,10},{10... | collective-permute-start | bytes 786440 | tf_op jit(solution)/shard_map/ppermute | solution.py:338
  141.2 14.5 %collective-permute-start.45 = (f32[4,128,128]{2,1,0:T(8,128)S(1)}, f32[4,128,128]{2,1,0:T(8,128)S(1)}, u32[]{:S(2)}, u32[]{:S(2)}) collective-permute-start(f32[4,128,128]{2,1,0:T(8,128)S(1)} %get-tuple-element.128), channel_id=1, source_target_pairs={{0,16},{8,24},{16,0},{24,8},{1,17},{9,25},{17,1},{25,9},{2,18},{10... | collective-permute-start | bytes 786440 | tf_op jit(solution)/shard_map/ppermute | solution.py:338
  144.3 11.3 %collective-permute-start.46 = (f32[4,128,128]{2,1,0:T(8,128)S(1)}, f32[4,128,128]{2,1,0:T(8,128)S(1)}, u32[]{:S(2)}, u32[]{:S(2)}) collective-permute-start(f32[4,128,128]{2,1,0:T(8,128)S(1)} %get-tuple-element.129), channel_id=1, source_target_pairs={{0,24},{8,16},{16,8},{24,0},{1,25},{9,17},{17,9},{25,1},{2,26},{10... | collective-permute-start | bytes 786440 | tf_op jit(solution)/shard_map/ppermute | solution.py:338
  156.3 13.0 %collective-permute-start.48 = (f32[264,128]{1,0:T(8,128)S(1)}, f32[264,128]{1,0:T(8,128)S(1)}, u32[]{:S(2)}, u32[]{:S(2)}) collective-permute-start(f32[264,128]{1,0:T(8,128)S(1)} %get-tuple-element.233), channel_id=1, source_target_pairs={{0,4},{1,5},{2,6},{3,7},{4,0},{5,1},{6,2},{7,3},{8,12},{9,13},{10,... | collective-permute-start | bytes 405512 | tf_op jit(solution)/shard_map/ppermute | solution.py:335
  158.4 10.9 %collective-permute-start.49 = (f32[264,128]{1,0:T(8,128)S(1)}, f32[264,128]{1,0:T(8,128)S(1)}, u32[]{:S(2)}, u32[]{:S(2)}) collective-permute-start(f32[264,128]{1,0:T(8,128)S(1)} %get-tuple-element.231), channel_id=1, source_target_pairs={{0,6},{1,7},{2,4},{3,5},{4,2},{5,3},{6,0},{7,1},{8,14},{9,15},{10,... | collective-permute-start | bytes 405512 | tf_op jit(solution)/shard_map/ppermute | solution.py:335
  160.2 9.7 %collective-permute-start.50 = (f32[136,128]{1,0:T(8,128)S(1)}, f32[136,128]{1,0:T(8,128)S(1)}, u32[]{:S(2)}, u32[]{:S(2)}) collective-permute-start(f32[136,128]{1,0:T(8,128)S(1)} %add.557), channel_id=1, source_target_pairs={{0,1},{1,0},{2,3},{3,2},{4,5},{5,4},{6,7},{7,6},{8,9},{9,8},{10,11... | collective-permute-start | bytes 208904 | tf_op jit(solution)/shard_map/ppermute | solution.py:332
  264.5 10.0 %collective-permute-start.100 = (f32[256,128]{1,0:T(8,128)S(1)}, f32[256,128]{1,0:T(8,128)S(1)}, u32[]{:S(2)}, u32[]{:S(2)}) collective-permute-start(f32[256,128]{1,0:T(8,128)S(1)} %bitcast.133), channel_id=1, source_target_pairs={{0,4},{1,5},{2,6},{3,7},{4,0},{5,1},{6,2},{7,3},{8,12},{9,13},{10,... | collective-permute-start | bytes 393224 | tf_op jit(solution)/shard_map/ppermute | solution.py:335
  282.2 12.9 %collective-permute-start.109 = (f32[256,128]{1,0:T(8,128)S(1)}, f32[256,128]{1,0:T(8,128)S(1)}, u32[]{:S(2)}, u32[]{:S(2)}) collective-permute-start(f32[256,128]{1,0:T(8,128)S(1)} %get-tuple-element.203), channel_id=1, source_target_pairs={{0,4},{1,5},{2,6},{3,7},{4,0},{5,1},{6,2},{7,3},{8,12},{9,13},{10,... | collective-permute-start | bytes 393224 | tf_op jit(solution)/shard_map/ppermute | solution.py:335
  282.9 12.2 %collective-permute-start.110 = (f32[256,128]{1,0:T(8,128)S(1)}, f32[256,128]{1,0:T(8,128)S(1)}, u32[]{:S(2)}, u32[]{:S(2)}) collective-permute-start(f32[256,128]{1,0:T(8,128)S(1)} %get-tuple-element.202), channel_id=1, source_target_pairs={{0,6},{1,7},{2,4},{3,5},{4,2},{5,3},{6,0},{7,1},{8,14},{9,15},{10,... | collective-permute-start | bytes 393224 | tf_op jit(solution)/shard_map/ppermute | solution.py:335
  297.5 11.9 %collective-permute-start.112 = (f32[256,128]{1,0:T(8,128)S(1)}, f32[256,128]{1,0:T(8,128)S(1)}, u32[]{:S(2)}, u32[]{:S(2)}) collective-permute-start(f32[256,128]{1,0:T(8,128)S(1)} %fusion.5.refs_0_), channel_id=1, source_target_pairs={{0,4},{1,5},{2,6},{3,7},{4,0},{5,1},{6,2},{7,3},{8,12},{9,13},{10,... | collective-permute-start | bytes 393224 | tf_op jit(solution)/shard_map/ppermute | solution.py:335
  298.1 11.4 %collective-permute-start.113 = (f32[256,128]{1,0:T(8,128)S(1)}, f32[256,128]{1,0:T(8,128)S(1)}, u32[]{:S(2)}, u32[]{:S(2)}) collective-permute-start(f32[256,128]{1,0:T(8,128)S(1)} %fusion.5.refs_0_), channel_id=1, source_target_pairs={{0,6},{1,7},{2,4},{3,5},{4,2},{5,3},{6,0},{7,1},{8,14},{9,15},{10,... | collective-permute-start | bytes 393224 | tf_op jit(solution)/shard_map/ppermute | solution.py:335
  300.0 10.0 %collective-permute-start.114 = (f32[256,128]{1,0:T(8,128)S(1)}, f32[256,128]{1,0:T(8,128)S(1)}, u32[]{:S(2)}, u32[]{:S(2)}) collective-permute-start(f32[256,128]{1,0:T(8,128)S(1)} %fusion.5.refs_0_), channel_id=1, source_target_pairs={{0,1},{1,0},{2,3},{3,2},{4,5},{5,4},{6,7},{7,6},{8,9},{9,8},{10,11... | collective-permute-start | bytes 393224 | tf_op jit(solution)/shard_map/ppermute | solution.py:332
  314.4 12.9 %collective-permute-start.119 = (f32[256,128]{1,0:T(8,128)S(1)}, f32[256,128]{1,0:T(8,128)S(1)}, u32[]{:S(2)}, u32[]{:S(2)}) collective-permute-start(f32[256,128]{1,0:T(8,128)S(1)} %bitcast.138), channel_id=1, source_target_pairs={{0,4},{1,5},{2,6},{3,7},{4,0},{5,1},{6,2},{7,3},{8,12},{9,13},{10,... | collective-permute-start | bytes 393224 | tf_op jit(solution)/shard_map/ppermute | solution.py:335
  314.9 12.3 %collective-permute-start.120 = (f32[256,128]{1,0:T(8,128)S(1)}, f32[256,128]{1,0:T(8,128)S(1)}, u32[]{:S(2)}, u32[]{:S(2)}) collective-permute-start(f32[256,128]{1,0:T(8,128)S(1)} %bitcast.139), channel_id=1, source_target_pairs={{0,6},{1,7},{2,4},{3,5},{4,2},{5,3},{6,0},{7,1},{8,14},{9,15},{10,... | collective-permute-start | bytes 393224 | tf_op jit(solution)/shard_map/ppermute | solution.py:335
  316.8 11.0 %collective-permute-start.125 = (f32[1,256,128]{2,1,0:T(8,128)S(1)}, f32[1,256,128]{2,1,0:T(8,128)S(1)}, u32[]{:S(2)}, u32[]{:S(2)}) collective-permute-start(f32[1,256,128]{2,1,0:T(8,128)S(1)} %beside.5), channel_id=1, source_target_pairs={{0,8},{8,0},{16,24},{24,16},{1,9},{9,1},{17,25},{25,17},{2,10},{10... | collective-permute-start | bytes 393224 | tf_op jit(solution)/shard_map/ppermute | solution.py:338
  337.0 12.9 %collective-permute-start.130 = (f32[256,128]{1,0:T(8,128)S(1)}, f32[256,128]{1,0:T(8,128)S(1)}, u32[]{:S(2)}, u32[]{:S(2)}) collective-permute-start(f32[256,128]{1,0:T(8,128)S(1)} %get-tuple-element.200), channel_id=1, source_target_pairs={{0,4},{1,5},{2,6},{3,7},{4,0},{5,1},{6,2},{7,3},{8,12},{9,13},{10,... | collective-permute-start | bytes 393224 | tf_op jit(solution)/shard_map/ppermute | solution.py:335
  337.5 12.3 %collective-permute-start.131 = (f32[256,128]{1,0:T(8,128)S(1)}, f32[256,128]{1,0:T(8,128)S(1)}, u32[]{:S(2)}, u32[]{:S(2)}) collective-permute-start(f32[256,128]{1,0:T(8,128)S(1)} %get-tuple-element.199), channel_id=1, source_target_pairs={{0,6},{1,7},{2,4},{3,5},{4,2},{5,3},{6,0},{7,1},{8,14},{9,15},{10,... | collective-permute-start | bytes 393224 | tf_op jit(solution)/shard_map/ppermute | solution.py:335
  352.3 11.9 %collective-permute-start.133 = (f32[256,128]{1,0:T(8,128)S(1)}, f32[256,128]{1,0:T(8,128)S(1)}, u32[]{:S(2)}, u32[]{:S(2)}) collective-permute-start(f32[256,128]{1,0:T(8,128)S(1)} %fusion.2.refs_0_), channel_id=1, source_target_pairs={{0,4},{1,5},{2,6},{3,7},{4,0},{5,1},{6,2},{7,3},{8,12},{9,13},{10,... | collective-permute-start | bytes 393224 | tf_op jit(solution)/shard_map/ppermute | solution.py:335
  352.9 11.4 %collective-permute-start.134 = (f32[256,128]{1,0:T(8,128)S(1)}, f32[256,128]{1,0:T(8,128)S(1)}, u32[]{:S(2)}, u32[]{:S(2)}) collective-permute-start(f32[256,128]{1,0:T(8,128)S(1)} %fusion.2.refs_0_), channel_id=1, source_target_pairs={{0,6},{1,7},{2,4},{3,5},{4,2},{5,3},{6,0},{7,1},{8,14},{9,15},{10,... | collective-permute-start | bytes 393224 | tf_op jit(solution)/shard_map/ppermute | solution.py:335
  354.9 10.0 %collective-permute-start.135 = (f32[256,128]{1,0:T(8,128)S(1)}, f32[256,128]{1,0:T(8,128)S(1)}, u32[]{:S(2)}, u32[]{:S(2)}) collective-permute-start(f32[256,128]{1,0:T(8,128)S(1)} %fusion.2.refs_0_), channel_id=1, source_target_pairs={{0,1},{1,0},{2,3},{3,2},{4,5},{5,4},{6,7},{7,6},{8,9},{9,8},{10,11... | collective-permute-start | bytes 393224 | tf_op jit(solution)/shard_map/ppermute | solution.py:332
  (143 other events, 1106.0 us)

commit v4 on v3

--- a/solution.py
+++ b/solution.py
@@ -71,15 +71,15 @@
     split_cores(meta, full, 0, *halves)
 
 
-def forward_top_kernel(leaves, group, meta, rhs, *refs):
+def forward_top_kernel(leaves, meta, rhs, *refs):
     owed, (inv, keep, send, source, full) = refs[:leaves], refs[leaves:]
-    rows = BLOCK // group
+    height = BLOCK // leaves
     source[...] = rhs[0]
     for d in range(leaves):
-        place = lax.rem(jnp.bitwise_xor(meta[2], d), group) * rows
+        place = jnp.bitwise_xor(meta[2], d) * height
         for b in range(rhs.shape[1] // BLOCK):
-            at = pl.ds(pl.multiple_of(b * BLOCK + place, 8), rows)
-            source[at, :] = source[at, :] - owed[d][b * rows : (b + 1) * rows, :]
+            at = pl.ds(pl.multiple_of(b * BLOCK + place, 8), height)
+            source[at, :] = source[at, :] - owed[d][b * height : (b + 1) * height, :]
     factor = wide(source[...])
     tile = tile_of(inv.shape[1])
     for start in range(0, inv.shape[1], tile):
@@ -123,65 +123,67 @@
 
 
 def deferred_kernel(meta, upper_rows, lower_rows, upper, lower, keep, send, chain):
+    leaves, count, rows = keep.shape[:3]
+    height = BLOCK // leaves
+    blocks = rows // height
     chain[...] = jnp.zeros_like(chain)
     add_blocks(chain, upper_rows, upper, 0)
     add_blocks(chain, lower_rows, lower, 0)
-    split_cores(meta, chain, 0, keep, send)
-
-
-def leaf_cuts_kernel(group, meta, keep, received, *cuts):
-    count = keep.shape[1] // BLOCK * group // len(cuts)
-    height = BLOCK // group
+    for i in range(leaves):
+        for k in range(count):
+            for b in range(blocks):
+                line = slice(b * height, (b + 1) * height)
+                own = ((2 * k + meta[1]) * blocks + b) * BLOCK + i * height
+                other = ((2 * k + 1 - meta[1]) * blocks + b) * BLOCK + i * height
+                keep[i, k, line, :] = chain[pl.ds(pl.multiple_of(own, 8), height), :]
+                send[i, k, line, :] = chain[pl.ds(pl.multiple_of(other, 8), height), :]
+
+
+def leaf_cuts_kernel(meta, keep, received, dependency, *cuts):
     for d, cut in enumerate(cuts):
         other = jnp.bitwise_xor(meta[2], d)
-        for b in range(count):
-            row = ((other // group) * count + b) * BLOCK + lax.rem(other, group) * height
-            at = pl.ds(pl.multiple_of(row, 8), height)
-            for k in range(keep.shape[0]):
-                cut[k, b * height : (b + 1) * height, :] = keep[k, at, :] + received[k, at, :]
-
-
-def forward_last_kernel(count, group, meta, rows, *refs):
-    parts, refs = refs[:count], refs[count:]
+        cut[...] = keep[other] + received[other]
+
+
+def forward_last_kernel(nz, group, leaves, meta, rows, *refs):
+    parts, refs = refs[: 2 * nz], refs[2 * nz :]
     panel, pieces, (full, update) = refs[0], refs[1:-2], refs[-2:]
     spread_parts(meta, full, parts)
     update[...] = panel_update(panel, full, 0, 1)
     listed = rows.shape[0]
-    height = BLOCK // group
-    for d in range(group):
-        place = jnp.bitwise_xor(lax.rem(meta[2], group), d) * height
+    height = BLOCK // leaves
+    for d in range(leaves):
+        place = jnp.bitwise_xor(meta[2], d) * height
         for k in range(listed):
             at = pl.ds(pl.multiple_of(k * BLOCK + place, 8), height)
             pieces[d][k * height : (k + 1) * height, :] = update[at, :]
         tail = pieces[d].shape[0] - listed * height
         numbers = jnp.zeros((tail, update.shape[1]), F32)
-        if d == 0:
+        if d % group == 0:
             line = lax.broadcasted_iota(jnp.int32, numbers.shape, 0)
             for k in range(listed):
                 numbers = jnp.where(line == k, rows[k].astype(F32), numbers)
         pieces[d][listed * height :, :] = numbers
 
 
-def owed_top_kernel(nz, group, listed, meta, *refs):
+def owed_top_kernel(listed, height, meta, *refs):
     parts, owed = refs[:-1], refs[-1]
-    height = BLOCK // group
     blocks = owed.shape[0] // height
+    start = parts[-1].shape[0]
+    size = listed * height + 8
     first = (2 * meta[0] + meta[1]) * blocks
     for b in range(blocks):
         wanted = (first + b).astype(F32)
         total = jnp.zeros((height, owed.shape[1]), F32)
         for item in parts:
-            for k in range(listed):
-                number = item[listed * height + k : listed * height + k + 1, :]
-                total = total + jnp.where(number == wanted, item[k * height : (k + 1) * height, :], 0.0)
+            if item.shape[0] > start:
+                total = total + item[start + b * height : start + (b + 1) * height, :]
+            for at in range(0, start, size):
+                for k in range(listed):
+                    number = item[at + listed * height + k : at + listed * height + k + 1, :]
+                    term = item[at + k * height : at + (k + 1) * height, :]
+                    total = total + jnp.where(number == wanted, term, 0.0)
         owed[b * height : (b + 1) * height, :] = total
-    start = parts[nz].shape[0]
-    count = parts[0].shape[0] - start
-    at = pl.ds(pl.multiple_of((meta[2] // group) * count, 8), count)
-    total = owed[at, :]
-    for item in parts[:nz]:
-        total = total + item[start:, :]
-    owed[at, :] = total
 
 
 def pick_kernel(count, leaves, levels, meta, *refs):
@@ -378,8 +380,10 @@
         wanted = (seps - first) * width_rows + line == at
         return jnp.sum(jnp.where(wanted, index_rows[l][None], 0), axis=(1, 2))
 
-    all_rows = [None] + [flat_rows(l, 0, index_rows[l].shape[0]) for l in (1, 2, 3)]
-    own_rows = [None] + [flat_rows(l, leaf * helds[l] // groups[l], helds[l]) for l in (1, 2, 3)]
+    def small_arrays():
+        own = [flat_rows(l, leaf * helds[l] // groups[l], helds[l]) for l in (1, 2, 3)]
+        every = [flat_rows(l, 0, index_rows[l].shape[0]) for l in (1, 2, 3)]
+        return own, every, [leaf_rows(rhs[l], l) for l in (1, 2)]
 
     def other_groups(x, l):
         return [x] + [to_leaf(x, k * groups[l]) for k in range(1, leaves // groups[l])]
@@ -405,14 +409,19 @@
             6 * inv[l].size * width,
             1,
             meta,
-            leaf_rows(rhs[l], l),
+            own_rhs[l],
             *owed,
             inv[l],
         )
 
     solved = [None] * 4
 
-    solved[3] = scatter_sum(*forward_inv(3, []))
+    own_rhs = [None, None, None, leaf_rows(rhs[3], 3)]
+    parts = scatter_parts(*forward_inv(3, []))
+    index_rows = (None,) + after(arguments[11:14], parts[0])
+    parts, (own_rows, all_rows, early) = lax.optimization_barrier((parts, small_arrays()))
+    own_rows, all_rows, own_rhs = [None] + own_rows, [None] + all_rows, [None] + early + own_rhs[3:]
+    solved[3] = sum(parts)
     def forward_panel(l, below):
         parts = gather(solved[l])
         return call(
@@ -434,65 +443,67 @@
     keep, send, updates[3] = forward_panel(3, [])
 
     def owed_parts(parts, l):
-        return parts if groups[l] == 1 else [leaf_sum(sum(parts), groups[l])]
+        if groups[l] == 1:
+            return parts
+        total = sum(parts)
+        return [total, to_leaf(total, 1)] if groups[l] == 2 else [leaf_sum(total, groups[l])]
 
     solved[2] = scatter_sum(*forward_inv(2, owed_parts(scatter_parts(keep, send), 2)))
     keep, send, updates[2] = forward_panel(2, [3])
     parts = scatter_parts(keep, send)
 
-    group, seps = groups[1], leaves // groups[1]
-    height = BLOCK // group
-    blocks = owned[0] // BLOCK
-    parts = scatter_parts(*forward_inv(1, owed_parts(parts, 1)))
+    group, thin = groups[1], BLOCK // leaves
+    top_rows = owned[0] // leaves
     top_keep, top_send = call(
         deferred_kernel,
         "deferred",
-        halves(owned[0]),
+        [shaped(leaves, nz, top_rows, width)] * 2,
         [room(sizes[0], width)],
-        BESIDE,
+        0,
         3,
         meta,
         own_rows[2],
         own_rows[3],
-        after(updates[2], parts[0]),
+        updates[2],
         updates[3],
     )
     leaf_cuts = call(
-        functools.partial(leaf_cuts_kernel, group),
+        leaf_cuts_kernel,
         "leaf_cuts",
-        [shaped(nz, owned[0] // leaves, width)] * leaves,
+        [shaped(nz, top_rows, width)] * leaves,
         [],
-        0,
+        BESIDE,
         1,
         meta,
         top_keep,
         to_core(top_send),
-    )
-    parts, leaf_cuts = lax.optimization_barrier((parts, leaf_cuts))
+        parts[0],
+    )
     deferred = to_leaves(leaf_cuts)
-    solved[1] = sum(parts)
-
-    parts = gather(solved[1])
+    solved[1] = scatter_sum(*forward_inv(1, owed_parts(parts, 1)))
+
     pieces = call(
-        functools.partial(forward_last_kernel, len(parts), group),
+        functools.partial(forward_last_kernel, nz, group, leaves),
         "forward_panel_1",
-        [shaped(listed[1] * height + 8, width)] * group,
+        [shaped(listed[1] * thin + 8, width)] * leaves,
         [room(spans[1], width), room(panel[1].shape[1], width)],
         6 * panel[1].size * width,
         2,
         meta,
         own_rows[1],
-        *parts,
+        *gather(solved[1]),
         panel[1],
     )
-    piece, deferred = sum(to_leaves(pieces)), sum(deferred)
+    pieces = to_leaves(pieces)
+    piece = jnp.concatenate([sum(pieces[d : d + group]) for d in range(0, leaves, group)], axis=0)
+    deferred = sum(deferred)
     own = scatter_chips(
         lambda k: jnp.concatenate([piece, lax.dynamic_index_in_dim(deferred, z ^ k, 0, False)], axis=0)
     )
     owed = call(
-        functools.partial(owed_top_kernel, nz, group, listed[1]),
+        functools.partial(owed_top_kernel, listed[1], thin),
         "owed_top",
-        shaped(blocks * height, width),
+        shaped(top_rows, width),
         [],
         0,
         1,
@@ -501,7 +512,7 @@
         *[to_core(item[: piece.shape[0]]) for item in own],
     )
     keep, send = call(
-        functools.partial(forward_top_kernel, leaves, group),
+        functools.partial(forward_top_kernel, leaves),
         "forward_inv_0",
         halves(chunks[0]),
         [room(owned[0], width), room(spans[0], width)],
@@ -544,7 +555,7 @@
         )
         return to_leaves(picks)
 
-    thin = BLOCK // leaves
+    blocks = owned[0] // BLOCK
     quarters, top_parts = lax.optimization_barrier((quarters, top_parts))
     top = jnp.zeros((blocks, leaves, thin, width), F32)
     for d, item in enumerate(top_parts):

time: 378 us -> 371 us (0.981)
  waiting for transfers between devices: 201 us -> 193 us
  starting transfers between devices: 136 us -> 141 us
    ppermute x28 -> x30, starting transfers between devices: 33.9 us -> 39.3 us  [to_leaf(): lax.ppermute(x, 'leaf', [(i, i ^ k) for i in range(leaves)])]
    ppermute x60, waiting for transfers between devices: 139 us -> 134 us  [to_chip(): return lax.ppermute(x, 'rows', [(r, r ^ 2 * k) for r in range(devices)])]
    ppermute x28 -> x30, waiting for transfers between devices: 36.7 us -> 34.6 us  [to_leaf(): lax.ppermute(x, 'leaf', [(i, i ^ k) for i in range(leaves)])]
  transfers between devices with their start and end apart: 142 -> 144, of which waited for: 83 -> 85; matrix products, arithmetic and copies ran while one was open for 1% -> 1% of each run, Pallas kernels for 1% -> 2%
where the time goes in v4:
time: 371 us; the launch traced here: 370 us
  waiting for transfers between devices  193 us (52%)
  starting transfers between devices  141 us (38%)
  Pallas kernels  25.8 us (7%)
  local copies, waits for them, and re-layouts  6.66 us (2%)
    ppermute x60, waiting for transfers between devices, to_chip(): return lax.ppermute(x, 'rows', [(r, r ^ 2 * k) for r in range(devices)])  134 us
    ppermute x60, starting transfers between devices, to_chip(): return lax.ppermute(x, 'rows', [(r, r ^ 2 * k) for r in range(devices)])  92.6 us
    ppermute x30, starting transfers between devices, to_leaf(): lax.ppermute(x, 'leaf', [(i, i ^ k) for i in range(leaves)])  39.3 us
    ppermute x30, waiting for transfers between devices, to_leaf(): lax.ppermute(x, 'leaf', [(i, i ^ k) for i in range(leaves)])  34.6 us
    pallas_call x19, Pallas kernels, call(): pl.pallas_call(kernel, out_shape=outs, in_specs=[SMEM] * smem_count + [VM...  25.7 us
    ppermute x54, waiting for transfers between devices, to_core(): return lax.ppermute(x, 'rows', [(r, r ^ 1) for r in range(devices)])  24.5 us
    ppermute x54, starting transfers between devices, to_core(): return lax.ppermute(x, 'rows', [(r, r ^ 1) for r in range(devices)])  9.42 us
  transfers between devices with their start and end apart: 144, of which 85 were waited for; matrix products, arithmetic and copies ran while one was open for 1% of the time, Pallas kernels for 2%

profile of v4, /device:TPU:0, one launch (start us, length us, event | category | flops | bytes accessed | tf_op | source)
XLA Modules:
  0.0 370.3 jit_solution(16463521722040211008)
XLA Ops:
  6.4 3.0 collective-permute-start.1
  9.4 2.6 collective-permute-start.2
  15.1 7.2 %collective-permute-done.2 = f32[256,128]{1,0:T(8,128)S(1)} collective-permute-done((f32[256,128]{1,0:T(8,128)S(1)}, f32[256,128]{1,0:T(8,128)S(1)}, u32[]{:S(2)}, u32[]{:S(2)}) %collective-permute-start.2) | collective-permute-done | bytes 131104 | tf_op jit(solution)/shard_map/ppermute | solution.py:337
  26.8 3.7 %collective-permute-done.6.refs_3_ = f32[256,128]{1,0:T(8,128)S(1)} collective-permute-done((f32[256,128]{1,0:T(8,128)S(1)}, f32[256,128]{1,0:T(8,128)S(1)}, u32[]{:S(2)}, u32[]{:S(2)}) %collective-permute-start.6) | collective-permute-done | bytes 131104 | tf_op jit(solution)/shard_map/ppermute | solution.py:337
  31.2 4.9 %collective-permute-done.5.refs_2_ = f32[256,128]{1,0:T(8,128)S(1)} collective-permute-done((f32[256,128]{1,0:T(8,128)S(1)}, f32[256,128]{1,0:T(8,128)S(1)}, u32[]{:S(2)}, u32[]{:S(2)}) %collective-permute-start.5) | collective-permute-done | bytes 131104 | tf_op jit(solution)/shard_map/ppermute | solution.py:337
  43.9 2.9 collective-permute-start.13
  48.3 3.4 collective-permute-done.12.refs_1_
  51.7 5.2 %collective-permute-done.13.refs_2_ = f32[256,128]{1,0:T(8,128)S(1)} collective-permute-done((f32[256,128]{1,0:T(8,128)S(1)}, f32[256,128]{1,0:T(8,128)S(1)}, u32[]{:S(2)}, u32[]{:S(2)}) %collective-permute-start.13) | collective-permute-done | bytes 131104 | tf_op jit(solution)/shard_map/ppermute | solution.py:337
  60.3 2.6 collective-permute-start.16
  65.4 3.2 collective-permute-done.16
  68.6 7.2 %collective-permute-done.17 = f32[256,128]{1,0:T(8,128)S(1)} collective-permute-done((f32[256,128]{1,0:T(8,128)S(1)}, f32[256,128]{1,0:T(8,128)S(1)}, u32[]{:S(2)}, u32[]{:S(2)}) %collective-permute-start.17) | collective-permute-done | bytes 131104 | tf_op jit(solution)/shard_map/ppermute | solution.py:337
  82.6 7.8 %collective-permute-done.20.refs_3_ = f32[256,128]{1,0:T(8,128)S(1)} collective-permute-done((f32[256,128]{1,0:T(8,128)S(1)}, f32[256,128]{1,0:T(8,128)S(1)}, u32[]{:S(2)}, u32[]{:S(2)}) %collective-permute-start.20) | collective-permute-done | bytes 131104 | tf_op jit(solution)/shard_map/ppermute | solution.py:337
  103.9 7.0 %collective-permute-done.28 = f32[256,128]{1,0:T(8,128)S(1)} collective-permute-done((f32[256,128]{1,0:T(8,128)S(1)}, f32[256,128]{1,0:T(8,128)S(1)}, u32[]{:S(2)}, u32[]{:S(2)}) %collective-permute-start.28) | collective-permute-done | bytes 131104 | tf_op jit(solution)/shard_map/ppermute | solution.py:337
  112.5 3.5 collective-permute-done.30.refs_1_
  123.5 5.8 %collective-permute-done.33 = f32[128,128]{1,0:T(8,128)S(1)} collective-permute-done((f32[128,128]{1,0:T(8,128)S(1)}, f32[128,128]{1,0:T(8,128)S(1)}, u32[]{:S(2)}, u32[]{:S(2)}) %collective-permute-start.33) | collective-permute-done | bytes 65568 | tf_op jit(solution)/shard_map/ppermute | solution.py:337
  157.0 3.1 collective-permute-done.49.refs_1_
  160.2 4.3 %collective-permute-done.50.refs_2_ = f32[272,128]{1,0:T(8,128)S(1)} collective-permute-done((f32[272,128]{1,0:T(8,128)S(1)}, f32[272,128]{1,0:T(8,128)S(1)}, u32[]{:S(2)}, u32[]{:S(2)}) %collective-permute-start.50) | collective-permute-done | bytes 139296 | tf_op jit(solution)/shard_map/ppermute | solution.py:337
  182.6 5.7 %collective-permute-done.61 = f32[128,128]{1,0:T(8,128)S(1)} collective-permute-done((f32[128,128]{1,0:T(8,128)S(1)}, f32[128,128]{1,0:T(8,128)S(1)}, u32[]{:S(2)}, u32[]{:S(2)}) %collective-permute-start.61) | collective-permute-done | bytes 65568 | tf_op jit(solution)/shard_map/ppermute | solution.py:337
  193.3 4.1 %collective-permute-done.64.refs_2_ = f32[128,128]{1,0:T(8,128)S(1)} collective-permute-done((f32[128,128]{1,0:T(8,128)S(1)}, f32[128,128]{1,0:T(8,128)S(1)}, u32[]{:S(2)}, u32[]{:S(2)}) %collective-permute-start.64) | collective-permute-done | bytes 65568 | tf_op jit(solution)/shard_map/ppermute | solution.py:337
  233.4 3.7 collective-permute-done.88
  249.5 2.9 collective-permute-done.98.refs_2_
  253.3 4.0 %collective-permute-done.100 = f32[1,256,128]{2,1,0:T(8,128)S(1)} collective-permute-done((f32[1,256,128]{2,1,0:T(8,128)S(1)}, f32[1,256,128]{2,1,0:T(8,128)S(1)}, u32[]{:S(2)}, u32[]{:S(2)}) %collective-permute-start.100) | collective-permute-done | bytes 131104 | tf_op jit(solution)/shard_map/ppermute | solution.py:340
  263.8 3.5 collective-permute-done.102.refs_6_
  277.5 3.1 collective-permute-done.110
  280.6 7.2 %collective-permute-done.111 = f32[256,128]{1,0:T(8,128)S(1)} collective-permute-done((f32[256,128]{1,0:T(8,128)S(1)}, f32[256,128]{1,0:T(8,128)S(1)}, u32[]{:S(2)}, u32[]{:S(2)}) %collective-permute-start.111) | collective-permute-done | bytes 131104 | tf_op jit(solution)/shard_map/ppermute | solution.py:337
  294.2 7.9 %collective-permute-done.114.refs_2_ = f32[256,128]{1,0:T(8,128)S(1)} collective-permute-done((f32[256,128]{1,0:T(8,128)S(1)}, f32[256,128]{1,0:T(8,128)S(1)}, u32[]{:S(2)}, u32[]{:S(2)}) %collective-permute-start.114) | collective-permute-done | bytes 131104 | tf_op jit(solution)/shard_map/ppermute | solution.py:337
  314.9 5.1 %collective-permute-done.121.refs_6_ = f32[256,128]{1,0:T(8,128)S(1)} collective-permute-done((f32[256,128]{1,0:T(8,128)S(1)}, f32[256,128]{1,0:T(8,128)S(1)}, u32[]{:S(2)}, u32[]{:S(2)}) %collective-permute-start.121) | collective-permute-done | bytes 131104 | tf_op jit(solution)/shard_map/ppermute | solution.py:337
  322.1 3.4 backward_panel_3.1
  332.2 3.0 collective-permute-done.131
  335.2 7.4 %collective-permute-done.132 = f32[256,128]{1,0:T(8,128)S(1)} collective-permute-done((f32[256,128]{1,0:T(8,128)S(1)}, f32[256,128]{1,0:T(8,128)S(1)}, u32[]{:S(2)}, u32[]{:S(2)}) %collective-permute-start.132) | collective-permute-done | bytes 131104 | tf_op jit(solution)/shard_map/ppermute | solution.py:337
  349.0 8.0 %collective-permute-done.135.refs_2_ = f32[256,128]{1,0:T(8,128)S(1)} collective-permute-done((f32[256,128]{1,0:T(8,128)S(1)}, f32[256,128]{1,0:T(8,128)S(1)}, u32[]{:S(2)}, u32[]{:S(2)}) %collective-permute-start.135) | collective-permute-done | bytes 131104 | tf_op jit(solution)/shard_map/ppermute | solution.py:337
  365.8 3.6 collective-permute-done.142
  (399 shorter events, 218.4 us)
Async XLA Ops:
  9.4 12.9 %collective-permute-start.2 = (f32[256,128]{1,0:T(8,128)S(1)}, f32[256,128]{1,0:T(8,128)S(1)}, u32[]{:S(2)}, u32[]{:S(2)}) collective-permute-start(f32[256,128]{1,0:T(8,128)S(1)} %get-tuple-element.233), channel_id=1, source_target_pairs={{0,4},{1,5},{2,6},{3,7},{4,0},{5,1},{6,2},{7,3},{8,12},{9,13},{10,... | collective-permute-start | bytes 393224 | tf_op jit(solution)/shard_map/ppermute | solution.py:337
  12.0 10.3 %collective-permute-start.3 = (f32[256,128]{1,0:T(8,128)S(1)}, f32[256,128]{1,0:T(8,128)S(1)}, u32[]{:S(2)}, u32[]{:S(2)}) collective-permute-start(f32[256,128]{1,0:T(8,128)S(1)} %get-tuple-element.232), channel_id=1, source_target_pairs={{0,6},{1,7},{2,4},{3,5},{4,2},{5,3},{6,0},{7,1},{8,14},{9,15},{10,... | collective-permute-start | bytes 393224 | tf_op jit(solution)/shard_map/ppermute | solution.py:337
  26.3 9.9 %collective-permute-start.5 = (f32[256,128]{1,0:T(8,128)S(1)}, f32[256,128]{1,0:T(8,128)S(1)}, u32[]{:S(2)}, u32[]{:S(2)}) collective-permute-start(f32[256,128]{1,0:T(8,128)S(1)} %add_add_fusion.2.refs_0_), channel_id=1, source_target_pairs={{0,4},{1,5},{2,6},{3,7},{4,0},{5,1},{6,2},{7,3},{8,12},{9,13},{10,... | collective-permute-start | bytes 393224 | tf_op jit(solution)/shard_map/ppermute | solution.py:337
  43.9 13.0 %collective-permute-start.13 = (f32[256,128]{1,0:T(8,128)S(1)}, f32[256,128]{1,0:T(8,128)S(1)}, u32[]{:S(2)}, u32[]{:S(2)}) collective-permute-start(f32[256,128]{1,0:T(8,128)S(1)} %get-tuple-element.229), channel_id=1, source_target_pairs={{0,4},{1,5},{2,6},{3,7},{4,0},{5,1},{6,2},{7,3},{8,12},{9,13},{10,... | collective-permute-start | bytes 393224 | tf_op jit(solution)/shard_map/ppermute | solution.py:337
  46.9 10.0 %collective-permute-start.14 = (f32[256,128]{1,0:T(8,128)S(1)}, f32[256,128]{1,0:T(8,128)S(1)}, u32[]{:S(2)}, u32[]{:S(2)}) collective-permute-start(f32[256,128]{1,0:T(8,128)S(1)} %get-tuple-element.228), channel_id=1, source_target_pairs={{0,6},{1,7},{2,4},{3,5},{4,2},{5,3},{6,0},{7,1},{8,14},{9,15},{10,... | collective-permute-start | bytes 393224 | tf_op jit(solution)/shard_map/ppermute | solution.py:337
  63.0 12.9 %collective-permute-start.17 = (f32[256,128]{1,0:T(8,128)S(1)}, f32[256,128]{1,0:T(8,128)S(1)}, u32[]{:S(2)}, u32[]{:S(2)}) collective-permute-start(f32[256,128]{1,0:T(8,128)S(1)} %get-tuple-element.227), channel_id=1, source_target_pairs={{0,4},{1,5},{2,6},{3,7},{4,0},{5,1},{6,2},{7,3},{8,12},{9,13},{10,... | collective-permute-start | bytes 393224 | tf_op jit(solution)/shard_map/ppermute | solution.py:337
  64.0 11.9 %collective-permute-start.18 = (f32[256,128]{1,0:T(8,128)S(1)}, f32[256,128]{1,0:T(8,128)S(1)}, u32[]{:S(2)}, u32[]{:S(2)}) collective-permute-start(f32[256,128]{1,0:T(8,128)S(1)} %get-tuple-element.226), channel_id=1, source_target_pairs={{0,6},{1,7},{2,4},{3,5},{4,2},{5,3},{6,0},{7,1},{8,14},{9,15},{10,... | collective-permute-start | bytes 393224 | tf_op jit(solution)/shard_map/ppermute | solution.py:337
  78.3 12.1 %collective-permute-start.20 = (f32[256,128]{1,0:T(8,128)S(1)}, f32[256,128]{1,0:T(8,128)S(1)}, u32[]{:S(2)}, u32[]{:S(2)}) collective-permute-start(f32[256,128]{1,0:T(8,128)S(1)} %fusion.10.refs_1_), channel_id=1, source_target_pairs={{0,4},{1,5},{2,6},{3,7},{4,0},{5,1},{6,2},{7,3},{8,12},{9,13},{10,... | collective-permute-start | bytes 393224 | tf_op jit(solution)/shard_map/ppermute | solution.py:337
  79.3 11.1 %collective-permute-start.21 = (f32[256,128]{1,0:T(8,128)S(1)}, f32[256,128]{1,0:T(8,128)S(1)}, u32[]{:S(2)}, u32[]{:S(2)}) collective-permute-start(f32[256,128]{1,0:T(8,128)S(1)} %fusion.10.refs_1_), channel_id=1, source_target_pairs={{0,6},{1,7},{2,4},{3,5},{4,2},{5,3},{6,0},{7,1},{8,14},{9,15},{10,... | collective-permute-start | bytes 393224 | tf_op jit(solution)/shard_map/ppermute | solution.py:337
  80.7 10.2 %collective-permute-start.22 = (f32[256,128]{1,0:T(8,128)S(1)}, f32[256,128]{1,0:T(8,128)S(1)}, u32[]{:S(2)}, u32[]{:S(2)}) collective-permute-start(f32[256,128]{1,0:T(8,128)S(1)} %fusion.10.refs_1_), channel_id=1, source_target_pairs={{0,1},{1,0},{2,3},{3,2},{4,5},{5,4},{6,7},{7,6},{8,9},{9,8},{10,11... | collective-permute-start | bytes 393224 | tf_op jit(solution)/shard_map/ppermute | solution.py:334
  98.0 12.9 %collective-permute-start.28 = (f32[256,128]{1,0:T(8,128)S(1)}, f32[256,128]{1,0:T(8,128)S(1)}, u32[]{:S(2)}, u32[]{:S(2)}) collective-permute-start(f32[256,128]{1,0:T(8,128)S(1)} %get-tuple-element.224), channel_id=1, source_target_pairs={{0,4},{1,5},{2,6},{3,7},{4,0},{5,1},{6,2},{7,3},{8,12},{9,13},{10,... | collective-permute-start | bytes 393224 | tf_op jit(solution)/shard_map/ppermute | solution.py:337
  99.1 11.8 %collective-permute-start.29 = (f32[256,128]{1,0:T(8,128)S(1)}, f32[256,128]{1,0:T(8,128)S(1)}, u32[]{:S(2)}, u32[]{:S(2)}) collective-permute-start(f32[256,128]{1,0:T(8,128)S(1)} %get-tuple-element.223), channel_id=1, source_target_pairs={{0,6},{1,7},{2,4},{3,5},{4,2},{5,3},{6,0},{7,1},{8,14},{9,15},{10,... | collective-permute-start | bytes 393224 | tf_op jit(solution)/shard_map/ppermute | solution.py:337
  101.8 32.0 %collective-permute-start.45 = (f32[4,4,128,128]{3,2,1,0:T(8,128)S(1)}, f32[4,4,128,128]{3,2,1,0:T(8,128)S(1)}, u32[]{:S(2)}, u32[]{:S(2)}) collective-permute-start(f32[4,4,128,128]{3,2,1,0:T(8,128)S(1)} %get-tuple-element.138), channel_id=1, source_target_pairs={{0,1},{1,0},{2,3},{3,2},{4,5},{5,4},{6,7},{7,6},{8,9},{9,8},{10,11... | collective-permute-start | bytes 3145736 | tf_op jit(solution)/shard_map/ppermute | solution.py:334
  134.5 17.9 %collective-permute-start.46 = (f32[4,128,128]{2,1,0:T(8,128)S(1)}, f32[4,128,128]{2,1,0:T(8,128)S(1)}, u32[]{:S(2)}, u32[]{:S(2)}) collective-permute-start(f32[4,128,128]{2,1,0:T(8,128)S(1)} %get-tuple-element.140), channel_id=1, source_target_pairs={{0,8},{8,0},{16,24},{24,16},{1,9},{9,1},{17,25},{25,17},{2,10},{10... | collective-permute-start | bytes 786440 | tf_op jit(solution)/shard_map/ppermute | solution.py:340
  136.0 16.3 %collective-permute-start.47 = (f32[4,128,128]{2,1,0:T(8,128)S(1)}, f32[4,128,128]{2,1,0:T(8,128)S(1)}, u32[]{:S(2)}, u32[]{:S(2)}) collective-permute-start(f32[4,128,128]{2,1,0:T(8,128)S(1)} %get-tuple-element.141), channel_id=1, source_target_pairs={{0,16},{8,24},{16,0},{24,8},{1,17},{9,25},{17,1},{25,9},{2,18},{10... | collective-permute-start | bytes 786440 | tf_op jit(solution)/shard_map/ppermute | solution.py:340
  137.5 14.8 %collective-permute-start.48 = (f32[4,128,128]{2,1,0:T(8,128)S(1)}, f32[4,128,128]{2,1,0:T(8,128)S(1)}, u32[]{:S(2)}, u32[]{:S(2)}) collective-permute-start(f32[4,128,128]{2,1,0:T(8,128)S(1)} %get-tuple-element.142), channel_id=1, source_target_pairs={{0,24},{8,16},{16,8},{24,0},{1,25},{9,17},{17,9},{25,1},{2,26},{10... | collective-permute-start | bytes 786440 | tf_op jit(solution)/shard_map/ppermute | solution.py:340
  153.4 11.1 %collective-permute-start.50 = (f32[272,128]{1,0:T(8,128)S(1)}, f32[272,128]{1,0:T(8,128)S(1)}, u32[]{:S(2)}, u32[]{:S(2)}) collective-permute-start(f32[272,128]{1,0:T(8,128)S(1)} %get-tuple-element.251), channel_id=1, source_target_pairs={{0,4},{1,5},{2,6},{3,7},{4,0},{5,1},{6,2},{7,3},{8,12},{9,13},{10,... | collective-permute-start | bytes 417800 | tf_op jit(solution)/shard_map/ppermute | solution.py:337
  257.5 9.8 %collective-permute-start.102 = (f32[256,128]{1,0:T(8,128)S(1)}, f32[256,128]{1,0:T(8,128)S(1)}, u32[]{:S(2)}, u32[]{:S(2)}) collective-permute-start(f32[256,128]{1,0:T(8,128)S(1)} %bitcast.130), channel_id=1, source_target_pairs={{0,4},{1,5},{2,6},{3,7},{4,0},{5,1},{6,2},{7,3},{8,12},{9,13},{10,... | collective-permute-start | bytes 393224 | tf_op jit(solution)/shard_map/ppermute | solution.py:337
  274.9 12.9 %collective-permute-start.111 = (f32[256,128]{1,0:T(8,128)S(1)}, f32[256,128]{1,0:T(8,128)S(1)}, u32[]{:S(2)}, u32[]{:S(2)}) collective-permute-start(f32[256,128]{1,0:T(8,128)S(1)} %get-tuple-element.221), channel_id=1, source_target_pairs={{0,4},{1,5},{2,6},{3,7},{4,0},{5,1},{6,2},{7,3},{8,12},{9,13},{10,... | collective-permute-start | bytes 393224 | tf_op jit(solution)/shard_map/ppermute | solution.py:337
  275.6 12.2 %collective-permute-start.112 = (f32[256,128]{1,0:T(8,128)S(1)}, f32[256,128]{1,0:T(8,128)S(1)}, u32[]{:S(2)}, u32[]{:S(2)}) collective-permute-start(f32[256,128]{1,0:T(8,128)S(1)} %get-tuple-element.220), channel_id=1, source_target_pairs={{0,6},{1,7},{2,4},{3,5},{4,2},{5,3},{6,0},{7,1},{8,14},{9,15},{10,... | collective-permute-start | bytes 393224 | tf_op jit(solution)/shard_map/ppermute | solution.py:337
  290.3 11.9 %collective-permute-start.114 = (f32[256,128]{1,0:T(8,128)S(1)}, f32[256,128]{1,0:T(8,128)S(1)}, u32[]{:S(2)}, u32[]{:S(2)}) collective-permute-start(f32[256,128]{1,0:T(8,128)S(1)} %fusion.8.refs_0_), channel_id=1, source_target_pairs={{0,4},{1,5},{2,6},{3,7},{4,0},{5,1},{6,2},{7,3},{8,12},{9,13},{10,... | collective-permute-start | bytes 393224 | tf_op jit(solution)/shard_map/ppermute | solution.py:337
  290.8 11.4 %collective-permute-start.115 = (f32[256,128]{1,0:T(8,128)S(1)}, f32[256,128]{1,0:T(8,128)S(1)}, u32[]{:S(2)}, u32[]{:S(2)}) collective-permute-start(f32[256,128]{1,0:T(8,128)S(1)} %fusion.8.refs_0_), channel_id=1, source_target_pairs={{0,6},{1,7},{2,4},{3,5},{4,2},{5,3},{6,0},{7,1},{8,14},{9,15},{10,... | collective-permute-start | bytes 393224 | tf_op jit(solution)/shard_map/ppermute | solution.py:337
  292.7 10.0 %collective-permute-start.116 = (f32[256,128]{1,0:T(8,128)S(1)}, f32[256,128]{1,0:T(8,128)S(1)}, u32[]{:S(2)}, u32[]{:S(2)}) collective-permute-start(f32[256,128]{1,0:T(8,128)S(1)} %fusion.8.refs_0_), channel_id=1, source_target_pairs={{0,1},{1,0},{2,3},{3,2},{4,5},{5,4},{6,7},{7,6},{8,9},{9,8},{10,11... | collective-permute-start | bytes 393224 | tf_op jit(solution)/shard_map/ppermute | solution.py:334
  307.1 12.9 %collective-permute-start.121 = (f32[256,128]{1,0:T(8,128)S(1)}, f32[256,128]{1,0:T(8,128)S(1)}, u32[]{:S(2)}, u32[]{:S(2)}) collective-permute-start(f32[256,128]{1,0:T(8,128)S(1)} %bitcast.135), channel_id=1, source_target_pairs={{0,4},{1,5},{2,6},{3,7},{4,0},{5,1},{6,2},{7,3},{8,12},{9,13},{10,... | collective-permute-start | bytes 393224 | tf_op jit(solution)/shard_map/ppermute | solution.py:337
  307.6 12.4 %collective-permute-start.122 = (f32[256,128]{1,0:T(8,128)S(1)}, f32[256,128]{1,0:T(8,128)S(1)}, u32[]{:S(2)}, u32[]{:S(2)}) collective-permute-start(f32[256,128]{1,0:T(8,128)S(1)} %bitcast.136), channel_id=1, source_target_pairs={{0,6},{1,7},{2,4},{3,5},{4,2},{5,3},{6,0},{7,1},{8,14},{9,15},{10,... | collective-permute-start | bytes 393224 | tf_op jit(solution)/shard_map/ppermute | solution.py:337
  309.6 11.0 %collective-permute-start.127 = (f32[1,256,128]{2,1,0:T(8,128)S(1)}, f32[1,256,128]{2,1,0:T(8,128)S(1)}, u32[]{:S(2)}, u32[]{:S(2)}) collective-permute-start(f32[1,256,128]{2,1,0:T(8,128)S(1)} %beside.5), channel_id=1, source_target_pairs={{0,8},{8,0},{16,24},{24,16},{1,9},{9,1},{17,25},{25,17},{2,10},{10... | collective-permute-start | bytes 393224 | tf_op jit(solution)/shard_map/ppermute | solution.py:340
  311.0 9.6 %collective-permute-start.128 = (f32[1,256,128]{2,1,0:T(8,128)S(1)}, f32[1,256,128]{2,1,0:T(8,128)S(1)}, u32[]{:S(2)}, u32[]{:S(2)}) collective-permute-start(f32[1,256,128]{2,1,0:T(8,128)S(1)} %beside.5), channel_id=1, source_target_pairs={{0,16},{8,24},{16,0},{24,8},{1,17},{9,25},{17,1},{25,9},{2,18},{10... | collective-permute-start | bytes 393224 | tf_op jit(solution)/shard_map/ppermute | solution.py:340
  329.7 12.9 %collective-permute-start.132 = (f32[256,128]{1,0:T(8,128)S(1)}, f32[256,128]{1,0:T(8,128)S(1)}, u32[]{:S(2)}, u32[]{:S(2)}) collective-permute-start(f32[256,128]{1,0:T(8,128)S(1)} %get-tuple-element.218), channel_id=1, source_target_pairs={{0,4},{1,5},{2,6},{3,7},{4,0},{5,1},{6,2},{7,3},{8,12},{9,13},{10,... | collective-permute-start | bytes 393224 | tf_op jit(solution)/shard_map/ppermute | solution.py:337
  330.2 12.4 %collective-permute-start.133 = (f32[256,128]{1,0:T(8,128)S(1)}, f32[256,128]{1,0:T(8,128)S(1)}, u32[]{:S(2)}, u32[]{:S(2)}) collective-permute-start(f32[256,128]{1,0:T(8,128)S(1)} %get-tuple-element.217), channel_id=1, source_target_pairs={{0,6},{1,7},{2,4},{3,5},{4,2},{5,3},{6,0},{7,1},{8,14},{9,15},{10,... | collective-permute-start | bytes 393224 | tf_op jit(solution)/shard_map/ppermute | solution.py:337
  345.1 11.9 %collective-permute-start.135 = (f32[256,128]{1,0:T(8,128)S(1)}, f32[256,128]{1,0:T(8,128)S(1)}, u32[]{:S(2)}, u32[]{:S(2)}) collective-permute-start(f32[256,128]{1,0:T(8,128)S(1)} %fusion.5.refs_0_), channel_id=1, source_target_pairs={{0,4},{1,5},{2,6},{3,7},{4,0},{5,1},{6,2},{7,3},{8,12},{9,13},{10,... | collective-permute-start | bytes 393224 | tf_op jit(solution)/shard_map/ppermute | solution.py:337
  345.5 11.5 %collective-permute-start.136 = (f32[256,128]{1,0:T(8,128)S(1)}, f32[256,128]{1,0:T(8,128)S(1)}, u32[]{:S(2)}, u32[]{:S(2)}) collective-permute-start(f32[256,128]{1,0:T(8,128)S(1)} %fusion.5.refs_0_), channel_id=1, source_target_pairs={{0,6},{1,7},{2,4},{3,5},{4,2},{5,3},{6,0},{7,1},{8,14},{9,15},{10,... | collective-permute-start | bytes 393224 | tf_op jit(solution)/shard_map/ppermute | solution.py:337
  347.6 10.0 %collective-permute-start.137 = (f32[256,128]{1,0:T(8,128)S(1)}, f32[256,128]{1,0:T(8,128)S(1)}, u32[]{:S(2)}, u32[]{:S(2)}) collective-permute-start(f32[256,128]{1,0:T(8,128)S(1)} %fusion.5.refs_0_), channel_id=1, source_target_pairs={{0,1},{1,0},{2,3},{3,2},{4,5},{5,4},{6,7},{7,6},{8,9},{9,8},{10,11... | collective-permute-start | bytes 393224 | tf_op jit(solution)/shard_map/ppermute | solution.py:334
  (139 other events, 1101.4 us)

commit v5 on v4

--- a/solution.py
+++ b/solution.py
@@ -40,13 +40,20 @@
     return min(rows, largest)
 
 
+def partners(count, rows):
+    far_first = list(range(count - 1, 0, -1))
+    return list(zip(far_first, far_first[-1:] + far_first[:-1] if rows >= 2 * BLOCK else far_first))
+
+
 def spread_parts(meta, full, parts, offset=0):
     half = len(parts) // 2
-    for k, part in enumerate(parts):
-        core = meta[1] if k < half else 1 - meta[1]
-        rows = part.shape[0]
-        at = offset + (2 * jnp.bitwise_xor(meta[0], k % half) + core) * rows
-        full[pl.ds(pl.multiple_of(at, 8), rows), :] = part[...]
+    rows = parts[0].shape[0]
+    steps = [(0, 0)] + partners(half, rows)
+    for n, part in enumerate(parts):
+        core = meta[1] if n < half else 1 - meta[1]
+        first, second = steps[n % half]
+        chip = jnp.bitwise_xor(meta[0], first + core * (second - first))
+        full[pl.ds(pl.multiple_of(offset + (2 * chip + core) * rows, 8), rows), :] = part[...]
 
 
 def split_cores(meta, full, offset, keep, send):
@@ -333,8 +340,8 @@
     def to_core(x):
         return lax.ppermute(x, "rows", [(r, r ^ 1) for r in range(devices)])
 
-    def to_chip(x, k):
-        return lax.ppermute(x, "rows", [(r, r ^ (2 * k)) for r in range(devices)])
+    def to_chip(x, step):
+        return lax.ppermute(x, "rows", [(r, r ^ (2 * step[r % 2])) for r in range(devices)])
 
     def to_leaf(x, k):
         return x if k == 0 else lax.ppermute(x, "leaf", [(i, i ^ k) for i in range(leaves)])
@@ -343,23 +350,22 @@
         far_first = {d: to_leaf(pieces[d], d) for d in reversed(range(len(pieces)))}
         return [far_first[d] for d in range(len(pieces))]
 
-    def scatter_chips(chunk):
-        far_first = {k: to_chip(chunk(k), k) for k in range(nz - 1, 0, -1)}
-        return [chunk(0)] + [far_first[k] for k in range(1, nz)]
+    def scatter_chips(chunk, steps):
+        return [chunk(z)] + [to_chip(chunk(z ^ jnp.where(core == 0, step[0], step[1])), step) for step in steps]
 
     def scatter_parts(keep, send):
         received = to_core(send)
         return scatter_chips(
-            lambda k: lax.dynamic_index_in_dim(keep, z ^ k, 0, False)
-            + lax.dynamic_index_in_dim(received, z ^ k, 0, False)
+            lambda chip: lax.dynamic_index_in_dim(keep, chip, 0, False)
+            + lax.dynamic_index_in_dim(received, chip, 0, False),
+            partners(nz, keep.shape[1]),
         )
 
     def scatter_sum(keep, send):
         return sum(scatter_parts(keep, send))
 
     def gather(x):
-        far_first = {k: to_chip(x, k) for k in range(nz - 1, 0, -1)}
-        own = [x] + [far_first[k] for k in range(1, nz)]
+        own = [x] + [to_chip(x, step) for step in partners(nz, x.shape[0])]
         return own + [to_core(item) for item in own]
 
     def leaf_sum(x, group):
@@ -498,7 +504,8 @@
     piece = jnp.concatenate([sum(pieces[d : d + group]) for d in range(0, leaves, group)], axis=0)
     deferred = sum(deferred)
     own = scatter_chips(
-        lambda k: jnp.concatenate([piece, lax.dynamic_index_in_dim(deferred, z ^ k, 0, False)], axis=0)
+        lambda chip: jnp.concatenate([piece, lax.dynamic_index_in_dim(deferred, chip, 0, False)], axis=0),
+        partners(nz, piece.shape[0] + top_rows),
     )
     owed = call(
         functools.partial(owed_top_kernel, listed[1], thin),

time: 371 us -> 368 us (level)
    ppermute x60, waiting for transfers between devices: 134 us -> 128 us  [to_chip(): lax.ppermute(x, 'rows', [(r, r ^ 2 * step[r % 2]) for r in range(devices)])]
  transfers between devices with their start and end apart: 144 -> 144, of which waited for: 85 -> 86; matrix products, arithmetic and copies ran while one was open for 1% -> 1% of each run, Pallas kernels for 2% -> 2%
where the time goes in v5:
time: 368 us; the launch traced here: 367 us
  waiting for transfers between devices  190 us (52%)
  starting transfers between devices  138 us (38%)
  Pallas kernels  27.4 us (7%)
  local copies, waits for them, and re-layouts  6.66 us (2%)
    ppermute x60, waiting for transfers between devices, to_chip(): lax.ppermute(x, 'rows', [(r, r ^ 2 * step[r % 2]) for r in range(devices)])  128 us
    ppermute x60, starting transfers between devices, to_chip(): lax.ppermute(x, 'rows', [(r, r ^ 2 * step[r % 2]) for r in range(devices)])  89.4 us
    ppermute x30, starting transfers between devices, to_leaf(): lax.ppermute(x, 'leaf', [(i, i ^ k) for i in range(leaves)])  39 us
    ppermute x30, waiting for transfers between devices, to_leaf(): lax.ppermute(x, 'leaf', [(i, i ^ k) for i in range(leaves)])  37.4 us
    pallas_call x19, Pallas kernels, call(): pl.pallas_call(kernel, out_shape=outs, in_specs=[SMEM] * smem_count + [VM...  27.4 us
    ppermute x54, waiting for transfers between devices, to_core(): return lax.ppermute(x, 'rows', [(r, r ^ 1) for r in range(devices)])  24.3 us
    ppermute x54, starting transfers between devices, to_core(): return lax.ppermute(x, 'rows', [(r, r ^ 1) for r in range(devices)])  9.68 us
  transfers between devices with their start and end apart: 144, of which 86 were waited for; matrix products, arithmetic and copies ran while one was open for 1% of the time, Pallas kernels for 2%

profile of v5, /device:TPU:0, one launch (start us, length us, event | category | flops | bytes accessed | tf_op | source)
XLA Modules:
  0.0 367.4 jit_solution(11078582525803165320)
XLA Ops:
  6.4 5.0 %collective-permute-start.1 = (f32[256,128]{1,0:T(8,128)S(1)}, f32[256,128]{1,0:T(8,128)S(1)}, u32[]{:S(2)}, u32[]{:S(2)}) collective-permute-start(f32[256,128]{1,0:T(8,128)S(1)} %get-tuple-element.234), channel_id=1, source_target_pairs={{0,6},{1,3},{2,4},{3,1},{4,2},{5,7},{6,0},{7,5},{8,14},{9,11},{10,... | collective-permute-start | bytes 393224 | tf_op jit(solution)/shard_map/ppermute | solution.py:344
  12.8 3.0 collective-permute-done.1
  15.8 7.5 %collective-permute-done.2 = f32[256,128]{1,0:T(8,128)S(1)} collective-permute-done((f32[256,128]{1,0:T(8,128)S(1)}, f32[256,128]{1,0:T(8,128)S(1)}, u32[]{:S(2)}, u32[]{:S(2)}) %collective-permute-start.2) | collective-permute-done | bytes 131104 | tf_op jit(solution)/shard_map/ppermute | solution.py:344
  27.1 4.9 %collective-permute-done.6.refs_3_ = f32[256,128]{1,0:T(8,128)S(1)} collective-permute-done((f32[256,128]{1,0:T(8,128)S(1)}, f32[256,128]{1,0:T(8,128)S(1)}, u32[]{:S(2)}, u32[]{:S(2)}) %collective-permute-start.6) | collective-permute-done | bytes 131104 | tf_op jit(solution)/shard_map/ppermute | solution.py:344
  33.0 5.1 %collective-permute-done.5.refs_2_ = f32[256,128]{1,0:T(8,128)S(1)} collective-permute-done((f32[256,128]{1,0:T(8,128)S(1)}, f32[256,128]{1,0:T(8,128)S(1)}, u32[]{:S(2)}, u32[]{:S(2)}) %collective-permute-start.5) | collective-permute-done | bytes 131104 | tf_op jit(solution)/shard_map/ppermute | solution.py:344
  50.2 3.8 %collective-permute-done.12.refs_1_ = f32[256,128]{1,0:T(8,128)S(1)} collective-permute-done((f32[256,128]{1,0:T(8,128)S(1)}, f32[256,128]{1,0:T(8,128)S(1)}, u32[]{:S(2)}, u32[]{:S(2)}) %collective-permute-start.12) | collective-permute-done | bytes 131104 | tf_op jit(solution)/shard_map/ppermute | solution.py:344
  54.1 5.0 %collective-permute-done.13.refs_2_ = f32[256,128]{1,0:T(8,128)S(1)} collective-permute-done((f32[256,128]{1,0:T(8,128)S(1)}, f32[256,128]{1,0:T(8,128)S(1)}, u32[]{:S(2)}, u32[]{:S(2)}) %collective-permute-start.13) | collective-permute-done | bytes 131104 | tf_op jit(solution)/shard_map/ppermute | solution.py:344
  66.9 3.8 %collective-permute-done.16 = f32[256,128]{1,0:T(8,128)S(1)} collective-permute-done((f32[256,128]{1,0:T(8,128)S(1)}, f32[256,128]{1,0:T(8,128)S(1)}, u32[]{:S(2)}, u32[]{:S(2)}) %collective-permute-start.16) | collective-permute-done | bytes 131104 | tf_op jit(solution)/shard_map/ppermute | solution.py:344
  70.8 5.2 %collective-permute-done.17 = f32[256,128]{1,0:T(8,128)S(1)} collective-permute-done((f32[256,128]{1,0:T(8,128)S(1)}, f32[256,128]{1,0:T(8,128)S(1)}, u32[]{:S(2)}, u32[]{:S(2)}) %collective-permute-start.17) | collective-permute-done | bytes 131104 | tf_op jit(solution)/shard_map/ppermute | solution.py:344
  80.5 3.8 %collective-permute-done.19.refs_2_ = f32[256,128]{1,0:T(8,128)S(1)} collective-permute-done((f32[256,128]{1,0:T(8,128)S(1)}, f32[256,128]{1,0:T(8,128)S(1)}, u32[]{:S(2)}, u32[]{:S(2)}) %collective-permute-start.19) | collective-permute-done | bytes 131104 | tf_op jit(solution)/shard_map/ppermute | solution.py:344
  84.3 5.2 %collective-permute-done.20.refs_3_ = f32[256,128]{1,0:T(8,128)S(1)} collective-permute-done((f32[256,128]{1,0:T(8,128)S(1)}, f32[256,128]{1,0:T(8,128)S(1)}, u32[]{:S(2)}, u32[]{:S(2)}) %collective-permute-start.20) | collective-permute-done | bytes 131104 | tf_op jit(solution)/shard_map/ppermute | solution.py:344
  103.5 5.2 %collective-permute-done.28 = f32[256,128]{1,0:T(8,128)S(1)} collective-permute-done((f32[256,128]{1,0:T(8,128)S(1)}, f32[256,128]{1,0:T(8,128)S(1)}, u32[]{:S(2)}, u32[]{:S(2)}) %collective-permute-start.28) | collective-permute-done | bytes 131104 | tf_op jit(solution)/shard_map/ppermute | solution.py:344
  110.3 4.2 %collective-permute-done.30.refs_1_ = f32[256,128]{1,0:T(8,128)S(1)} collective-permute-done((f32[256,128]{1,0:T(8,128)S(1)}, f32[256,128]{1,0:T(8,128)S(1)}, u32[]{:S(2)}, u32[]{:S(2)}) %collective-permute-start.30) | collective-permute-done | bytes 131104 | tf_op jit(solution)/shard_map/ppermute | solution.py:347
  144.2 3.5 collective-permute-done.42
  157.3 2.7 collective-permute-done.49.refs_1_
  160.0 5.7 %collective-permute-done.50.refs_2_ = f32[272,128]{1,0:T(8,128)S(1)} collective-permute-done((f32[272,128]{1,0:T(8,128)S(1)}, f32[272,128]{1,0:T(8,128)S(1)}, u32[]{:S(2)}, u32[]{:S(2)}) %collective-permute-start.50) | collective-permute-done | bytes 139296 | tf_op jit(solution)/shard_map/ppermute | solution.py:344
  181.2 2.7 collective-permute-start.62
  190.0 2.7 collective-permute-start.65
  250.4 2.8 collective-permute-done.98.refs_2_
  254.5 3.7 %collective-permute-done.100 = f32[1,256,128]{2,1,0:T(8,128)S(1)} collective-permute-done((f32[1,256,128]{2,1,0:T(8,128)S(1)}, f32[1,256,128]{2,1,0:T(8,128)S(1)}, u32[]{:S(2)}, u32[]{:S(2)}) %collective-permute-start.100) | collective-permute-done | bytes 131104 | tf_op jit(solution)/shard_map/ppermute | solution.py:347
  265.3 4.9 %collective-permute-done.102.refs_6_ = f32[256,128]{1,0:T(8,128)S(1)} collective-permute-done((f32[256,128]{1,0:T(8,128)S(1)}, f32[256,128]{1,0:T(8,128)S(1)}, u32[]{:S(2)}, u32[]{:S(2)}) %collective-permute-start.102) | collective-permute-done | bytes 131104 | tf_op jit(solution)/shard_map/ppermute | solution.py:344
  280.5 3.8 %collective-permute-done.110 = f32[256,128]{1,0:T(8,128)S(1)} collective-permute-done((f32[256,128]{1,0:T(8,128)S(1)}, f32[256,128]{1,0:T(8,128)S(1)}, u32[]{:S(2)}, u32[]{:S(2)}) %collective-permute-start.110) | collective-permute-done | bytes 131104 | tf_op jit(solution)/shard_map/ppermute | solution.py:344
  284.3 5.2 %collective-permute-done.111 = f32[256,128]{1,0:T(8,128)S(1)} collective-permute-done((f32[256,128]{1,0:T(8,128)S(1)}, f32[256,128]{1,0:T(8,128)S(1)}, u32[]{:S(2)}, u32[]{:S(2)}) %collective-permute-start.111) | collective-permute-done | bytes 131104 | tf_op jit(solution)/shard_map/ppermute | solution.py:344
  294.0 3.8 %collective-permute-done.113.refs_1_ = f32[256,128]{1,0:T(8,128)S(1)} collective-permute-done((f32[256,128]{1,0:T(8,128)S(1)}, f32[256,128]{1,0:T(8,128)S(1)}, u32[]{:S(2)}, u32[]{:S(2)}) %collective-permute-start.113) | collective-permute-done | bytes 131104 | tf_op jit(solution)/shard_map/ppermute | solution.py:344
  297.8 5.2 %collective-permute-done.114.refs_2_ = f32[256,128]{1,0:T(8,128)S(1)} collective-permute-done((f32[256,128]{1,0:T(8,128)S(1)}, f32[256,128]{1,0:T(8,128)S(1)}, u32[]{:S(2)}, u32[]{:S(2)}) %collective-permute-start.114) | collective-permute-done | bytes 131104 | tf_op jit(solution)/shard_map/ppermute | solution.py:344
  315.6 3.8 %collective-permute-done.121.refs_6_ = f32[256,128]{1,0:T(8,128)S(1)} collective-permute-done((f32[256,128]{1,0:T(8,128)S(1)}, f32[256,128]{1,0:T(8,128)S(1)}, u32[]{:S(2)}, u32[]{:S(2)}) %collective-permute-start.121) | collective-permute-done | bytes 131104 | tf_op jit(solution)/shard_map/ppermute | solution.py:344
  321.6 3.5 backward_panel_3.1
  331.5 3.7 %collective-permute-done.131 = f32[256,128]{1,0:T(8,128)S(1)} collective-permute-done((f32[256,128]{1,0:T(8,128)S(1)}, f32[256,128]{1,0:T(8,128)S(1)}, u32[]{:S(2)}, u32[]{:S(2)}) %collective-permute-start.131) | collective-permute-done | bytes 131104 | tf_op jit(solution)/shard_map/ppermute | solution.py:344
  335.3 5.2 %collective-permute-done.132 = f32[256,128]{1,0:T(8,128)S(1)} collective-permute-done((f32[256,128]{1,0:T(8,128)S(1)}, f32[256,128]{1,0:T(8,128)S(1)}, u32[]{:S(2)}, u32[]{:S(2)}) %collective-permute-start.132) | collective-permute-done | bytes 131104 | tf_op jit(solution)/shard_map/ppermute | solution.py:344
  345.2 3.6 collective-permute-done.134.refs_1_
  348.8 5.2 %collective-permute-done.135.refs_2_ = f32[256,128]{1,0:T(8,128)S(1)} collective-permute-done((f32[256,128]{1,0:T(8,128)S(1)}, f32[256,128]{1,0:T(8,128)S(1)}, u32[]{:S(2)}, u32[]{:S(2)}) %collective-permute-start.135) | collective-permute-done | bytes 131104 | tf_op jit(solution)/shard_map/ppermute | solution.py:344
  362.7 3.8 %collective-permute-done.142 = f32[2,128,128]{2,1,0:T(8,128)S(1)} collective-permute-done((f32[2,128,128]{2,1,0:T(8,128)S(1)}, f32[2,128,128]{2,1,0:T(8,128)S(1)}, u32[]{:S(2)}, u32[]{:S(2)}) %collective-permute-start.142) | collective-permute-done | bytes 131104 | tf_op jit(solution)/shard_map/ppermute | solution.py:347
  (401 shorter events, 228.4 us)
Async XLA Ops:
  11.4 11.9 %collective-permute-start.2 = (f32[256,128]{1,0:T(8,128)S(1)}, f32[256,128]{1,0:T(8,128)S(1)}, u32[]{:S(2)}, u32[]{:S(2)}) collective-permute-start(f32[256,128]{1,0:T(8,128)S(1)} %get-tuple-element.233), channel_id=1, source_target_pairs={{0,4},{1,7},{2,6},{3,5},{4,0},{5,3},{6,2},{7,1},{8,12},{9,15},{10,... | collective-permute-start | bytes 393224 | tf_op jit(solution)/shard_map/ppermute | solution.py:344
  11.4 11.9 %collective-permute-start.3 = (f32[256,128]{1,0:T(8,128)S(1)}, f32[256,128]{1,0:T(8,128)S(1)}, u32[]{:S(2)}, u32[]{:S(2)}) collective-permute-start(f32[256,128]{1,0:T(8,128)S(1)} %get-tuple-element.232), channel_id=1, source_target_pairs={{0,2},{1,5},{2,0},{3,7},{4,6},{5,1},{6,4},{7,3},{8,10},{9,13},{10,... | collective-permute-start | bytes 393224 | tf_op jit(solution)/shard_map/ppermute | solution.py:344
  25.9 12.2 %collective-permute-start.5 = (f32[256,128]{1,0:T(8,128)S(1)}, f32[256,128]{1,0:T(8,128)S(1)}, u32[]{:S(2)}, u32[]{:S(2)}) collective-permute-start(f32[256,128]{1,0:T(8,128)S(1)} %add_add_fusion.2.refs_0_), channel_id=1, source_target_pairs={{0,4},{1,7},{2,6},{3,5},{4,0},{5,3},{6,2},{7,1},{8,12},{9,15},{10,... | collective-permute-start | bytes 393224 | tf_op jit(solution)/shard_map/ppermute | solution.py:344
  26.9 11.2 %collective-permute-start.7 = (f32[256,128]{1,0:T(8,128)S(1)}, f32[256,128]{1,0:T(8,128)S(1)}, u32[]{:S(2)}, u32[]{:S(2)}) collective-permute-start(f32[256,128]{1,0:T(8,128)S(1)} %add_add_fusion.2.refs_0_), channel_id=1, source_target_pairs={{0,1},{1,0},{2,3},{3,2},{4,5},{5,4},{6,7},{7,6},{8,9},{9,8},{10,11... | collective-permute-start | bytes 393224 | tf_op jit(solution)/shard_map/ppermute | solution.py:341
  47.6 11.5 %collective-permute-start.13 = (f32[256,128]{1,0:T(8,128)S(1)}, f32[256,128]{1,0:T(8,128)S(1)}, u32[]{:S(2)}, u32[]{:S(2)}) collective-permute-start(f32[256,128]{1,0:T(8,128)S(1)} %get-tuple-element.229), channel_id=1, source_target_pairs={{0,4},{1,7},{2,6},{3,5},{4,0},{5,3},{6,2},{7,1},{8,12},{9,15},{10,... | collective-permute-start | bytes 393224 | tf_op jit(solution)/shard_map/ppermute | solution.py:344
  47.6 11.5 %collective-permute-start.14 = (f32[256,128]{1,0:T(8,128)S(1)}, f32[256,128]{1,0:T(8,128)S(1)}, u32[]{:S(2)}, u32[]{:S(2)}) collective-permute-start(f32[256,128]{1,0:T(8,128)S(1)} %get-tuple-element.228), channel_id=1, source_target_pairs={{0,2},{1,5},{2,0},{3,7},{4,6},{5,1},{6,4},{7,3},{8,10},{9,13},{10,... | collective-permute-start | bytes 393224 | tf_op jit(solution)/shard_map/ppermute | solution.py:344
  64.3 11.7 %collective-permute-start.17 = (f32[256,128]{1,0:T(8,128)S(1)}, f32[256,128]{1,0:T(8,128)S(1)}, u32[]{:S(2)}, u32[]{:S(2)}) collective-permute-start(f32[256,128]{1,0:T(8,128)S(1)} %get-tuple-element.227), channel_id=1, source_target_pairs={{0,4},{1,7},{2,6},{3,5},{4,0},{5,3},{6,2},{7,1},{8,12},{9,15},{10,... | collective-permute-start | bytes 393224 | tf_op jit(solution)/shard_map/ppermute | solution.py:344
  64.3 11.7 %collective-permute-start.18 = (f32[256,128]{1,0:T(8,128)S(1)}, f32[256,128]{1,0:T(8,128)S(1)}, u32[]{:S(2)}, u32[]{:S(2)}) collective-permute-start(f32[256,128]{1,0:T(8,128)S(1)} %get-tuple-element.226), channel_id=1, source_target_pairs={{0,2},{1,5},{2,0},{3,7},{4,6},{5,1},{6,4},{7,3},{8,10},{9,13},{10,... | collective-permute-start | bytes 393224 | tf_op jit(solution)/shard_map/ppermute | solution.py:344
  77.8 11.7 %collective-permute-start.20 = (f32[256,128]{1,0:T(8,128)S(1)}, f32[256,128]{1,0:T(8,128)S(1)}, u32[]{:S(2)}, u32[]{:S(2)}) collective-permute-start(f32[256,128]{1,0:T(8,128)S(1)} %fusion.10.refs_1_), channel_id=1, source_target_pairs={{0,4},{1,7},{2,6},{3,5},{4,0},{5,3},{6,2},{7,1},{8,12},{9,15},{10,... | collective-permute-start | bytes 393224 | tf_op jit(solution)/shard_map/ppermute | solution.py:344
  77.8 11.7 %collective-permute-start.21 = (f32[256,128]{1,0:T(8,128)S(1)}, f32[256,128]{1,0:T(8,128)S(1)}, u32[]{:S(2)}, u32[]{:S(2)}) collective-permute-start(f32[256,128]{1,0:T(8,128)S(1)} %fusion.10.refs_1_), channel_id=1, source_target_pairs={{0,2},{1,5},{2,0},{3,7},{4,6},{5,1},{6,4},{7,3},{8,10},{9,13},{10,... | collective-permute-start | bytes 393224 | tf_op jit(solution)/shard_map/ppermute | solution.py:344
  97.1 11.7 %collective-permute-start.28 = (f32[256,128]{1,0:T(8,128)S(1)}, f32[256,128]{1,0:T(8,128)S(1)}, u32[]{:S(2)}, u32[]{:S(2)}) collective-permute-start(f32[256,128]{1,0:T(8,128)S(1)} %get-tuple-element.224), channel_id=1, source_target_pairs={{0,4},{1,7},{2,6},{3,5},{4,0},{5,3},{6,2},{7,1},{8,12},{9,15},{10,... | collective-permute-start | bytes 393224 | tf_op jit(solution)/shard_map/ppermute | solution.py:344
  97.1 11.7 %collective-permute-start.29 = (f32[256,128]{1,0:T(8,128)S(1)}, f32[256,128]{1,0:T(8,128)S(1)}, u32[]{:S(2)}, u32[]{:S(2)}) collective-permute-start(f32[256,128]{1,0:T(8,128)S(1)} %get-tuple-element.223), channel_id=1, source_target_pairs={{0,2},{1,5},{2,0},{3,7},{4,6},{5,1},{6,4},{7,3},{8,10},{9,13},{10,... | collective-permute-start | bytes 393224 | tf_op jit(solution)/shard_map/ppermute | solution.py:344
  101.8 30.6 %collective-permute-start.45 = (f32[4,4,128,128]{3,2,1,0:T(8,128)}, f32[4,4,128,128]{3,2,1,0:T(8,128)}, u32[]{:S(2)}, u32[]{:S(2)}) collective-permute-start(f32[4,4,128,128]{3,2,1,0:T(8,128)} %get-tuple-element.138), channel_id=1, source_target_pairs={{0,1},{1,0},{2,3},{3,2},{4,5},{5,4},{6,7},{7,6},{8,9},{9,8},{10,11... | collective-permute-start | bytes 3145736 | tf_op jit(solution)/shard_map/ppermute | solution.py:341
  133.9 18.8 %collective-permute-start.46 = (f32[4,128,128]{2,1,0:T(8,128)S(1)}, f32[4,128,128]{2,1,0:T(8,128)S(1)}, u32[]{:S(2)}, u32[]{:S(2)}) collective-permute-start(f32[4,128,128]{2,1,0:T(8,128)S(1)} %get-tuple-element.140), channel_id=1, source_target_pairs={{0,8},{8,0},{16,24},{24,16},{1,9},{9,1},{17,25},{25,17},{2,10},{10... | collective-permute-start | bytes 786440 | tf_op jit(solution)/shard_map/ppermute | solution.py:347
  135.4 17.2 %collective-permute-start.47 = (f32[4,128,128]{2,1,0:T(8,128)S(1)}, f32[4,128,128]{2,1,0:T(8,128)S(1)}, u32[]{:S(2)}, u32[]{:S(2)}) collective-permute-start(f32[4,128,128]{2,1,0:T(8,128)S(1)} %get-tuple-element.141), channel_id=1, source_target_pairs={{0,16},{8,24},{16,0},{24,8},{1,17},{9,25},{17,1},{25,9},{2,18},{10... | collective-permute-start | bytes 786440 | tf_op jit(solution)/shard_map/ppermute | solution.py:347
  137.0 15.7 %collective-permute-start.48 = (f32[4,128,128]{2,1,0:T(8,128)S(1)}, f32[4,128,128]{2,1,0:T(8,128)S(1)}, u32[]{:S(2)}, u32[]{:S(2)}) collective-permute-start(f32[4,128,128]{2,1,0:T(8,128)S(1)} %get-tuple-element.142), channel_id=1, source_target_pairs={{0,24},{8,16},{16,8},{24,0},{1,25},{9,17},{17,9},{25,1},{2,26},{10... | collective-permute-start | bytes 786440 | tf_op jit(solution)/shard_map/ppermute | solution.py:347
  154.7 11.1 %collective-permute-start.50 = (f32[272,128]{1,0:T(8,128)S(1)}, f32[272,128]{1,0:T(8,128)S(1)}, u32[]{:S(2)}, u32[]{:S(2)}) collective-permute-start(f32[272,128]{1,0:T(8,128)S(1)} %get-tuple-element.251), channel_id=1, source_target_pairs={{0,4},{1,7},{2,6},{3,5},{4,0},{5,3},{6,2},{7,1},{8,12},{9,15},{10,... | collective-permute-start | bytes 417800 | tf_op jit(solution)/shard_map/ppermute | solution.py:344
  154.7 11.1 %collective-permute-start.51 = (f32[272,128]{1,0:T(8,128)S(1)}, f32[272,128]{1,0:T(8,128)S(1)}, u32[]{:S(2)}, u32[]{:S(2)}) collective-permute-start(f32[272,128]{1,0:T(8,128)S(1)} %get-tuple-element.249), channel_id=1, source_target_pairs={{0,2},{1,5},{2,0},{3,7},{4,6},{5,1},{6,4},{7,3},{8,10},{9,13},{10,... | collective-permute-start | bytes 417800 | tf_op jit(solution)/shard_map/ppermute | solution.py:344
  243.3 9.9 %collective-permute-start.98 = (f32[384,128]{1,0:T(8,128)S(1)}, f32[384,128]{1,0:T(8,128)S(1)}, u32[]{:S(2)}, u32[]{:S(2)}) collective-permute-start(f32[384,128]{1,0:T(8,128)S(1)} %get-tuple-element.180), channel_id=1, source_target_pairs={{0,16},{8,24},{16,0},{24,8},{1,17},{9,25},{17,1},{25,9},{2,18},{10... | collective-permute-start | bytes 589832 | tf_op jit(solution)/shard_map/ppermute | solution.py:347
  260.2 10.0 %collective-permute-start.102 = (f32[256,128]{1,0:T(8,128)S(1)}, f32[256,128]{1,0:T(8,128)S(1)}, u32[]{:S(2)}, u32[]{:S(2)}) collective-permute-start(f32[256,128]{1,0:T(8,128)S(1)} %bitcast.130), channel_id=1, source_target_pairs={{0,4},{1,7},{2,6},{3,5},{4,0},{5,3},{6,2},{7,1},{8,12},{9,15},{10,... | collective-permute-start | bytes 393224 | tf_op jit(solution)/shard_map/ppermute | solution.py:344
  260.3 10.0 %collective-permute-start.103 = (f32[256,128]{1,0:T(8,128)S(1)}, f32[256,128]{1,0:T(8,128)S(1)}, u32[]{:S(2)}, u32[]{:S(2)}) collective-permute-start(f32[256,128]{1,0:T(8,128)S(1)} %bitcast.131), channel_id=1, source_target_pairs={{0,2},{1,5},{2,0},{3,7},{4,6},{5,1},{6,4},{7,3},{8,10},{9,13},{10,... | collective-permute-start | bytes 393224 | tf_op jit(solution)/shard_map/ppermute | solution.py:344
  278.0 11.4 %collective-permute-start.111 = (f32[256,128]{1,0:T(8,128)S(1)}, f32[256,128]{1,0:T(8,128)S(1)}, u32[]{:S(2)}, u32[]{:S(2)}) collective-permute-start(f32[256,128]{1,0:T(8,128)S(1)} %get-tuple-element.221), channel_id=1, source_target_pairs={{0,4},{1,7},{2,6},{3,5},{4,0},{5,3},{6,2},{7,1},{8,12},{9,15},{10,... | collective-permute-start | bytes 393224 | tf_op jit(solution)/shard_map/ppermute | solution.py:344
  278.1 11.4 %collective-permute-start.112 = (f32[256,128]{1,0:T(8,128)S(1)}, f32[256,128]{1,0:T(8,128)S(1)}, u32[]{:S(2)}, u32[]{:S(2)}) collective-permute-start(f32[256,128]{1,0:T(8,128)S(1)} %get-tuple-element.220), channel_id=1, source_target_pairs={{0,2},{1,5},{2,0},{3,7},{4,6},{5,1},{6,4},{7,3},{8,10},{9,13},{10,... | collective-permute-start | bytes 393224 | tf_op jit(solution)/shard_map/ppermute | solution.py:344
  291.6 11.4 %collective-permute-start.114 = (f32[256,128]{1,0:T(8,128)S(1)}, f32[256,128]{1,0:T(8,128)S(1)}, u32[]{:S(2)}, u32[]{:S(2)}) collective-permute-start(f32[256,128]{1,0:T(8,128)S(1)} %fusion.8.refs_0_), channel_id=1, source_target_pairs={{0,4},{1,7},{2,6},{3,5},{4,0},{5,3},{6,2},{7,1},{8,12},{9,15},{10,... | collective-permute-start | bytes 393224 | tf_op jit(solution)/shard_map/ppermute | solution.py:344
  291.6 11.4 %collective-permute-start.115 = (f32[256,128]{1,0:T(8,128)S(1)}, f32[256,128]{1,0:T(8,128)S(1)}, u32[]{:S(2)}, u32[]{:S(2)}) collective-permute-start(f32[256,128]{1,0:T(8,128)S(1)} %fusion.8.refs_0_), channel_id=1, source_target_pairs={{0,2},{1,5},{2,0},{3,7},{4,6},{5,1},{6,4},{7,3},{8,10},{9,13},{10,... | collective-permute-start | bytes 393224 | tf_op jit(solution)/shard_map/ppermute | solution.py:344
  308.0 11.4 %collective-permute-start.121 = (f32[256,128]{1,0:T(8,128)S(1)}, f32[256,128]{1,0:T(8,128)S(1)}, u32[]{:S(2)}, u32[]{:S(2)}) collective-permute-start(f32[256,128]{1,0:T(8,128)S(1)} %bitcast.135), channel_id=1, source_target_pairs={{0,4},{1,7},{2,6},{3,5},{4,0},{5,3},{6,2},{7,1},{8,12},{9,15},{10,... | collective-permute-start | bytes 393224 | tf_op jit(solution)/shard_map/ppermute | solution.py:344
  308.0 11.4 %collective-permute-start.122 = (f32[256,128]{1,0:T(8,128)S(1)}, f32[256,128]{1,0:T(8,128)S(1)}, u32[]{:S(2)}, u32[]{:S(2)}) collective-permute-start(f32[256,128]{1,0:T(8,128)S(1)} %bitcast.136), channel_id=1, source_target_pairs={{0,2},{1,5},{2,0},{3,7},{4,6},{5,1},{6,4},{7,3},{8,10},{9,13},{10,... | collective-permute-start | bytes 393224 | tf_op jit(solution)/shard_map/ppermute | solution.py:344
  310.4 9.7 %collective-permute-start.127 = (f32[1,256,128]{2,1,0:T(8,128)S(1)}, f32[1,256,128]{2,1,0:T(8,128)S(1)}, u32[]{:S(2)}, u32[]{:S(2)}) collective-permute-start(f32[1,256,128]{2,1,0:T(8,128)S(1)} %beside.5), channel_id=1, source_target_pairs={{0,8},{8,0},{16,24},{24,16},{1,9},{9,1},{17,25},{25,17},{2,10},{10... | collective-permute-start | bytes 393224 | tf_op jit(solution)/shard_map/ppermute | solution.py:347
  329.0 11.4 %collective-permute-start.132 = (f32[256,128]{1,0:T(8,128)S(1)}, f32[256,128]{1,0:T(8,128)S(1)}, u32[]{:S(2)}, u32[]{:S(2)}) collective-permute-start(f32[256,128]{1,0:T(8,128)S(1)} %get-tuple-element.218), channel_id=1, source_target_pairs={{0,4},{1,7},{2,6},{3,5},{4,0},{5,3},{6,2},{7,1},{8,12},{9,15},{10,... | collective-permute-start | bytes 393224 | tf_op jit(solution)/shard_map/ppermute | solution.py:344
  329.0 11.4 %collective-permute-start.133 = (f32[256,128]{1,0:T(8,128)S(1)}, f32[256,128]{1,0:T(8,128)S(1)}, u32[]{:S(2)}, u32[]{:S(2)}) collective-permute-start(f32[256,128]{1,0:T(8,128)S(1)} %get-tuple-element.217), channel_id=1, source_target_pairs={{0,2},{1,5},{2,0},{3,7},{4,6},{5,1},{6,4},{7,3},{8,10},{9,13},{10,... | collective-permute-start | bytes 393224 | tf_op jit(solution)/shard_map/ppermute | solution.py:344
  342.6 11.4 %collective-permute-start.135 = (f32[256,128]{1,0:T(8,128)S(1)}, f32[256,128]{1,0:T(8,128)S(1)}, u32[]{:S(2)}, u32[]{:S(2)}) collective-permute-start(f32[256,128]{1,0:T(8,128)S(1)} %fusion.5.refs_0_), channel_id=1, source_target_pairs={{0,4},{1,7},{2,6},{3,5},{4,0},{5,3},{6,2},{7,1},{8,12},{9,15},{10,... | collective-permute-start | bytes 393224 | tf_op jit(solution)/shard_map/ppermute | solution.py:344
  342.6 11.4 %collective-permute-start.136 = (f32[256,128]{1,0:T(8,128)S(1)}, f32[256,128]{1,0:T(8,128)S(1)}, u32[]{:S(2)}, u32[]{:S(2)}) collective-permute-start(f32[256,128]{1,0:T(8,128)S(1)} %fusion.5.refs_0_), channel_id=1, source_target_pairs={{0,2},{1,5},{2,0},{3,7},{4,6},{5,1},{6,4},{7,3},{8,10},{9,13},{10,... | collective-permute-start | bytes 393224 | tf_op jit(solution)/shard_map/ppermute | solution.py:344
  (140 other events, 1146.3 us)

commit v6 on v5

--- a/solution.py
+++ b/solution.py
@@ -41,8 +41,8 @@
 
 
 def partners(count, rows):
-    far_first = list(range(count - 1, 0, -1))
-    return list(zip(far_first, far_first[-1:] + far_first[:-1] if rows >= 2 * BLOCK else far_first))
+    near_first = list(range(1, count))
+    return list(zip(near_first, near_first[-1:] + near_first[:-1] if rows >= 2 * BLOCK else near_first))
 
 
 def spread_parts(meta, full, parts, offset=0):
@@ -174,18 +174,15 @@
 
 
 def owed_top_kernel(listed, height, meta, *refs):
-    parts, owed = refs[:-1], refs[-1]
+    parts, (deferred, owed) = refs[:-2], refs[-2:]
     blocks = owed.shape[0] // height
-    start = parts[-1].shape[0]
     size = listed * height + 8
     first = (2 * meta[0] + meta[1]) * blocks
     for b in range(blocks):
         wanted = (first + b).astype(F32)
-        total = jnp.zeros((height, owed.shape[1]), F32)
+        total = deferred[b * height : (b + 1) * height, :]
         for item in parts:
-            if item.shape[0] > start:
-                total = total + item[start + b * height : start + (b + 1) * height, :]
-            for at in range(0, start, size):
+            for at in range(0, item.shape[0], size):
                 for k in range(listed):
                     number = item[at + listed * height + k : at + listed * height + k + 1, :]
                     term = item[at + k * height : at + (k + 1) * height, :]
@@ -487,6 +484,7 @@
     )
     deferred = to_leaves(leaf_cuts)
     solved[1] = scatter_sum(*forward_inv(1, owed_parts(parts, 1)))
+    parts, deferred = lax.optimization_barrier((gather(solved[1]), deferred))
 
     pieces = call(
         functools.partial(forward_last_kernel, nz, group, leaves),
@@ -497,15 +495,15 @@
         2,
         meta,
         own_rows[1],
-        *gather(solved[1]),
+        *parts,
         panel[1],
     )
+    own_piece = pieces[0]
     pieces = to_leaves(pieces)
     piece = jnp.concatenate([sum(pieces[d : d + group]) for d in range(0, leaves, group)], axis=0)
-    deferred = sum(deferred)
-    own = scatter_chips(
-        lambda chip: jnp.concatenate([piece, lax.dynamic_index_in_dim(deferred, chip, 0, False)], axis=0),
-        partners(nz, piece.shape[0] + top_rows),
+    deferred = beside(sum(deferred), own_piece)
+    deferred = scatter_chips(
+        lambda chip: lax.dynamic_index_in_dim(deferred, chip, 0, False), partners(nz, top_rows)
     )
     owed = call(
         functools.partial(owed_top_kernel, listed[1], thin),
@@ -515,8 +513,8 @@
         0,
         1,
         meta,
-        *own,
-        *[to_core(item[: piece.shape[0]]) for item in own],
+        *gather(piece),
+        sum(deferred),
     )
     keep, send = call(
         functools.partial(forward_top_kernel, leaves),

time: 368 us -> 363 us (0.986)
  waiting for transfers between devices: 190 us -> 185 us
    ppermute x60 -> x63, starting transfers between devices: 89.4 us -> 94.1 us  [to_chip(): lax.ppermute(x, 'rows', [(r, r ^ 2 * step[r % 2]) for r in range(devices)])]
    ppermute x30, starting transfers between devices: 39 us -> 34.4 us  [to_leaf(): lax.ppermute(x, 'leaf', [(i, i ^ k) for i in range(leaves)])]
    ppermute x30, waiting for transfers between devices: 37.4 us -> 33 us  [to_leaf(): lax.ppermute(x, 'leaf', [(i, i ^ k) for i in range(leaves)])]
    ppermute x60 -> x63, waiting for transfers between devices: 128 us -> 127 us  [to_chip(): lax.ppermute(x, 'rows', [(r, r ^ 2 * step[r % 2]) for r in range(devices)])]
  transfers between devices with their start and end apart: 144 -> 147, of which waited for: 86 -> 85; matrix products, arithmetic and copies ran while one was open for 1% -> 1% of each run, Pallas kernels for 2% -> 2%
where the time goes in v6:
time: 363 us
  waiting for transfers between devices  185 us (51%)
  starting transfers between devices  140 us (39%)
  Pallas kernels  26.7 us (7%)
  local copies, waits for them, and re-layouts  6.64 us (2%)
  other arithmetic  3.69 us (1%)
    ppermute x63, waiting for transfers between devices, to_chip(): lax.ppermute(x, 'rows', [(r, r ^ 2 * step[r % 2]) for r in range(devices)])  127 us
    ppermute x63, starting transfers between devices, to_chip(): lax.ppermute(x, 'rows', [(r, r ^ 2 * step[r % 2]) for r in range(devices)])  94.1 us
    ppermute x30, starting transfers between devices, to_leaf(): lax.ppermute(x, 'leaf', [(i, i ^ k) for i in range(leaves)])  34.4 us
    ppermute x30, waiting for transfers between devices, to_leaf(): lax.ppermute(x, 'leaf', [(i, i ^ k) for i in range(leaves)])  33 us
    pallas_call x19, Pallas kernels, call(): pl.pallas_call(kernel, out_shape=outs, in_specs=[SMEM] * smem_count + [VM...  26.7 us
    ppermute x54, waiting for transfers between devices, to_core(): return lax.ppermute(x, 'rows', [(r, r ^ 1) for r in range(devices)])  24.5 us
    ppermute x54, starting transfers between devices, to_core(): return lax.ppermute(x, 'rows', [(r, r ^ 1) for r in range(devices)])  11.2 us
  transfers between devices with their start and end apart: 147, of which 85 were waited for; matrix products, arithmetic and copies ran while one was open for 1% of the time, Pallas kernels for 2%

profile of v6, /device:TPU:0, one launch (start us, length us, event | category | flops | bytes accessed | tf_op | source)
XLA Modules:
  0.0 363.0 jit_solution(14371847402554362418)
XLA Ops:
  6.4 3.0 collective-permute-start.1
  9.4 2.6 collective-permute-start.2
  12.7 8.3 %collective-permute-done.2 = f32[256,128]{1,0:T(8,128)S(1)} collective-permute-done((f32[256,128]{1,0:T(8,128)S(1)}, f32[256,128]{1,0:T(8,128)S(1)}, u32[]{:S(2)}, u32[]{:S(2)}) %collective-permute-start.2) | collective-permute-done | bytes 131104 | tf_op jit(solution)/shard_map/ppermute | solution.py:341
  21.1 3.6 collective-permute-start.6
  25.8 3.7 %collective-permute-done.6.refs_3_ = f32[256,128]{1,0:T(8,128)S(1)} collective-permute-done((f32[256,128]{1,0:T(8,128)S(1)}, f32[256,128]{1,0:T(8,128)S(1)}, u32[]{:S(2)}, u32[]{:S(2)}) %collective-permute-start.6) | collective-permute-done | bytes 131104 | tf_op jit(solution)/shard_map/ppermute | solution.py:341
  33.4 3.1 collective-permute-done.5.refs_2_
  48.6 4.2 %collective-permute-done.12.refs_1_ = f32[256,128]{1,0:T(8,128)S(1)} collective-permute-done((f32[256,128]{1,0:T(8,128)S(1)}, f32[256,128]{1,0:T(8,128)S(1)}, u32[]{:S(2)}, u32[]{:S(2)}) %collective-permute-start.12) | collective-permute-done | bytes 131104 | tf_op jit(solution)/shard_map/ppermute | solution.py:341
  52.8 4.3 %collective-permute-done.13.refs_2_ = f32[256,128]{1,0:T(8,128)S(1)} collective-permute-done((f32[256,128]{1,0:T(8,128)S(1)}, f32[256,128]{1,0:T(8,128)S(1)}, u32[]{:S(2)}, u32[]{:S(2)}) %collective-permute-start.13) | collective-permute-done | bytes 131104 | tf_op jit(solution)/shard_map/ppermute | solution.py:341
  65.2 3.7 %collective-permute-done.16 = f32[256,128]{1,0:T(8,128)S(1)} collective-permute-done((f32[256,128]{1,0:T(8,128)S(1)}, f32[256,128]{1,0:T(8,128)S(1)}, u32[]{:S(2)}, u32[]{:S(2)}) %collective-permute-start.16) | collective-permute-done | bytes 131104 | tf_op jit(solution)/shard_map/ppermute | solution.py:341
  68.8 5.5 %collective-permute-done.17 = f32[256,128]{1,0:T(8,128)S(1)} collective-permute-done((f32[256,128]{1,0:T(8,128)S(1)}, f32[256,128]{1,0:T(8,128)S(1)}, u32[]{:S(2)}, u32[]{:S(2)}) %collective-permute-start.17) | collective-permute-done | bytes 131104 | tf_op jit(solution)/shard_map/ppermute | solution.py:341
  79.3 5.5 %collective-permute-done.19.refs_2_ = f32[256,128]{1,0:T(8,128)S(1)} collective-permute-done((f32[256,128]{1,0:T(8,128)S(1)}, f32[256,128]{1,0:T(8,128)S(1)}, u32[]{:S(2)}, u32[]{:S(2)}) %collective-permute-start.19) | collective-permute-done | bytes 131104 | tf_op jit(solution)/shard_map/ppermute | solution.py:341
  85.3 2.7 collective-permute-done.21.refs_4_
  98.7 4.2 %collective-permute-done.27 = f32[256,128]{1,0:T(8,128)S(1)} collective-permute-done((f32[256,128]{1,0:T(8,128)S(1)}, f32[256,128]{1,0:T(8,128)S(1)}, u32[]{:S(2)}, u32[]{:S(2)}) %collective-permute-start.27) | collective-permute-done | bytes 131104 | tf_op jit(solution)/shard_map/ppermute | solution.py:341
  102.9 5.1 %collective-permute-done.28 = f32[256,128]{1,0:T(8,128)S(1)} collective-permute-done((f32[256,128]{1,0:T(8,128)S(1)}, f32[256,128]{1,0:T(8,128)S(1)}, u32[]{:S(2)}, u32[]{:S(2)}) %collective-permute-start.28) | collective-permute-done | bytes 131104 | tf_op jit(solution)/shard_map/ppermute | solution.py:341
  109.6 4.2 %collective-permute-done.30.refs_1_ = f32[256,128]{1,0:T(8,128)S(1)} collective-permute-done((f32[256,128]{1,0:T(8,128)S(1)}, f32[256,128]{1,0:T(8,128)S(1)}, u32[]{:S(2)}, u32[]{:S(2)}) %collective-permute-start.30) | collective-permute-done | bytes 131104 | tf_op jit(solution)/shard_map/ppermute | solution.py:344
  122.6 4.6 %collective-permute-done.33 = f32[128,128]{1,0:T(8,128)S(1)} collective-permute-done((f32[128,128]{1,0:T(8,128)S(1)}, f32[128,128]{1,0:T(8,128)S(1)}, u32[]{:S(2)}, u32[]{:S(2)}) %collective-permute-start.33) | collective-permute-done | bytes 65568 | tf_op jit(solution)/shard_map/ppermute | solution.py:341
  136.1 2.9 collective-permute-done.36.refs_2_
  158.4 7.1 %collective-permute-done.57 = f32[128,128]{1,0:T(8,128)S(1)} collective-permute-done((f32[128,128]{1,0:T(8,128)S(1)}, f32[128,128]{1,0:T(8,128)S(1)}, u32[]{:S(2)}, u32[]{:S(2)}) %collective-permute-start.57) | collective-permute-done | bytes 65568 | tf_op jit(solution)/shard_map/ppermute | solution.py:341
  183.2 3.5 collective-permute-done.64
  191.6 2.8 collective-permute-done.67.refs_2_
  232.9 3.5 collective-permute-done.91
  252.1 3.8 %collective-permute-done.103 = f32[1,256,128]{2,1,0:T(8,128)S(1)} collective-permute-done((f32[1,256,128]{2,1,0:T(8,128)S(1)}, f32[1,256,128]{2,1,0:T(8,128)S(1)}, u32[]{:S(2)}, u32[]{:S(2)}) %collective-permute-start.103) | collective-permute-done | bytes 131104 | tf_op jit(solution)/shard_map/ppermute | solution.py:344
  261.4 2.9 collective-permute-done.104.refs_5_
  278.7 7.2 %collective-permute-done.114 = f32[256,128]{1,0:T(8,128)S(1)} collective-permute-done((f32[256,128]{1,0:T(8,128)S(1)}, f32[256,128]{1,0:T(8,128)S(1)}, u32[]{:S(2)}, u32[]{:S(2)}) %collective-permute-start.114) | collective-permute-done | bytes 131104 | tf_op jit(solution)/shard_map/ppermute | solution.py:341
  290.5 5.3 %collective-permute-done.116.refs_1_ = f32[256,128]{1,0:T(8,128)S(1)} collective-permute-done((f32[256,128]{1,0:T(8,128)S(1)}, f32[256,128]{1,0:T(8,128)S(1)}, u32[]{:S(2)}, u32[]{:S(2)}) %collective-permute-start.116) | collective-permute-done | bytes 131104 | tf_op jit(solution)/shard_map/ppermute | solution.py:341
  296.4 2.6 collective-permute-done.118.refs_3_
  310.0 5.3 %collective-permute-done.124.refs_6_ = f32[256,128]{1,0:T(8,128)S(1)} collective-permute-done((f32[256,128]{1,0:T(8,128)S(1)}, f32[256,128]{1,0:T(8,128)S(1)}, u32[]{:S(2)}, u32[]{:S(2)}) %collective-permute-start.124) | collective-permute-done | bytes 131104 | tf_op jit(solution)/shard_map/ppermute | solution.py:341
  317.5 3.5 backward_panel_3.1
  329.4 7.2 %collective-permute-done.135 = f32[256,128]{1,0:T(8,128)S(1)} collective-permute-done((f32[256,128]{1,0:T(8,128)S(1)}, f32[256,128]{1,0:T(8,128)S(1)}, u32[]{:S(2)}, u32[]{:S(2)}) %collective-permute-start.135) | collective-permute-done | bytes 131104 | tf_op jit(solution)/shard_map/ppermute | solution.py:341
  341.8 5.2 %collective-permute-done.137.refs_1_ = f32[256,128]{1,0:T(8,128)S(1)} collective-permute-done((f32[256,128]{1,0:T(8,128)S(1)}, f32[256,128]{1,0:T(8,128)S(1)}, u32[]{:S(2)}, u32[]{:S(2)}) %collective-permute-start.137) | collective-permute-done | bytes 131104 | tf_op jit(solution)/shard_map/ppermute | solution.py:341
  347.6 2.8 collective-permute-done.139.refs_3_
  359.1 3.0 collective-permute-done.145
  (407 shorter events, 224.5 us)
Async XLA Ops:
  9.4 11.6 %collective-permute-start.2 = (f32[256,128]{1,0:T(8,128)S(1)}, f32[256,128]{1,0:T(8,128)S(1)}, u32[]{:S(2)}, u32[]{:S(2)}) collective-permute-start(f32[256,128]{1,0:T(8,128)S(1)} %get-tuple-element.257), channel_id=1, source_target_pairs={{0,4},{1,3},{2,6},{3,1},{4,0},{5,7},{6,2},{7,5},{8,12},{9,11},{10,... | collective-permute-start | bytes 393224 | tf_op jit(solution)/shard_map/ppermute | solution.py:341
  25.8 10.7 %collective-permute-start.5 = (f32[256,128]{1,0:T(8,128)S(1)}, f32[256,128]{1,0:T(8,128)S(1)}, u32[]{:S(2)}, u32[]{:S(2)}) collective-permute-start(f32[256,128]{1,0:T(8,128)S(1)} %add_add_fusion.2.refs_0_), channel_id=1, source_target_pairs={{0,4},{1,3},{2,6},{3,1},{4,0},{5,7},{6,2},{7,5},{8,12},{9,11},{10,... | collective-permute-start | bytes 393224 | tf_op jit(solution)/shard_map/ppermute | solution.py:341
  25.8 10.7 %collective-permute-start.7 = (f32[256,128]{1,0:T(8,128)S(1)}, f32[256,128]{1,0:T(8,128)S(1)}, u32[]{:S(2)}, u32[]{:S(2)}) collective-permute-start(f32[256,128]{1,0:T(8,128)S(1)} %add_add_fusion.2.refs_0_), channel_id=1, source_target_pairs={{0,1},{1,0},{2,3},{3,2},{4,5},{5,4},{6,7},{7,6},{8,9},{9,8},{10,11... | collective-permute-start | bytes 393224 | tf_op jit(solution)/shard_map/ppermute | solution.py:338
  44.3 12.9 %collective-permute-start.13 = (f32[256,128]{1,0:T(8,128)S(1)}, f32[256,128]{1,0:T(8,128)S(1)}, u32[]{:S(2)}, u32[]{:S(2)}) collective-permute-start(f32[256,128]{1,0:T(8,128)S(1)} %get-tuple-element.253), channel_id=1, source_target_pairs={{0,4},{1,3},{2,6},{3,1},{4,0},{5,7},{6,2},{7,5},{8,12},{9,11},{10,... | collective-permute-start | bytes 393224 | tf_op jit(solution)/shard_map/ppermute | solution.py:341
  46.4 10.7 %collective-permute-start.14 = (f32[256,128]{1,0:T(8,128)S(1)}, f32[256,128]{1,0:T(8,128)S(1)}, u32[]{:S(2)}, u32[]{:S(2)}) collective-permute-start(f32[256,128]{1,0:T(8,128)S(1)} %get-tuple-element.252), channel_id=1, source_target_pairs={{0,6},{1,5},{2,4},{3,7},{4,2},{5,1},{6,0},{7,3},{8,14},{9,13},{10,... | collective-permute-start | bytes 393224 | tf_op jit(solution)/shard_map/ppermute | solution.py:341
  62.7 11.6 %collective-permute-start.17 = (f32[256,128]{1,0:T(8,128)S(1)}, f32[256,128]{1,0:T(8,128)S(1)}, u32[]{:S(2)}, u32[]{:S(2)}) collective-permute-start(f32[256,128]{1,0:T(8,128)S(1)} %get-tuple-element.251), channel_id=1, source_target_pairs={{0,4},{1,3},{2,6},{3,1},{4,0},{5,7},{6,2},{7,5},{8,12},{9,11},{10,... | collective-permute-start | bytes 393224 | tf_op jit(solution)/shard_map/ppermute | solution.py:341
  63.0 11.4 %collective-permute-start.18 = (f32[256,128]{1,0:T(8,128)S(1)}, f32[256,128]{1,0:T(8,128)S(1)}, u32[]{:S(2)}, u32[]{:S(2)}) collective-permute-start(f32[256,128]{1,0:T(8,128)S(1)} %get-tuple-element.250), channel_id=1, source_target_pairs={{0,6},{1,5},{2,4},{3,7},{4,2},{5,1},{6,0},{7,3},{8,14},{9,13},{10,... | collective-permute-start | bytes 393224 | tf_op jit(solution)/shard_map/ppermute | solution.py:341
  74.4 10.4 %collective-permute-start.19 = (f32[256,128]{1,0:T(8,128)S(1)}, f32[256,128]{1,0:T(8,128)S(1)}, u32[]{:S(2)}, u32[]{:S(2)}) collective-permute-start(f32[256,128]{1,0:T(8,128)S(1)} %fusion.7.refs_1_), channel_id=1, source_target_pairs={{0,2},{1,7},{2,0},{3,5},{4,6},{5,3},{6,4},{7,1},{8,10},{9,15},{10,... | collective-permute-start | bytes 393224 | tf_op jit(solution)/shard_map/ppermute | solution.py:341
  77.1 10.9 %collective-permute-start.21 = (f32[256,128]{1,0:T(8,128)S(1)}, f32[256,128]{1,0:T(8,128)S(1)}, u32[]{:S(2)}, u32[]{:S(2)}) collective-permute-start(f32[256,128]{1,0:T(8,128)S(1)} %fusion.7.refs_1_), channel_id=1, source_target_pairs={{0,6},{1,5},{2,4},{3,7},{4,2},{5,1},{6,0},{7,3},{8,14},{9,13},{10,... | collective-permute-start | bytes 393224 | tf_op jit(solution)/shard_map/ppermute | solution.py:341
  93.9 28.1 %collective-permute-start.42 = (f32[4,4,128,128]{3,2,1,0:T(8,128)}, f32[4,4,128,128]{3,2,1,0:T(8,128)S(1)}, u32[]{:S(2)}, u32[]{:S(2)}) collective-permute-start(f32[4,4,128,128]{3,2,1,0:T(8,128)} %get-tuple-element.146), channel_id=1, source_target_pairs={{0,1},{1,0},{2,3},{3,2},{4,5},{5,4},{6,7},{7,6},{8,9},{9,8},{10,11... | collective-permute-start | bytes 3145736 | tf_op jit(solution)/shard_map/ppermute | solution.py:338
  96.2 11.8 %collective-permute-start.28 = (f32[256,128]{1,0:T(8,128)S(1)}, f32[256,128]{1,0:T(8,128)S(1)}, u32[]{:S(2)}, u32[]{:S(2)}) collective-permute-start(f32[256,128]{1,0:T(8,128)S(1)} %get-tuple-element.248), channel_id=1, source_target_pairs={{0,4},{1,3},{2,6},{3,1},{4,0},{5,7},{6,2},{7,5},{8,12},{9,11},{10,... | collective-permute-start | bytes 393224 | tf_op jit(solution)/shard_map/ppermute | solution.py:341
  96.5 11.6 %collective-permute-start.29 = (f32[256,128]{1,0:T(8,128)S(1)}, f32[256,128]{1,0:T(8,128)S(1)}, u32[]{:S(2)}, u32[]{:S(2)}) collective-permute-start(f32[256,128]{1,0:T(8,128)S(1)} %get-tuple-element.247), channel_id=1, source_target_pairs={{0,6},{1,5},{2,4},{3,7},{4,2},{5,1},{6,0},{7,3},{8,14},{9,13},{10,... | collective-permute-start | bytes 393224 | tf_op jit(solution)/shard_map/ppermute | solution.py:341
  129.5 13.0 %collective-permute-start.43 = (f32[4,128,128]{2,1,0:T(8,128)S(1)}, f32[4,128,128]{2,1,0:T(8,128)S(1)}, u32[]{:S(2)}, u32[]{:S(2)}) collective-permute-start(f32[4,128,128]{2,1,0:T(8,128)S(1)} %get-tuple-element.148), channel_id=1, source_target_pairs={{0,8},{8,0},{16,24},{24,16},{1,9},{9,1},{17,25},{25,17},{2,10},{10... | collective-permute-start | bytes 786440 | tf_op jit(solution)/shard_map/ppermute | solution.py:344
  131.0 12.8 %collective-permute-start.44 = (f32[4,128,128]{2,1,0:T(8,128)S(1)}, f32[4,128,128]{2,1,0:T(8,128)S(1)}, u32[]{:S(2)}, u32[]{:S(2)}) collective-permute-start(f32[4,128,128]{2,1,0:T(8,128)S(1)} %get-tuple-element.149), channel_id=1, source_target_pairs={{0,16},{8,24},{16,0},{24,8},{1,17},{9,25},{17,1},{25,9},{2,18},{10... | collective-permute-start | bytes 786440 | tf_op jit(solution)/shard_map/ppermute | solution.py:344
  132.6 11.2 %collective-permute-start.45 = (f32[4,128,128]{2,1,0:T(8,128)S(1)}, f32[4,128,128]{2,1,0:T(8,128)S(1)}, u32[]{:S(2)}, u32[]{:S(2)}) collective-permute-start(f32[4,128,128]{2,1,0:T(8,128)S(1)} %get-tuple-element.150), channel_id=1, source_target_pairs={{0,24},{8,16},{16,8},{24,0},{1,25},{9,17},{17,9},{25,1},{2,26},{10... | collective-permute-start | bytes 786440 | tf_op jit(solution)/shard_map/ppermute | solution.py:344
  151.9 13.6 %collective-permute-start.49 = (f32[144,128]{1,0:T(8,128)S(1)}, f32[144,128]{1,0:T(8,128)S(1)}, u32[]{:S(2)}, u32[]{:S(2)}) collective-permute-start(f32[144,128]{1,0:T(8,128)S(1)} %pad_maximum_fusion.refs_0_), channel_id=1, source_target_pairs={{0,2},{1,3},{2,0},{3,1},{4,6},{5,7},{6,4},{7,5},{8,10},{9,11},{10,... | collective-permute-start | bytes 221192 | tf_op jit(solution)/shard_map/ppermute | solution.py:341
  152.5 13.5 %collective-permute-start.50 = (f32[144,128]{1,0:T(8,128)S(1)}, f32[144,128]{1,0:T(8,128)S(1)}, u32[]{:S(2)}, u32[]{:S(2)}) collective-permute-start(f32[144,128]{1,0:T(8,128)S(1)} %pad_maximum_fusion.refs_0_), channel_id=1, source_target_pairs={{0,4},{1,5},{2,6},{3,7},{4,0},{5,1},{6,2},{7,3},{8,12},{9,13},{10,... | collective-permute-start | bytes 221192 | tf_op jit(solution)/shard_map/ppermute | solution.py:341
  154.3 11.7 %collective-permute-start.51 = (f32[144,128]{1,0:T(8,128)S(1)}, f32[144,128]{1,0:T(8,128)S(1)}, u32[]{:S(2)}, u32[]{:S(2)}) collective-permute-start(f32[144,128]{1,0:T(8,128)S(1)} %pad_maximum_fusion.refs_0_), channel_id=1, source_target_pairs={{0,6},{1,7},{2,4},{3,5},{4,2},{5,3},{6,0},{7,1},{8,14},{9,15},{10,... | collective-permute-start | bytes 221192 | tf_op jit(solution)/shard_map/ppermute | solution.py:341
  156.3 9.1 %collective-permute-start.57 = (f32[128,128]{1,0:T(8,128)S(1)}, f32[128,128]{1,0:T(8,128)S(1)}, u32[]{:S(2)}, u32[]{:S(2)}) collective-permute-start(f32[128,128]{1,0:T(8,128)S(1)} %get-tuple-element.271), channel_id=1, source_target_pairs={{0,4},{1,5},{2,6},{3,7},{4,0},{5,1},{6,2},{7,3},{8,12},{9,13},{10,... | collective-permute-start | bytes 196616 | tf_op jit(solution)/shard_map/ppermute | solution.py:341
  156.3 10.2 %collective-permute-start.58 = (f32[128,128]{1,0:T(8,128)S(1)}, f32[128,128]{1,0:T(8,128)S(1)}, u32[]{:S(2)}, u32[]{:S(2)}) collective-permute-start(f32[128,128]{1,0:T(8,128)S(1)} %get-tuple-element.270), channel_id=1, source_target_pairs={{0,6},{1,7},{2,4},{3,5},{4,2},{5,3},{6,0},{7,1},{8,14},{9,15},{10,... | collective-permute-start | bytes 196616 | tf_op jit(solution)/shard_map/ppermute | solution.py:341
  256.2 10.1 %collective-permute-start.105 = (f32[256,128]{1,0:T(8,128)S(1)}, f32[256,128]{1,0:T(8,128)S(1)}, u32[]{:S(2)}, u32[]{:S(2)}) collective-permute-start(f32[256,128]{1,0:T(8,128)S(1)} %bitcast.134), channel_id=1, source_target_pairs={{0,4},{1,3},{2,6},{3,1},{4,0},{5,7},{6,2},{7,5},{8,12},{9,11},{10,... | collective-permute-start | bytes 393224 | tf_op jit(solution)/shard_map/ppermute | solution.py:341
  273.9 12.0 %collective-permute-start.114 = (f32[256,128]{1,0:T(8,128)S(1)}, f32[256,128]{1,0:T(8,128)S(1)}, u32[]{:S(2)}, u32[]{:S(2)}) collective-permute-start(f32[256,128]{1,0:T(8,128)S(1)} %get-tuple-element.245), channel_id=1, source_target_pairs={{0,4},{1,3},{2,6},{3,1},{4,0},{5,7},{6,2},{7,5},{8,12},{9,11},{10,... | collective-permute-start | bytes 393224 | tf_op jit(solution)/shard_map/ppermute | solution.py:341
  274.6 11.2 %collective-permute-start.115 = (f32[256,128]{1,0:T(8,128)S(1)}, f32[256,128]{1,0:T(8,128)S(1)}, u32[]{:S(2)}, u32[]{:S(2)}) collective-permute-start(f32[256,128]{1,0:T(8,128)S(1)} %get-tuple-element.244), channel_id=1, source_target_pairs={{0,6},{1,5},{2,4},{3,7},{4,2},{5,1},{6,0},{7,3},{8,14},{9,13},{10,... | collective-permute-start | bytes 393224 | tf_op jit(solution)/shard_map/ppermute | solution.py:341
  285.9 9.8 %collective-permute-start.116 = (f32[256,128]{1,0:T(8,128)S(1)}, f32[256,128]{1,0:T(8,128)S(1)}, u32[]{:S(2)}, u32[]{:S(2)}) collective-permute-start(f32[256,128]{1,0:T(8,128)S(1)} %fusion.5.refs_0_), channel_id=1, source_target_pairs={{0,2},{1,7},{2,0},{3,5},{4,6},{5,3},{6,4},{7,1},{8,10},{9,15},{10,... | collective-permute-start | bytes 393224 | tf_op jit(solution)/shard_map/ppermute | solution.py:341
  288.6 10.5 %collective-permute-start.118 = (f32[256,128]{1,0:T(8,128)S(1)}, f32[256,128]{1,0:T(8,128)S(1)}, u32[]{:S(2)}, u32[]{:S(2)}) collective-permute-start(f32[256,128]{1,0:T(8,128)S(1)} %fusion.5.refs_0_), channel_id=1, source_target_pairs={{0,6},{1,5},{2,4},{3,7},{4,2},{5,1},{6,0},{7,3},{8,14},{9,13},{10,... | collective-permute-start | bytes 393224 | tf_op jit(solution)/shard_map/ppermute | solution.py:341
  303.7 11.6 %collective-permute-start.124 = (f32[256,128]{1,0:T(8,128)S(1)}, f32[256,128]{1,0:T(8,128)S(1)}, u32[]{:S(2)}, u32[]{:S(2)}) collective-permute-start(f32[256,128]{1,0:T(8,128)S(1)} %bitcast.139), channel_id=1, source_target_pairs={{0,4},{1,3},{2,6},{3,1},{4,0},{5,7},{6,2},{7,5},{8,12},{9,11},{10,... | collective-permute-start | bytes 393224 | tf_op jit(solution)/shard_map/ppermute | solution.py:341
  304.3 11.0 %collective-permute-start.125 = (f32[256,128]{1,0:T(8,128)S(1)}, f32[256,128]{1,0:T(8,128)S(1)}, u32[]{:S(2)}, u32[]{:S(2)}) collective-permute-start(f32[256,128]{1,0:T(8,128)S(1)} %bitcast.140), channel_id=1, source_target_pairs={{0,6},{1,5},{2,4},{3,7},{4,2},{5,1},{6,0},{7,3},{8,14},{9,13},{10,... | collective-permute-start | bytes 393224 | tf_op jit(solution)/shard_map/ppermute | solution.py:341
  306.2 9.7 %collective-permute-start.130 = (f32[1,256,128]{2,1,0:T(8,128)S(1)}, f32[1,256,128]{2,1,0:T(8,128)S(1)}, u32[]{:S(2)}, u32[]{:S(2)}) collective-permute-start(f32[1,256,128]{2,1,0:T(8,128)S(1)} %beside.7), channel_id=1, source_target_pairs={{0,8},{8,0},{16,24},{24,16},{1,9},{9,1},{17,25},{25,17},{2,10},{10... | collective-permute-start | bytes 393224 | tf_op jit(solution)/shard_map/ppermute | solution.py:344
  325.1 11.6 %collective-permute-start.135 = (f32[256,128]{1,0:T(8,128)S(1)}, f32[256,128]{1,0:T(8,128)S(1)}, u32[]{:S(2)}, u32[]{:S(2)}) collective-permute-start(f32[256,128]{1,0:T(8,128)S(1)} %get-tuple-element.242), channel_id=1, source_target_pairs={{0,4},{1,3},{2,6},{3,1},{4,0},{5,7},{6,2},{7,5},{8,12},{9,11},{10,... | collective-permute-start | bytes 393224 | tf_op jit(solution)/shard_map/ppermute | solution.py:341
  325.7 11.0 %collective-permute-start.136 = (f32[256,128]{1,0:T(8,128)S(1)}, f32[256,128]{1,0:T(8,128)S(1)}, u32[]{:S(2)}, u32[]{:S(2)}) collective-permute-start(f32[256,128]{1,0:T(8,128)S(1)} %get-tuple-element.241), channel_id=1, source_target_pairs={{0,6},{1,5},{2,4},{3,7},{4,2},{5,1},{6,0},{7,3},{8,14},{9,13},{10,... | collective-permute-start | bytes 393224 | tf_op jit(solution)/shard_map/ppermute | solution.py:341
  336.8 10.3 %collective-permute-start.137 = (f32[256,128]{1,0:T(8,128)S(1)}, f32[256,128]{1,0:T(8,128)S(1)}, u32[]{:S(2)}, u32[]{:S(2)}) collective-permute-start(f32[256,128]{1,0:T(8,128)S(1)} %fusion.2.refs_0_), channel_id=1, source_target_pairs={{0,2},{1,7},{2,0},{3,5},{4,6},{5,3},{6,4},{7,1},{8,10},{9,15},{10,... | collective-permute-start | bytes 393224 | tf_op jit(solution)/shard_map/ppermute | solution.py:341
  339.8 10.6 %collective-permute-start.139 = (f32[256,128]{1,0:T(8,128)S(1)}, f32[256,128]{1,0:T(8,128)S(1)}, u32[]{:S(2)}, u32[]{:S(2)}) collective-permute-start(f32[256,128]{1,0:T(8,128)S(1)} %fusion.2.refs_0_), channel_id=1, source_target_pairs={{0,6},{1,5},{2,4},{3,7},{4,2},{5,1},{6,0},{7,3},{8,14},{9,13},{10,... | collective-permute-start | bytes 393224 | tf_op jit(solution)/shard_map/ppermute | solution.py:341
  (144 other events, 1129.2 us)

commit v7 on v6

--- a/solution.py
+++ b/solution.py
@@ -347,8 +347,23 @@
         far_first = {d: to_leaf(pieces[d], d) for d in reversed(range(len(pieces)))}
         return [far_first[d] for d in range(len(pieces))]
 
+    known = {}
+
+    def chip_index(step):
+        return known[step] if step in known else (z ^ jnp.where(core == 0, step[0], step[1])).astype(jnp.uint32)
+
+    def leaf_index(group, k):
+        return known[group, k, "leaf"] if known else (leaf // group ^ k).astype(jnp.uint32)
+
+    def small_indices():
+        steps = [(0, 0)] + partners(nz, BLOCK) + partners(nz, 2 * BLOCK)
+        found = {step: chip_index(step) for step in steps}
+        for group in {1, *groups}:
+            found.update({(group, k, "leaf"): leaf_index(group, k) for k in range(leaves // group)})
+        return list(found), list(found.values())
+
     def scatter_chips(chunk, steps):
-        return [chunk(z)] + [to_chip(chunk(z ^ jnp.where(core == 0, step[0], step[1])), step) for step in steps]
+        return [chunk(chip_index((0, 0)))] + [to_chip(chunk(chip_index(step)), step) for step in steps]
 
     def scatter_parts(keep, send):
         received = to_core(send)
@@ -394,7 +409,7 @@
     def place(parts, l):
         out = jnp.zeros(rhs[l].shape, F32)
         for k, item in enumerate(parts):
-            out = lax.dynamic_update_slice_in_dim(out, item, (leaf // groups[l] ^ k) * helds[l], 0)
+            out = lax.dynamic_update_slice_in_dim(out, item, leaf_index(groups[l], k) * helds[l], 0)
         return out
 
     def halves(rows):
@@ -422,7 +437,9 @@
     own_rhs = [None, None, None, leaf_rows(rhs[3], 3)]
     parts = scatter_parts(*forward_inv(3, []))
     index_rows = (None,) + after(arguments[11:14], parts[0])
-    parts, (own_rows, all_rows, early) = lax.optimization_barrier((parts, small_arrays()))
+    names, places = small_indices()
+    parts, (own_rows, all_rows, early), places = lax.optimization_barrier((parts, small_arrays(), places))
+    known.update(zip(names, places))
     own_rows, all_rows, own_rhs = [None] + own_rows, [None] + all_rows, [None] + early + own_rhs[3:]
     solved[3] = sum(parts)
     def forward_panel(l, below):
@@ -562,9 +579,9 @@
 
     blocks = owned[0] // BLOCK
     quarters, top_parts = lax.optimization_barrier((quarters, top_parts))
-    top = jnp.zeros((blocks, leaves, thin, width), F32)
+    top, zero = jnp.zeros((blocks, leaves, thin, width), F32), jnp.uint32(0)
     for d, item in enumerate(top_parts):
-        top = lax.dynamic_update_slice(top, item.reshape(blocks, 1, thin, width), (0, leaf ^ d, 0, 0))
+        top = lax.dynamic_update_slice(top, item.reshape(blocks, 1, thin, width), (zero, leaf_index(1, d), zero, zero))
     results = [top.reshape(rhs[0].shape)]
     picks = picked([1], "pick_1", quarters, 0)
     chain, parts = [], []

time: 363 us -> 361 us (level)
  transfers between devices with their start and end apart: 147 -> 147, of which waited for: 85 -> 88; matrix products, arithmetic and copies ran while one was open for 1% -> 1% of each run, Pallas kernels for 2% -> 1%
where the time goes in v7:
time: 361 us; the launch traced here: 360 us
  waiting for transfers between devices  184 us (51%)
  starting transfers between devices  140 us (39%)
  Pallas kernels  25.8 us (7%)
  local copies, waits for them, and re-layouts  6.62 us (2%)
    ppermute x63, waiting for transfers between devices, to_chip(): lax.ppermute(x, 'rows', [(r, r ^ 2 * step[r % 2]) for r in range(devices)])  126 us
    ppermute x63, starting transfers between devices, to_chip(): lax.ppermute(x, 'rows', [(r, r ^ 2 * step[r % 2]) for r in range(devices)])  94 us
    ppermute x30, starting transfers between devices, to_leaf(): lax.ppermute(x, 'leaf', [(i, i ^ k) for i in range(leaves)])  34.6 us
    ppermute x30, waiting for transfers between devices, to_leaf(): lax.ppermute(x, 'leaf', [(i, i ^ k) for i in range(leaves)])  33.3 us
    pallas_call x19, Pallas kernels, call(): pl.pallas_call(kernel, out_shape=outs, in_specs=[SMEM] * smem_count + [VM...  25.7 us
    ppermute x54, waiting for transfers between devices, to_core(): return lax.ppermute(x, 'rows', [(r, r ^ 1) for r in range(devices)])  24.6 us
    ppermute x54, starting transfers between devices, to_core(): return lax.ppermute(x, 'rows', [(r, r ^ 1) for r in range(devices)])  11.4 us
  transfers between devices with their start and end apart: 147, of which 88 were waited for; matrix products, arithmetic and copies ran while one was open for 1% of the time, Pallas kernels for 1%

profile of v7, /device:TPU:0, one launch (start us, length us, event | category | flops | bytes accessed | tf_op | source)
XLA Modules:
  0.0 360.4 jit_solution(4502696518090313268)
XLA Ops:
  6.4 3.0 collective-permute-start.1
  9.4 2.6 collective-permute-start.2
  12.7 8.3 %collective-permute-done.2 = f32[256,128]{1,0:T(8,128)S(1)} collective-permute-done((f32[256,128]{1,0:T(8,128)S(1)}, f32[256,128]{1,0:T(8,128)S(1)}, u32[]{:S(2)}, u32[]{:S(2)}) %collective-permute-start.2) | collective-permute-done | bytes 131104 | tf_op jit(solution)/shard_map/ppermute | solution.py:341
  21.1 3.6 %collective-permute-start.6 = (f32[256,128]{1,0:T(8,128)S(1)}, f32[256,128]{1,0:T(8,128)S(1)}, u32[]{:S(2)}, u32[]{:S(2)}) collective-permute-start(f32[256,128]{1,0:T(8,128)S(1)} %add_add_fusion.2.refs_0_), channel_id=1, source_target_pairs={{0,6},{1,5},{2,4},{3,7},{4,2},{5,1},{6,0},{7,3},{8,14},{9,13},{10,... | collective-permute-start | bytes 393224 | tf_op jit(solution)/shard_map/ppermute | solution.py:341
  25.8 3.7 %collective-permute-done.6.refs_3_ = f32[256,128]{1,0:T(8,128)S(1)} collective-permute-done((f32[256,128]{1,0:T(8,128)S(1)}, f32[256,128]{1,0:T(8,128)S(1)}, u32[]{:S(2)}, u32[]{:S(2)}) %collective-permute-start.6) | collective-permute-done | bytes 131104 | tf_op jit(solution)/shard_map/ppermute | solution.py:341
  33.4 3.1 collective-permute-done.5.refs_2_
  48.7 4.3 %collective-permute-done.12.refs_1_ = f32[256,128]{1,0:T(8,128)S(1)} collective-permute-done((f32[256,128]{1,0:T(8,128)S(1)}, f32[256,128]{1,0:T(8,128)S(1)}, u32[]{:S(2)}, u32[]{:S(2)}) %collective-permute-start.12) | collective-permute-done | bytes 131104 | tf_op jit(solution)/shard_map/ppermute | solution.py:341
  52.9 4.2 %collective-permute-done.13.refs_2_ = f32[256,128]{1,0:T(8,128)S(1)} collective-permute-done((f32[256,128]{1,0:T(8,128)S(1)}, f32[256,128]{1,0:T(8,128)S(1)}, u32[]{:S(2)}, u32[]{:S(2)}) %collective-permute-start.13) | collective-permute-done | bytes 131104 | tf_op jit(solution)/shard_map/ppermute | solution.py:341
  65.2 3.7 %collective-permute-done.16 = f32[256,128]{1,0:T(8,128)S(1)} collective-permute-done((f32[256,128]{1,0:T(8,128)S(1)}, f32[256,128]{1,0:T(8,128)S(1)}, u32[]{:S(2)}, u32[]{:S(2)}) %collective-permute-start.16) | collective-permute-done | bytes 131104 | tf_op jit(solution)/shard_map/ppermute | solution.py:341
  68.9 5.4 %collective-permute-done.17 = f32[256,128]{1,0:T(8,128)S(1)} collective-permute-done((f32[256,128]{1,0:T(8,128)S(1)}, f32[256,128]{1,0:T(8,128)S(1)}, u32[]{:S(2)}, u32[]{:S(2)}) %collective-permute-start.17) | collective-permute-done | bytes 131104 | tf_op jit(solution)/shard_map/ppermute | solution.py:341
  79.3 5.5 %collective-permute-done.19.refs_2_ = f32[256,128]{1,0:T(8,128)S(1)} collective-permute-done((f32[256,128]{1,0:T(8,128)S(1)}, f32[256,128]{1,0:T(8,128)S(1)}, u32[]{:S(2)}, u32[]{:S(2)}) %collective-permute-start.19) | collective-permute-done | bytes 131104 | tf_op jit(solution)/shard_map/ppermute | solution.py:341
  85.3 2.6 collective-permute-done.21.refs_4_
  98.0 4.2 %collective-permute-done.27 = f32[256,128]{1,0:T(8,128)S(1)} collective-permute-done((f32[256,128]{1,0:T(8,128)S(1)}, f32[256,128]{1,0:T(8,128)S(1)}, u32[]{:S(2)}, u32[]{:S(2)}) %collective-permute-start.27) | collective-permute-done | bytes 131104 | tf_op jit(solution)/shard_map/ppermute | solution.py:341
  102.2 5.1 %collective-permute-done.28 = f32[256,128]{1,0:T(8,128)S(1)} collective-permute-done((f32[256,128]{1,0:T(8,128)S(1)}, f32[256,128]{1,0:T(8,128)S(1)}, u32[]{:S(2)}, u32[]{:S(2)}) %collective-permute-start.28) | collective-permute-done | bytes 131104 | tf_op jit(solution)/shard_map/ppermute | solution.py:341
  109.0 4.1 %collective-permute-done.30.refs_1_ = f32[256,128]{1,0:T(8,128)S(1)} collective-permute-done((f32[256,128]{1,0:T(8,128)S(1)}, f32[256,128]{1,0:T(8,128)S(1)}, u32[]{:S(2)}, u32[]{:S(2)}) %collective-permute-start.30) | collective-permute-done | bytes 131104 | tf_op jit(solution)/shard_map/ppermute | solution.py:344
  120.9 4.5 %collective-permute-done.33 = f32[128,128]{1,0:T(8,128)S(1)} collective-permute-done((f32[128,128]{1,0:T(8,128)S(1)}, f32[128,128]{1,0:T(8,128)S(1)}, u32[]{:S(2)}, u32[]{:S(2)}) %collective-permute-start.33) | collective-permute-done | bytes 65568 | tf_op jit(solution)/shard_map/ppermute | solution.py:341
  133.4 2.9 collective-permute-done.36.refs_2_
  155.8 7.0 %collective-permute-done.57 = f32[128,128]{1,0:T(8,128)S(1)} collective-permute-done((f32[128,128]{1,0:T(8,128)S(1)}, f32[128,128]{1,0:T(8,128)S(1)}, u32[]{:S(2)}, u32[]{:S(2)}) %collective-permute-start.57) | collective-permute-done | bytes 65568 | tf_op jit(solution)/shard_map/ppermute | solution.py:341
  180.6 3.5 collective-permute-done.64
  189.0 2.8 collective-permute-done.67.refs_2_
  230.3 3.5 collective-permute-done.91
  249.5 3.9 %collective-permute-done.103 = f32[1,256,128]{2,1,0:T(8,128)S(1)} collective-permute-done((f32[1,256,128]{2,1,0:T(8,128)S(1)}, f32[1,256,128]{2,1,0:T(8,128)S(1)}, u32[]{:S(2)}, u32[]{:S(2)}) %collective-permute-start.103) | collective-permute-done | bytes 131104 | tf_op jit(solution)/shard_map/ppermute | solution.py:344
  258.8 2.9 collective-permute-done.104.refs_5_
  275.9 7.3 %collective-permute-done.114 = f32[256,128]{1,0:T(8,128)S(1)} collective-permute-done((f32[256,128]{1,0:T(8,128)S(1)}, f32[256,128]{1,0:T(8,128)S(1)}, u32[]{:S(2)}, u32[]{:S(2)}) %collective-permute-start.114) | collective-permute-done | bytes 131104 | tf_op jit(solution)/shard_map/ppermute | solution.py:341
  287.8 5.2 %collective-permute-done.116.refs_1_ = f32[256,128]{1,0:T(8,128)S(1)} collective-permute-done((f32[256,128]{1,0:T(8,128)S(1)}, f32[256,128]{1,0:T(8,128)S(1)}, u32[]{:S(2)}, u32[]{:S(2)}) %collective-permute-start.116) | collective-permute-done | bytes 131104 | tf_op jit(solution)/shard_map/ppermute | solution.py:341
  293.8 2.6 collective-permute-done.118.refs_3_
  307.3 5.3 %collective-permute-done.124.refs_6_ = f32[256,128]{1,0:T(8,128)S(1)} collective-permute-done((f32[256,128]{1,0:T(8,128)S(1)}, f32[256,128]{1,0:T(8,128)S(1)}, u32[]{:S(2)}, u32[]{:S(2)}) %collective-permute-start.124) | collective-permute-done | bytes 131104 | tf_op jit(solution)/shard_map/ppermute | solution.py:341
  314.9 3.5 backward_panel_3.1
  326.8 7.2 %collective-permute-done.135 = f32[256,128]{1,0:T(8,128)S(1)} collective-permute-done((f32[256,128]{1,0:T(8,128)S(1)}, f32[256,128]{1,0:T(8,128)S(1)}, u32[]{:S(2)}, u32[]{:S(2)}) %collective-permute-start.135) | collective-permute-done | bytes 131104 | tf_op jit(solution)/shard_map/ppermute | solution.py:341
  339.1 5.1 %collective-permute-done.137.refs_1_ = f32[256,128]{1,0:T(8,128)S(1)} collective-permute-done((f32[256,128]{1,0:T(8,128)S(1)}, f32[256,128]{1,0:T(8,128)S(1)}, u32[]{:S(2)}, u32[]{:S(2)}) %collective-permute-start.137) | collective-permute-done | bytes 131104 | tf_op jit(solution)/shard_map/ppermute | solution.py:341
  344.9 2.8 collective-permute-done.139.refs_3_
  356.5 3.1 collective-permute-done.145
  (405 shorter events, 222.1 us)
Async XLA Ops:
  9.4 11.6 %collective-permute-start.2 = (f32[256,128]{1,0:T(8,128)S(1)}, f32[256,128]{1,0:T(8,128)S(1)}, u32[]{:S(2)}, u32[]{:S(2)}) collective-permute-start(f32[256,128]{1,0:T(8,128)S(1)} %get-tuple-element.283), channel_id=1, source_target_pairs={{0,4},{1,3},{2,6},{3,1},{4,0},{5,7},{6,2},{7,5},{8,12},{9,11},{10,... | collective-permute-start | bytes 393224 | tf_op jit(solution)/shard_map/ppermute | solution.py:341
  25.8 10.7 %collective-permute-start.5 = (f32[256,128]{1,0:T(8,128)S(1)}, f32[256,128]{1,0:T(8,128)S(1)}, u32[]{:S(2)}, u32[]{:S(2)}) collective-permute-start(f32[256,128]{1,0:T(8,128)S(1)} %add_add_fusion.2.refs_0_), channel_id=1, source_target_pairs={{0,4},{1,3},{2,6},{3,1},{4,0},{5,7},{6,2},{7,5},{8,12},{9,11},{10,... | collective-permute-start | bytes 393224 | tf_op jit(solution)/shard_map/ppermute | solution.py:341
  25.8 10.7 %collective-permute-start.7 = (f32[256,128]{1,0:T(8,128)S(1)}, f32[256,128]{1,0:T(8,128)S(1)}, u32[]{:S(2)}, u32[]{:S(2)}) collective-permute-start(f32[256,128]{1,0:T(8,128)S(1)} %add_add_fusion.2.refs_0_), channel_id=1, source_target_pairs={{0,1},{1,0},{2,3},{3,2},{4,5},{5,4},{6,7},{7,6},{8,9},{9,8},{10,11... | collective-permute-start | bytes 393224 | tf_op jit(solution)/shard_map/ppermute | solution.py:338
  44.3 12.9 %collective-permute-start.13 = (f32[256,128]{1,0:T(8,128)S(1)}, f32[256,128]{1,0:T(8,128)S(1)}, u32[]{:S(2)}, u32[]{:S(2)}) collective-permute-start(f32[256,128]{1,0:T(8,128)S(1)} %get-tuple-element.279), channel_id=1, source_target_pairs={{0,4},{1,3},{2,6},{3,1},{4,0},{5,7},{6,2},{7,5},{8,12},{9,11},{10,... | collective-permute-start | bytes 393224 | tf_op jit(solution)/shard_map/ppermute | solution.py:341
  46.4 10.7 %collective-permute-start.14 = (f32[256,128]{1,0:T(8,128)S(1)}, f32[256,128]{1,0:T(8,128)S(1)}, u32[]{:S(2)}, u32[]{:S(2)}) collective-permute-start(f32[256,128]{1,0:T(8,128)S(1)} %get-tuple-element.278), channel_id=1, source_target_pairs={{0,6},{1,5},{2,4},{3,7},{4,2},{5,1},{6,0},{7,3},{8,14},{9,13},{10,... | collective-permute-start | bytes 393224 | tf_op jit(solution)/shard_map/ppermute | solution.py:341
  62.7 11.6 %collective-permute-start.17 = (f32[256,128]{1,0:T(8,128)S(1)}, f32[256,128]{1,0:T(8,128)S(1)}, u32[]{:S(2)}, u32[]{:S(2)}) collective-permute-start(f32[256,128]{1,0:T(8,128)S(1)} %get-tuple-element.277), channel_id=1, source_target_pairs={{0,4},{1,3},{2,6},{3,1},{4,0},{5,7},{6,2},{7,5},{8,12},{9,11},{10,... | collective-permute-start | bytes 393224 | tf_op jit(solution)/shard_map/ppermute | solution.py:341
  63.0 11.4 %collective-permute-start.18 = (f32[256,128]{1,0:T(8,128)S(1)}, f32[256,128]{1,0:T(8,128)S(1)}, u32[]{:S(2)}, u32[]{:S(2)}) collective-permute-start(f32[256,128]{1,0:T(8,128)S(1)} %get-tuple-element.276), channel_id=1, source_target_pairs={{0,6},{1,5},{2,4},{3,7},{4,2},{5,1},{6,0},{7,3},{8,14},{9,13},{10,... | collective-permute-start | bytes 393224 | tf_op jit(solution)/shard_map/ppermute | solution.py:341
  74.4 10.4 %collective-permute-start.19 = (f32[256,128]{1,0:T(8,128)S(1)}, f32[256,128]{1,0:T(8,128)S(1)}, u32[]{:S(2)}, u32[]{:S(2)}) collective-permute-start(f32[256,128]{1,0:T(8,128)S(1)} %fusion.7.refs_1_), channel_id=1, source_target_pairs={{0,2},{1,7},{2,0},{3,5},{4,6},{5,3},{6,4},{7,1},{8,10},{9,15},{10,... | collective-permute-start | bytes 393224 | tf_op jit(solution)/shard_map/ppermute | solution.py:341
  77.1 10.9 %collective-permute-start.21 = (f32[256,128]{1,0:T(8,128)S(1)}, f32[256,128]{1,0:T(8,128)S(1)}, u32[]{:S(2)}, u32[]{:S(2)}) collective-permute-start(f32[256,128]{1,0:T(8,128)S(1)} %fusion.7.refs_1_), channel_id=1, source_target_pairs={{0,6},{1,5},{2,4},{3,7},{4,2},{5,1},{6,0},{7,3},{8,14},{9,13},{10,... | collective-permute-start | bytes 393224 | tf_op jit(solution)/shard_map/ppermute | solution.py:341
  92.9 27.4 %collective-permute-start.42 = (f32[4,4,128,128]{3,2,1,0:T(8,128)S(1)}, f32[4,4,128,128]{3,2,1,0:T(8,128)S(1)}, u32[]{:S(2)}, u32[]{:S(2)}) collective-permute-start(f32[4,4,128,128]{3,2,1,0:T(8,128)S(1)} %get-tuple-element.166), channel_id=1, source_target_pairs={{0,1},{1,0},{2,3},{3,2},{4,5},{5,4},{6,7},{7,6},{8,9},{9,8},{10,11... | collective-permute-start | bytes 3145736 | tf_op jit(solution)/shard_map/ppermute | solution.py:338
  95.5 11.8 %collective-permute-start.28 = (f32[256,128]{1,0:T(8,128)S(1)}, f32[256,128]{1,0:T(8,128)S(1)}, u32[]{:S(2)}, u32[]{:S(2)}) collective-permute-start(f32[256,128]{1,0:T(8,128)S(1)} %get-tuple-element.274), channel_id=1, source_target_pairs={{0,4},{1,3},{2,6},{3,1},{4,0},{5,7},{6,2},{7,5},{8,12},{9,11},{10,... | collective-permute-start | bytes 393224 | tf_op jit(solution)/shard_map/ppermute | solution.py:341
  95.8 11.5 %collective-permute-start.29 = (f32[256,128]{1,0:T(8,128)S(1)}, f32[256,128]{1,0:T(8,128)S(1)}, u32[]{:S(2)}, u32[]{:S(2)}) collective-permute-start(f32[256,128]{1,0:T(8,128)S(1)} %get-tuple-element.273), channel_id=1, source_target_pairs={{0,6},{1,5},{2,4},{3,7},{4,2},{5,1},{6,0},{7,3},{8,14},{9,13},{10,... | collective-permute-start | bytes 393224 | tf_op jit(solution)/shard_map/ppermute | solution.py:341
  126.9 13.1 %collective-permute-start.43 = (f32[4,128,128]{2,1,0:T(8,128)S(1)}, f32[4,128,128]{2,1,0:T(8,128)S(1)}, u32[]{:S(2)}, u32[]{:S(2)}) collective-permute-start(f32[4,128,128]{2,1,0:T(8,128)S(1)} %get-tuple-element.168), channel_id=1, source_target_pairs={{0,8},{8,0},{16,24},{24,16},{1,9},{9,1},{17,25},{25,17},{2,10},{10... | collective-permute-start | bytes 786440 | tf_op jit(solution)/shard_map/ppermute | solution.py:344
  128.4 12.8 %collective-permute-start.44 = (f32[4,128,128]{2,1,0:T(8,128)S(1)}, f32[4,128,128]{2,1,0:T(8,128)S(1)}, u32[]{:S(2)}, u32[]{:S(2)}) collective-permute-start(f32[4,128,128]{2,1,0:T(8,128)S(1)} %get-tuple-element.169), channel_id=1, source_target_pairs={{0,16},{8,24},{16,0},{24,8},{1,17},{9,25},{17,1},{25,9},{2,18},{10... | collective-permute-start | bytes 786440 | tf_op jit(solution)/shard_map/ppermute | solution.py:344
  129.9 11.3 %collective-permute-start.45 = (f32[4,128,128]{2,1,0:T(8,128)S(1)}, f32[4,128,128]{2,1,0:T(8,128)S(1)}, u32[]{:S(2)}, u32[]{:S(2)}) collective-permute-start(f32[4,128,128]{2,1,0:T(8,128)S(1)} %get-tuple-element.170), channel_id=1, source_target_pairs={{0,24},{8,16},{16,8},{24,0},{1,25},{9,17},{17,9},{25,1},{2,26},{10... | collective-permute-start | bytes 786440 | tf_op jit(solution)/shard_map/ppermute | solution.py:344
  149.3 13.5 %collective-permute-start.49 = (f32[144,128]{1,0:T(8,128)S(1)}, f32[144,128]{1,0:T(8,128)S(1)}, u32[]{:S(2)}, u32[]{:S(2)}) collective-permute-start(f32[144,128]{1,0:T(8,128)S(1)} %pad_maximum_fusion.refs_0_), channel_id=1, source_target_pairs={{0,2},{1,3},{2,0},{3,1},{4,6},{5,7},{6,4},{7,5},{8,10},{9,11},{10,... | collective-permute-start | bytes 221192 | tf_op jit(solution)/shard_map/ppermute | solution.py:341
  149.9 13.4 %collective-permute-start.50 = (f32[144,128]{1,0:T(8,128)S(1)}, f32[144,128]{1,0:T(8,128)S(1)}, u32[]{:S(2)}, u32[]{:S(2)}) collective-permute-start(f32[144,128]{1,0:T(8,128)S(1)} %pad_maximum_fusion.refs_0_), channel_id=1, source_target_pairs={{0,4},{1,5},{2,6},{3,7},{4,0},{5,1},{6,2},{7,3},{8,12},{9,13},{10,... | collective-permute-start | bytes 221192 | tf_op jit(solution)/shard_map/ppermute | solution.py:341
  151.6 11.8 %collective-permute-start.51 = (f32[144,128]{1,0:T(8,128)S(1)}, f32[144,128]{1,0:T(8,128)S(1)}, u32[]{:S(2)}, u32[]{:S(2)}) collective-permute-start(f32[144,128]{1,0:T(8,128)S(1)} %pad_maximum_fusion.refs_0_), channel_id=1, source_target_pairs={{0,6},{1,7},{2,4},{3,5},{4,2},{5,3},{6,0},{7,1},{8,14},{9,15},{10,... | collective-permute-start | bytes 221192 | tf_op jit(solution)/shard_map/ppermute | solution.py:341
  153.7 9.1 %collective-permute-start.57 = (f32[128,128]{1,0:T(8,128)S(1)}, f32[128,128]{1,0:T(8,128)S(1)}, u32[]{:S(2)}, u32[]{:S(2)}) collective-permute-start(f32[128,128]{1,0:T(8,128)S(1)} %get-tuple-element.297), channel_id=1, source_target_pairs={{0,4},{1,5},{2,6},{3,7},{4,0},{5,1},{6,2},{7,3},{8,12},{9,13},{10,... | collective-permute-start | bytes 196616 | tf_op jit(solution)/shard_map/ppermute | solution.py:341
  153.7 10.1 %collective-permute-start.58 = (f32[128,128]{1,0:T(8,128)S(1)}, f32[128,128]{1,0:T(8,128)S(1)}, u32[]{:S(2)}, u32[]{:S(2)}) collective-permute-start(f32[128,128]{1,0:T(8,128)S(1)} %get-tuple-element.296), channel_id=1, source_target_pairs={{0,6},{1,7},{2,4},{3,5},{4,2},{5,3},{6,0},{7,1},{8,14},{9,15},{10,... | collective-permute-start | bytes 196616 | tf_op jit(solution)/shard_map/ppermute | solution.py:341
  253.6 10.1 %collective-permute-start.105 = (f32[256,128]{1,0:T(8,128)S(1)}, f32[256,128]{1,0:T(8,128)S(1)}, u32[]{:S(2)}, u32[]{:S(2)}) collective-permute-start(f32[256,128]{1,0:T(8,128)S(1)} %bitcast.134), channel_id=1, source_target_pairs={{0,4},{1,3},{2,6},{3,1},{4,0},{5,7},{6,2},{7,5},{8,12},{9,11},{10,... | collective-permute-start | bytes 393224 | tf_op jit(solution)/shard_map/ppermute | solution.py:341
  271.3 11.9 %collective-permute-start.114 = (f32[256,128]{1,0:T(8,128)S(1)}, f32[256,128]{1,0:T(8,128)S(1)}, u32[]{:S(2)}, u32[]{:S(2)}) collective-permute-start(f32[256,128]{1,0:T(8,128)S(1)} %get-tuple-element.271), channel_id=1, source_target_pairs={{0,4},{1,3},{2,6},{3,1},{4,0},{5,7},{6,2},{7,5},{8,12},{9,11},{10,... | collective-permute-start | bytes 393224 | tf_op jit(solution)/shard_map/ppermute | solution.py:341
  272.1 11.1 %collective-permute-start.115 = (f32[256,128]{1,0:T(8,128)S(1)}, f32[256,128]{1,0:T(8,128)S(1)}, u32[]{:S(2)}, u32[]{:S(2)}) collective-permute-start(f32[256,128]{1,0:T(8,128)S(1)} %get-tuple-element.270), channel_id=1, source_target_pairs={{0,6},{1,5},{2,4},{3,7},{4,2},{5,1},{6,0},{7,3},{8,14},{9,13},{10,... | collective-permute-start | bytes 393224 | tf_op jit(solution)/shard_map/ppermute | solution.py:341
  283.3 9.8 %collective-permute-start.116 = (f32[256,128]{1,0:T(8,128)S(1)}, f32[256,128]{1,0:T(8,128)S(1)}, u32[]{:S(2)}, u32[]{:S(2)}) collective-permute-start(f32[256,128]{1,0:T(8,128)S(1)} %fusion.5.refs_0_), channel_id=1, source_target_pairs={{0,2},{1,7},{2,0},{3,5},{4,6},{5,3},{6,4},{7,1},{8,10},{9,15},{10,... | collective-permute-start | bytes 393224 | tf_op jit(solution)/shard_map/ppermute | solution.py:341
  286.0 10.4 %collective-permute-start.118 = (f32[256,128]{1,0:T(8,128)S(1)}, f32[256,128]{1,0:T(8,128)S(1)}, u32[]{:S(2)}, u32[]{:S(2)}) collective-permute-start(f32[256,128]{1,0:T(8,128)S(1)} %fusion.5.refs_0_), channel_id=1, source_target_pairs={{0,6},{1,5},{2,4},{3,7},{4,2},{5,1},{6,0},{7,3},{8,14},{9,13},{10,... | collective-permute-start | bytes 393224 | tf_op jit(solution)/shard_map/ppermute | solution.py:341
  301.1 11.6 %collective-permute-start.124 = (f32[256,128]{1,0:T(8,128)S(1)}, f32[256,128]{1,0:T(8,128)S(1)}, u32[]{:S(2)}, u32[]{:S(2)}) collective-permute-start(f32[256,128]{1,0:T(8,128)S(1)} %bitcast.139), channel_id=1, source_target_pairs={{0,4},{1,3},{2,6},{3,1},{4,0},{5,7},{6,2},{7,5},{8,12},{9,11},{10,... | collective-permute-start | bytes 393224 | tf_op jit(solution)/shard_map/ppermute | solution.py:341
  301.8 10.9 %collective-permute-start.125 = (f32[256,128]{1,0:T(8,128)S(1)}, f32[256,128]{1,0:T(8,128)S(1)}, u32[]{:S(2)}, u32[]{:S(2)}) collective-permute-start(f32[256,128]{1,0:T(8,128)S(1)} %bitcast.140), channel_id=1, source_target_pairs={{0,6},{1,5},{2,4},{3,7},{4,2},{5,1},{6,0},{7,3},{8,14},{9,13},{10,... | collective-permute-start | bytes 393224 | tf_op jit(solution)/shard_map/ppermute | solution.py:341
  303.6 9.8 %collective-permute-start.130 = (f32[1,256,128]{2,1,0:T(8,128)S(1)}, f32[1,256,128]{2,1,0:T(8,128)S(1)}, u32[]{:S(2)}, u32[]{:S(2)}) collective-permute-start(f32[1,256,128]{2,1,0:T(8,128)S(1)} %beside.7), channel_id=1, source_target_pairs={{0,8},{8,0},{16,24},{24,16},{1,9},{9,1},{17,25},{25,17},{2,10},{10... | collective-permute-start | bytes 393224 | tf_op jit(solution)/shard_map/ppermute | solution.py:344
  322.4 11.6 %collective-permute-start.135 = (f32[256,128]{1,0:T(8,128)S(1)}, f32[256,128]{1,0:T(8,128)S(1)}, u32[]{:S(2)}, u32[]{:S(2)}) collective-permute-start(f32[256,128]{1,0:T(8,128)S(1)} %get-tuple-element.268), channel_id=1, source_target_pairs={{0,4},{1,3},{2,6},{3,1},{4,0},{5,7},{6,2},{7,5},{8,12},{9,11},{10,... | collective-permute-start | bytes 393224 | tf_op jit(solution)/shard_map/ppermute | solution.py:341
  323.1 10.9 %collective-permute-start.136 = (f32[256,128]{1,0:T(8,128)S(1)}, f32[256,128]{1,0:T(8,128)S(1)}, u32[]{:S(2)}, u32[]{:S(2)}) collective-permute-start(f32[256,128]{1,0:T(8,128)S(1)} %get-tuple-element.267), channel_id=1, source_target_pairs={{0,6},{1,5},{2,4},{3,7},{4,2},{5,1},{6,0},{7,3},{8,14},{9,13},{10,... | collective-permute-start | bytes 393224 | tf_op jit(solution)/shard_map/ppermute | solution.py:341
  334.0 10.2 %collective-permute-start.137 = (f32[256,128]{1,0:T(8,128)S(1)}, f32[256,128]{1,0:T(8,128)S(1)}, u32[]{:S(2)}, u32[]{:S(2)}) collective-permute-start(f32[256,128]{1,0:T(8,128)S(1)} %fusion.2.refs_0_), channel_id=1, source_target_pairs={{0,2},{1,7},{2,0},{3,5},{4,6},{5,3},{6,4},{7,1},{8,10},{9,15},{10,... | collective-permute-start | bytes 393224 | tf_op jit(solution)/shard_map/ppermute | solution.py:341
  337.2 10.5 %collective-permute-start.139 = (f32[256,128]{1,0:T(8,128)S(1)}, f32[256,128]{1,0:T(8,128)S(1)}, u32[]{:S(2)}, u32[]{:S(2)}) collective-permute-start(f32[256,128]{1,0:T(8,128)S(1)} %fusion.2.refs_0_), channel_id=1, source_target_pairs={{0,6},{1,5},{2,4},{3,7},{4,2},{5,1},{6,0},{7,3},{8,14},{9,13},{10,... | collective-permute-start | bytes 393224 | tf_op jit(solution)/shard_map/ppermute | solution.py:341
  (143 other events, 1097.2 us)

commit v8 on v7

--- a/solution.py
+++ b/solution.py
@@ -598,8 +598,9 @@
                 len(chain),
             ),
             f"backward_panel_{l}",
-            halves(chunks[l]) + ([shaped(above, width)] if l > 1 else []),
-            [
+            halves(chunks[l]) + ([shaped(above, width)] if l == 2 else []),
+            ([room(above, width)] if l == 3 else [])
+            + [
                 room(panel[l].shape[1], width),
                 pltpu.VMEM((panel[l].shape[1], 2 * width), BF16),
                 room(spans[l], width),

time: 361 us -> 362 us (level)
  other arithmetic: 1.97 us -> 7.94 us
  waiting for transfers between devices: 184 us -> 179 us
    reduce_sum x6, other arithmetic: 0.68 us -> 4.76 us  [flat_rows(): return jnp.sum(jnp.where(wanted, index_rows[l][None], 0), axis=(1, 2))]
    ppermute x63, waiting for transfers between devices: 126 us -> 123 us  [to_chip(): lax.ppermute(x, 'rows', [(r, r ^ 2 * step[r % 2]) for r in range(devices)])]
  transfers between devices with their start and end apart: 147 -> 147, of which waited for: 88 -> 87; matrix products, arithmetic and copies ran while one was open for 1% -> 2% of each run, Pallas kernels for 1% -> 1%
where the time goes in v8:
time: 362 us; the launch traced here: 361 us
  waiting for transfers between devices  179 us (49%)
  starting transfers between devices  140 us (39%)
  Pallas kernels  24.5 us (7%)
  local copies, waits for them, and re-layouts  8.3 us (2%)
  other arithmetic  7.94 us (2%)
    ppermute x63, waiting for transfers between devices, to_chip(): lax.ppermute(x, 'rows', [(r, r ^ 2 * step[r % 2]) for r in range(devices)])  123 us
    ppermute x63, starting transfers between devices, to_chip(): lax.ppermute(x, 'rows', [(r, r ^ 2 * step[r % 2]) for r in range(devices)])  94.1 us
    ppermute x30, starting transfers between devices, to_leaf(): lax.ppermute(x, 'leaf', [(i, i ^ k) for i in range(leaves)])  34.6 us
    ppermute x30, waiting for transfers between devices, to_leaf(): lax.ppermute(x, 'leaf', [(i, i ^ k) for i in range(leaves)])  33.3 us
    pallas_call x19, Pallas kernels, call(): pl.pallas_call(kernel, out_shape=outs, in_specs=[SMEM] * smem_count + [VM...  24.5 us
    ppermute x54, waiting for transfers between devices, to_core(): return lax.ppermute(x, 'rows', [(r, r ^ 1) for r in range(devices)])  23.1 us
    ppermute x54, starting transfers between devices, to_core(): return lax.ppermute(x, 'rows', [(r, r ^ 1) for r in range(devices)])  11.3 us
  transfers between devices with their start and end apart: 147, of which 87 were waited for; matrix products, arithmetic and copies ran while one was open for 2% of the time, Pallas kernels for 1%

profile of v8, /device:TPU:0, one launch (start us, length us, event | category | flops | bytes accessed | tf_op | source)
XLA Modules:
  0.0 361.4 jit_solution(4950705010463304691)
XLA Ops:
  6.3 3.0 collective-permute-start.1
  9.3 2.6 collective-permute-start.2
  16.7 4.2 %collective-permute-done.2 = f32[256,128]{1,0:T(8,128)S(1)} collective-permute-done((f32[256,128]{1,0:T(8,128)S(1)}, f32[256,128]{1,0:T(8,128)S(1)}, u32[]{:S(2)}, u32[]{:S(2)}) %collective-permute-start.2) | collective-permute-done | bytes 131104 | tf_op jit(solution)/shard_map/ppermute | solution.py:341
  21.0 3.6 %collective-permute-start.6 = (f32[256,128]{1,0:T(8,128)S(1)}, f32[256,128]{1,0:T(8,128)S(1)}, u32[]{:S(2)}, u32[]{:S(2)}) collective-permute-start(f32[256,128]{1,0:T(8,128)S(1)} %add_add_fusion.2.refs_0_), channel_id=1, source_target_pairs={{0,6},{1,5},{2,4},{3,7},{4,2},{5,1},{6,0},{7,3},{8,14},{9,13},{10,... | collective-permute-start | bytes 393224 | tf_op jit(solution)/shard_map/ppermute | solution.py:341
  25.7 3.7 %collective-permute-done.6.refs_3_ = f32[256,128]{1,0:T(8,128)S(1)} collective-permute-done((f32[256,128]{1,0:T(8,128)S(1)}, f32[256,128]{1,0:T(8,128)S(1)}, u32[]{:S(2)}, u32[]{:S(2)}) %collective-permute-start.6) | collective-permute-done | bytes 131104 | tf_op jit(solution)/shard_map/ppermute | solution.py:341
  33.3 3.1 collective-permute-done.5.refs_2_
  48.6 4.2 %collective-permute-done.12.refs_1_ = f32[256,128]{1,0:T(8,128)S(1)} collective-permute-done((f32[256,128]{1,0:T(8,128)S(1)}, f32[256,128]{1,0:T(8,128)S(1)}, u32[]{:S(2)}, u32[]{:S(2)}) %collective-permute-start.12) | collective-permute-done | bytes 131104 | tf_op jit(solution)/shard_map/ppermute | solution.py:341
  52.8 4.3 %collective-permute-done.13.refs_2_ = f32[256,128]{1,0:T(8,128)S(1)} collective-permute-done((f32[256,128]{1,0:T(8,128)S(1)}, f32[256,128]{1,0:T(8,128)S(1)}, u32[]{:S(2)}, u32[]{:S(2)}) %collective-permute-start.13) | collective-permute-done | bytes 131104 | tf_op jit(solution)/shard_map/ppermute | solution.py:341
  65.1 3.7 %collective-permute-done.16 = f32[256,128]{1,0:T(8,128)S(1)} collective-permute-done((f32[256,128]{1,0:T(8,128)S(1)}, f32[256,128]{1,0:T(8,128)S(1)}, u32[]{:S(2)}, u32[]{:S(2)}) %collective-permute-start.16) | collective-permute-done | bytes 131104 | tf_op jit(solution)/shard_map/ppermute | solution.py:341
  68.8 5.4 %collective-permute-done.17 = f32[256,128]{1,0:T(8,128)S(1)} collective-permute-done((f32[256,128]{1,0:T(8,128)S(1)}, f32[256,128]{1,0:T(8,128)S(1)}, u32[]{:S(2)}, u32[]{:S(2)}) %collective-permute-start.17) | collective-permute-done | bytes 131104 | tf_op jit(solution)/shard_map/ppermute | solution.py:341
  79.2 5.5 %collective-permute-done.19.refs_2_ = f32[256,128]{1,0:T(8,128)S(1)} collective-permute-done((f32[256,128]{1,0:T(8,128)S(1)}, f32[256,128]{1,0:T(8,128)S(1)}, u32[]{:S(2)}, u32[]{:S(2)}) %collective-permute-start.19) | collective-permute-done | bytes 131104 | tf_op jit(solution)/shard_map/ppermute | solution.py:341
  85.2 2.7 collective-permute-done.21.refs_4_
  97.9 4.2 %collective-permute-done.27 = f32[256,128]{1,0:T(8,128)S(1)} collective-permute-done((f32[256,128]{1,0:T(8,128)S(1)}, f32[256,128]{1,0:T(8,128)S(1)}, u32[]{:S(2)}, u32[]{:S(2)}) %collective-permute-start.27) | collective-permute-done | bytes 131104 | tf_op jit(solution)/shard_map/ppermute | solution.py:341
  102.2 5.1 %collective-permute-done.28 = f32[256,128]{1,0:T(8,128)S(1)} collective-permute-done((f32[256,128]{1,0:T(8,128)S(1)}, f32[256,128]{1,0:T(8,128)S(1)}, u32[]{:S(2)}, u32[]{:S(2)}) %collective-permute-start.28) | collective-permute-done | bytes 131104 | tf_op jit(solution)/shard_map/ppermute | solution.py:341
  108.9 4.1 %collective-permute-done.30.refs_1_ = f32[256,128]{1,0:T(8,128)S(1)} collective-permute-done((f32[256,128]{1,0:T(8,128)S(1)}, f32[256,128]{1,0:T(8,128)S(1)}, u32[]{:S(2)}, u32[]{:S(2)}) %collective-permute-start.30) | collective-permute-done | bytes 131104 | tf_op jit(solution)/shard_map/ppermute | solution.py:344
  120.8 4.6 %collective-permute-done.33 = f32[128,128]{1,0:T(8,128)S(1)} collective-permute-done((f32[128,128]{1,0:T(8,128)S(1)}, f32[128,128]{1,0:T(8,128)S(1)}, u32[]{:S(2)}, u32[]{:S(2)}) %collective-permute-start.33) | collective-permute-done | bytes 65568 | tf_op jit(solution)/shard_map/ppermute | solution.py:341
  133.3 2.9 collective-permute-done.36.refs_2_
  155.7 7.1 %collective-permute-done.57 = f32[128,128]{1,0:T(8,128)S(1)} collective-permute-done((f32[128,128]{1,0:T(8,128)S(1)}, f32[128,128]{1,0:T(8,128)S(1)}, u32[]{:S(2)}, u32[]{:S(2)}) %collective-permute-start.57) | collective-permute-done | bytes 65568 | tf_op jit(solution)/shard_map/ppermute | solution.py:341
  180.5 3.5 collective-permute-done.64
  189.0 2.8 collective-permute-done.67.refs_2_
  230.3 3.5 collective-permute-done.91
  249.4 3.8 %collective-permute-done.103 = f32[1,256,128]{2,1,0:T(8,128)S(1)} collective-permute-done((f32[1,256,128]{2,1,0:T(8,128)S(1)}, f32[1,256,128]{2,1,0:T(8,128)S(1)}, u32[]{:S(2)}, u32[]{:S(2)}) %collective-permute-start.103) | collective-permute-done | bytes 131104 | tf_op jit(solution)/shard_map/ppermute | solution.py:344
  258.8 2.9 collective-permute-done.104.refs_5_
  275.9 7.3 %collective-permute-done.114 = f32[256,128]{1,0:T(8,128)S(1)} collective-permute-done((f32[256,128]{1,0:T(8,128)S(1)}, f32[256,128]{1,0:T(8,128)S(1)}, u32[]{:S(2)}, u32[]{:S(2)}) %collective-permute-start.114) | collective-permute-done | bytes 131104 | tf_op jit(solution)/shard_map/ppermute | solution.py:341
  287.8 5.2 %collective-permute-done.116.refs_1_ = f32[256,128]{1,0:T(8,128)S(1)} collective-permute-done((f32[256,128]{1,0:T(8,128)S(1)}, f32[256,128]{1,0:T(8,128)S(1)}, u32[]{:S(2)}, u32[]{:S(2)}) %collective-permute-start.116) | collective-permute-done | bytes 131104 | tf_op jit(solution)/shard_map/ppermute | solution.py:341
  293.7 2.6 collective-permute-done.118.refs_3_
  307.3 5.3 %collective-permute-done.124.refs_6_ = f32[256,128]{1,0:T(8,128)S(1)} collective-permute-done((f32[256,128]{1,0:T(8,128)S(1)}, f32[256,128]{1,0:T(8,128)S(1)}, u32[]{:S(2)}, u32[]{:S(2)}) %collective-permute-start.124) | collective-permute-done | bytes 131104 | tf_op jit(solution)/shard_map/ppermute | solution.py:341
  327.0 7.1 %collective-permute-done.135 = f32[256,128]{1,0:T(8,128)S(1)} collective-permute-done((f32[256,128]{1,0:T(8,128)S(1)}, f32[256,128]{1,0:T(8,128)S(1)}, u32[]{:S(2)}, u32[]{:S(2)}) %collective-permute-start.135) | collective-permute-done | bytes 131104 | tf_op jit(solution)/shard_map/ppermute | solution.py:341
  340.2 5.2 %collective-permute-done.137.refs_1_ = f32[256,128]{1,0:T(8,128)S(1)} collective-permute-done((f32[256,128]{1,0:T(8,128)S(1)}, f32[256,128]{1,0:T(8,128)S(1)}, u32[]{:S(2)}, u32[]{:S(2)}) %collective-permute-start.137) | collective-permute-done | bytes 131104 | tf_op jit(solution)/shard_map/ppermute | solution.py:341
  345.9 2.9 collective-permute-done.139.refs_3_
  354.9 2.6 collective-permute-done.144
  357.5 3.0 collective-permute-done.145
  (403 shorter events, 228.1 us)
Async XLA Ops:
  6.3 10.4 %collective-permute-start.1 = (f32[256,128]{1,0:T(8,128)S(1)}, f32[256,128]{1,0:T(8,128)S(1)}, u32[]{:S(2)}, u32[]{:S(2)}) collective-permute-start(f32[256,128]{1,0:T(8,128)S(1)} %get-tuple-element.284), channel_id=1, source_target_pairs={{0,2},{1,7},{2,0},{3,5},{4,6},{5,3},{6,4},{7,1},{8,10},{9,15},{10,... | collective-permute-start | bytes 393224 | tf_op jit(solution)/shard_map/ppermute | solution.py:341
  9.3 11.6 %collective-permute-start.2 = (f32[256,128]{1,0:T(8,128)S(1)}, f32[256,128]{1,0:T(8,128)S(1)}, u32[]{:S(2)}, u32[]{:S(2)}) collective-permute-start(f32[256,128]{1,0:T(8,128)S(1)} %get-tuple-element.283), channel_id=1, source_target_pairs={{0,4},{1,3},{2,6},{3,1},{4,0},{5,7},{6,2},{7,5},{8,12},{9,11},{10,... | collective-permute-start | bytes 393224 | tf_op jit(solution)/shard_map/ppermute | solution.py:341
  25.7 10.7 %collective-permute-start.5 = (f32[256,128]{1,0:T(8,128)S(1)}, f32[256,128]{1,0:T(8,128)S(1)}, u32[]{:S(2)}, u32[]{:S(2)}) collective-permute-start(f32[256,128]{1,0:T(8,128)S(1)} %add_add_fusion.2.refs_0_), channel_id=1, source_target_pairs={{0,4},{1,3},{2,6},{3,1},{4,0},{5,7},{6,2},{7,5},{8,12},{9,11},{10,... | collective-permute-start | bytes 393224 | tf_op jit(solution)/shard_map/ppermute | solution.py:341
  25.7 10.7 %collective-permute-start.7 = (f32[256,128]{1,0:T(8,128)S(1)}, f32[256,128]{1,0:T(8,128)S(1)}, u32[]{:S(2)}, u32[]{:S(2)}) collective-permute-start(f32[256,128]{1,0:T(8,128)S(1)} %add_add_fusion.2.refs_0_), channel_id=1, source_target_pairs={{0,1},{1,0},{2,3},{3,2},{4,5},{5,4},{6,7},{7,6},{8,9},{9,8},{10,11... | collective-permute-start | bytes 393224 | tf_op jit(solution)/shard_map/ppermute | solution.py:338
  44.2 12.9 %collective-permute-start.13 = (f32[256,128]{1,0:T(8,128)S(1)}, f32[256,128]{1,0:T(8,128)S(1)}, u32[]{:S(2)}, u32[]{:S(2)}) collective-permute-start(f32[256,128]{1,0:T(8,128)S(1)} %get-tuple-element.279), channel_id=1, source_target_pairs={{0,4},{1,3},{2,6},{3,1},{4,0},{5,7},{6,2},{7,5},{8,12},{9,11},{10,... | collective-permute-start | bytes 393224 | tf_op jit(solution)/shard_map/ppermute | solution.py:341
  46.4 10.7 %collective-permute-start.14 = (f32[256,128]{1,0:T(8,128)S(1)}, f32[256,128]{1,0:T(8,128)S(1)}, u32[]{:S(2)}, u32[]{:S(2)}) collective-permute-start(f32[256,128]{1,0:T(8,128)S(1)} %get-tuple-element.278), channel_id=1, source_target_pairs={{0,6},{1,5},{2,4},{3,7},{4,2},{5,1},{6,0},{7,3},{8,14},{9,13},{10,... | collective-permute-start | bytes 393224 | tf_op jit(solution)/shard_map/ppermute | solution.py:341
  62.7 11.6 %collective-permute-start.17 = (f32[256,128]{1,0:T(8,128)S(1)}, f32[256,128]{1,0:T(8,128)S(1)}, u32[]{:S(2)}, u32[]{:S(2)}) collective-permute-start(f32[256,128]{1,0:T(8,128)S(1)} %get-tuple-element.277), channel_id=1, source_target_pairs={{0,4},{1,3},{2,6},{3,1},{4,0},{5,7},{6,2},{7,5},{8,12},{9,11},{10,... | collective-permute-start | bytes 393224 | tf_op jit(solution)/shard_map/ppermute | solution.py:341
  62.9 11.3 %collective-permute-start.18 = (f32[256,128]{1,0:T(8,128)S(1)}, f32[256,128]{1,0:T(8,128)S(1)}, u32[]{:S(2)}, u32[]{:S(2)}) collective-permute-start(f32[256,128]{1,0:T(8,128)S(1)} %get-tuple-element.276), channel_id=1, source_target_pairs={{0,6},{1,5},{2,4},{3,7},{4,2},{5,1},{6,0},{7,3},{8,14},{9,13},{10,... | collective-permute-start | bytes 393224 | tf_op jit(solution)/shard_map/ppermute | solution.py:341
  74.3 10.4 %collective-permute-start.19 = (f32[256,128]{1,0:T(8,128)S(1)}, f32[256,128]{1,0:T(8,128)S(1)}, u32[]{:S(2)}, u32[]{:S(2)}) collective-permute-start(f32[256,128]{1,0:T(8,128)S(1)} %fusion.7.refs_1_), channel_id=1, source_target_pairs={{0,2},{1,7},{2,0},{3,5},{4,6},{5,3},{6,4},{7,1},{8,10},{9,15},{10,... | collective-permute-start | bytes 393224 | tf_op jit(solution)/shard_map/ppermute | solution.py:341
  77.0 10.9 %collective-permute-start.21 = (f32[256,128]{1,0:T(8,128)S(1)}, f32[256,128]{1,0:T(8,128)S(1)}, u32[]{:S(2)}, u32[]{:S(2)}) collective-permute-start(f32[256,128]{1,0:T(8,128)S(1)} %fusion.7.refs_1_), channel_id=1, source_target_pairs={{0,6},{1,5},{2,4},{3,7},{4,2},{5,1},{6,0},{7,3},{8,14},{9,13},{10,... | collective-permute-start | bytes 393224 | tf_op jit(solution)/shard_map/ppermute | solution.py:341
  92.8 27.3 %collective-permute-start.42 = (f32[4,4,128,128]{3,2,1,0:T(8,128)S(1)}, f32[4,4,128,128]{3,2,1,0:T(8,128)S(1)}, u32[]{:S(2)}, u32[]{:S(2)}) collective-permute-start(f32[4,4,128,128]{3,2,1,0:T(8,128)S(1)} %get-tuple-element.166), channel_id=1, source_target_pairs={{0,1},{1,0},{2,3},{3,2},{4,5},{5,4},{6,7},{7,6},{8,9},{9,8},{10,11... | collective-permute-start | bytes 3145736 | tf_op jit(solution)/shard_map/ppermute | solution.py:338
  95.4 11.8 %collective-permute-start.28 = (f32[256,128]{1,0:T(8,128)S(1)}, f32[256,128]{1,0:T(8,128)S(1)}, u32[]{:S(2)}, u32[]{:S(2)}) collective-permute-start(f32[256,128]{1,0:T(8,128)S(1)} %get-tuple-element.274), channel_id=1, source_target_pairs={{0,4},{1,3},{2,6},{3,1},{4,0},{5,7},{6,2},{7,5},{8,12},{9,11},{10,... | collective-permute-start | bytes 393224 | tf_op jit(solution)/shard_map/ppermute | solution.py:341
  95.7 11.6 %collective-permute-start.29 = (f32[256,128]{1,0:T(8,128)S(1)}, f32[256,128]{1,0:T(8,128)S(1)}, u32[]{:S(2)}, u32[]{:S(2)}) collective-permute-start(f32[256,128]{1,0:T(8,128)S(1)} %get-tuple-element.273), channel_id=1, source_target_pairs={{0,6},{1,5},{2,4},{3,7},{4,2},{5,1},{6,0},{7,3},{8,14},{9,13},{10,... | collective-permute-start | bytes 393224 | tf_op jit(solution)/shard_map/ppermute | solution.py:341
  126.8 13.1 %collective-permute-start.43 = (f32[4,128,128]{2,1,0:T(8,128)S(1)}, f32[4,128,128]{2,1,0:T(8,128)S(1)}, u32[]{:S(2)}, u32[]{:S(2)}) collective-permute-start(f32[4,128,128]{2,1,0:T(8,128)S(1)} %get-tuple-element.168), channel_id=1, source_target_pairs={{0,8},{8,0},{16,24},{24,16},{1,9},{9,1},{17,25},{25,17},{2,10},{10... | collective-permute-start | bytes 786440 | tf_op jit(solution)/shard_map/ppermute | solution.py:344
  128.4 12.8 %collective-permute-start.44 = (f32[4,128,128]{2,1,0:T(8,128)S(1)}, f32[4,128,128]{2,1,0:T(8,128)S(1)}, u32[]{:S(2)}, u32[]{:S(2)}) collective-permute-start(f32[4,128,128]{2,1,0:T(8,128)S(1)} %get-tuple-element.169), channel_id=1, source_target_pairs={{0,16},{8,24},{16,0},{24,8},{1,17},{9,25},{17,1},{25,9},{2,18},{10... | collective-permute-start | bytes 786440 | tf_op jit(solution)/shard_map/ppermute | solution.py:344
  129.9 11.3 %collective-permute-start.45 = (f32[4,128,128]{2,1,0:T(8,128)S(1)}, f32[4,128,128]{2,1,0:T(8,128)S(1)}, u32[]{:S(2)}, u32[]{:S(2)}) collective-permute-start(f32[4,128,128]{2,1,0:T(8,128)S(1)} %get-tuple-element.170), channel_id=1, source_target_pairs={{0,24},{8,16},{16,8},{24,0},{1,25},{9,17},{17,9},{25,1},{2,26},{10... | collective-permute-start | bytes 786440 | tf_op jit(solution)/shard_map/ppermute | solution.py:344
  149.2 13.6 %collective-permute-start.49 = (f32[144,128]{1,0:T(8,128)S(1)}, f32[144,128]{1,0:T(8,128)S(1)}, u32[]{:S(2)}, u32[]{:S(2)}) collective-permute-start(f32[144,128]{1,0:T(8,128)S(1)} %pad_maximum_fusion.refs_0_), channel_id=1, source_target_pairs={{0,2},{1,3},{2,0},{3,1},{4,6},{5,7},{6,4},{7,5},{8,10},{9,11},{10,... | collective-permute-start | bytes 221192 | tf_op jit(solution)/shard_map/ppermute | solution.py:341
  149.8 13.5 %collective-permute-start.50 = (f32[144,128]{1,0:T(8,128)S(1)}, f32[144,128]{1,0:T(8,128)S(1)}, u32[]{:S(2)}, u32[]{:S(2)}) collective-permute-start(f32[144,128]{1,0:T(8,128)S(1)} %pad_maximum_fusion.refs_0_), channel_id=1, source_target_pairs={{0,4},{1,5},{2,6},{3,7},{4,0},{5,1},{6,2},{7,3},{8,12},{9,13},{10,... | collective-permute-start | bytes 221192 | tf_op jit(solution)/shard_map/ppermute | solution.py:341
  151.6 11.7 %collective-permute-start.51 = (f32[144,128]{1,0:T(8,128)S(1)}, f32[144,128]{1,0:T(8,128)S(1)}, u32[]{:S(2)}, u32[]{:S(2)}) collective-permute-start(f32[144,128]{1,0:T(8,128)S(1)} %pad_maximum_fusion.refs_0_), channel_id=1, source_target_pairs={{0,6},{1,7},{2,4},{3,5},{4,2},{5,3},{6,0},{7,1},{8,14},{9,15},{10,... | collective-permute-start | bytes 221192 | tf_op jit(solution)/shard_map/ppermute | solution.py:341
  153.7 10.1 %collective-permute-start.58 = (f32[128,128]{1,0:T(8,128)S(1)}, f32[128,128]{1,0:T(8,128)S(1)}, u32[]{:S(2)}, u32[]{:S(2)}) collective-permute-start(f32[128,128]{1,0:T(8,128)S(1)} %get-tuple-element.296), channel_id=1, source_target_pairs={{0,6},{1,7},{2,4},{3,5},{4,2},{5,3},{6,0},{7,1},{8,14},{9,15},{10,... | collective-permute-start | bytes 196616 | tf_op jit(solution)/shard_map/ppermute | solution.py:341
  253.5 10.1 %collective-permute-start.105 = (f32[256,128]{1,0:T(8,128)S(1)}, f32[256,128]{1,0:T(8,128)S(1)}, u32[]{:S(2)}, u32[]{:S(2)}) collective-permute-start(f32[256,128]{1,0:T(8,128)S(1)} %bitcast.134), channel_id=1, source_target_pairs={{0,4},{1,3},{2,6},{3,1},{4,0},{5,7},{6,2},{7,5},{8,12},{9,11},{10,... | collective-permute-start | bytes 393224 | tf_op jit(solution)/shard_map/ppermute | solution.py:341
  271.2 11.9 %collective-permute-start.114 = (f32[256,128]{1,0:T(8,128)S(1)}, f32[256,128]{1,0:T(8,128)S(1)}, u32[]{:S(2)}, u32[]{:S(2)}) collective-permute-start(f32[256,128]{1,0:T(8,128)S(1)} %get-tuple-element.271), channel_id=1, source_target_pairs={{0,4},{1,3},{2,6},{3,1},{4,0},{5,7},{6,2},{7,5},{8,12},{9,11},{10,... | collective-permute-start | bytes 393224 | tf_op jit(solution)/shard_map/ppermute | solution.py:341
  272.0 11.2 %collective-permute-start.115 = (f32[256,128]{1,0:T(8,128)S(1)}, f32[256,128]{1,0:T(8,128)S(1)}, u32[]{:S(2)}, u32[]{:S(2)}) collective-permute-start(f32[256,128]{1,0:T(8,128)S(1)} %get-tuple-element.270), channel_id=1, source_target_pairs={{0,6},{1,5},{2,4},{3,7},{4,2},{5,1},{6,0},{7,3},{8,14},{9,13},{10,... | collective-permute-start | bytes 393224 | tf_op jit(solution)/shard_map/ppermute | solution.py:341
  283.2 9.8 %collective-permute-start.116 = (f32[256,128]{1,0:T(8,128)S(1)}, f32[256,128]{1,0:T(8,128)S(1)}, u32[]{:S(2)}, u32[]{:S(2)}) collective-permute-start(f32[256,128]{1,0:T(8,128)S(1)} %fusion.5.refs_0_), channel_id=1, source_target_pairs={{0,2},{1,7},{2,0},{3,5},{4,6},{5,3},{6,4},{7,1},{8,10},{9,15},{10,... | collective-permute-start | bytes 393224 | tf_op jit(solution)/shard_map/ppermute | solution.py:341
  285.9 10.4 %collective-permute-start.118 = (f32[256,128]{1,0:T(8,128)S(1)}, f32[256,128]{1,0:T(8,128)S(1)}, u32[]{:S(2)}, u32[]{:S(2)}) collective-permute-start(f32[256,128]{1,0:T(8,128)S(1)} %fusion.5.refs_0_), channel_id=1, source_target_pairs={{0,6},{1,5},{2,4},{3,7},{4,2},{5,1},{6,0},{7,3},{8,14},{9,13},{10,... | collective-permute-start | bytes 393224 | tf_op jit(solution)/shard_map/ppermute | solution.py:341
  301.0 11.6 %collective-permute-start.124 = (f32[256,128]{1,0:T(8,128)S(1)}, f32[256,128]{1,0:T(8,128)S(1)}, u32[]{:S(2)}, u32[]{:S(2)}) collective-permute-start(f32[256,128]{1,0:T(8,128)S(1)} %bitcast.139), channel_id=1, source_target_pairs={{0,4},{1,3},{2,6},{3,1},{4,0},{5,7},{6,2},{7,5},{8,12},{9,11},{10,... | collective-permute-start | bytes 393224 | tf_op jit(solution)/shard_map/ppermute | solution.py:341
  301.7 10.9 %collective-permute-start.125 = (f32[256,128]{1,0:T(8,128)S(1)}, f32[256,128]{1,0:T(8,128)S(1)}, u32[]{:S(2)}, u32[]{:S(2)}) collective-permute-start(f32[256,128]{1,0:T(8,128)S(1)} %bitcast.140), channel_id=1, source_target_pairs={{0,6},{1,5},{2,4},{3,7},{4,2},{5,1},{6,0},{7,3},{8,14},{9,13},{10,... | collective-permute-start | bytes 393224 | tf_op jit(solution)/shard_map/ppermute | solution.py:341
  303.5 9.8 %collective-permute-start.130 = (f32[1,256,128]{2,1,0:T(8,128)S(1)}, f32[1,256,128]{2,1,0:T(8,128)S(1)}, u32[]{:S(2)}, u32[]{:S(2)}) collective-permute-start(f32[1,256,128]{2,1,0:T(8,128)S(1)} %beside.7), channel_id=1, source_target_pairs={{0,8},{8,0},{16,24},{24,16},{1,9},{9,1},{17,25},{25,17},{2,10},{10... | collective-permute-start | bytes 393224 | tf_op jit(solution)/shard_map/ppermute | solution.py:344
  322.4 11.6 %collective-permute-start.135 = (f32[256,128]{1,0:T(8,128)S(1)}, f32[256,128]{1,0:T(8,128)S(1)}, u32[]{:S(2)}, u32[]{:S(2)}) collective-permute-start(f32[256,128]{1,0:T(8,128)S(1)} %get-tuple-element.268), channel_id=1, source_target_pairs={{0,4},{1,3},{2,6},{3,1},{4,0},{5,7},{6,2},{7,5},{8,12},{9,11},{10,... | collective-permute-start | bytes 393224 | tf_op jit(solution)/shard_map/ppermute | solution.py:341
  323.2 10.8 %collective-permute-start.136 = (f32[256,128]{1,0:T(8,128)S(1)}, f32[256,128]{1,0:T(8,128)S(1)}, u32[]{:S(2)}, u32[]{:S(2)}) collective-permute-start(f32[256,128]{1,0:T(8,128)S(1)} %get-tuple-element.267), channel_id=1, source_target_pairs={{0,6},{1,5},{2,4},{3,7},{4,2},{5,1},{6,0},{7,3},{8,14},{9,13},{10,... | collective-permute-start | bytes 393224 | tf_op jit(solution)/shard_map/ppermute | solution.py:341
  335.0 10.3 %collective-permute-start.137 = (f32[256,128]{1,0:T(8,128)S(1)}, f32[256,128]{1,0:T(8,128)S(1)}, u32[]{:S(2)}, u32[]{:S(2)}) collective-permute-start(f32[256,128]{1,0:T(8,128)S(1)} %fusion.2.refs_0_), channel_id=1, source_target_pairs={{0,2},{1,7},{2,0},{3,5},{4,6},{5,3},{6,4},{7,1},{8,10},{9,15},{10,... | collective-permute-start | bytes 393224 | tf_op jit(solution)/shard_map/ppermute | solution.py:341
  338.2 10.6 %collective-permute-start.139 = (f32[256,128]{1,0:T(8,128)S(1)}, f32[256,128]{1,0:T(8,128)S(1)}, u32[]{:S(2)}, u32[]{:S(2)}) collective-permute-start(f32[256,128]{1,0:T(8,128)S(1)} %fusion.2.refs_0_), channel_id=1, source_target_pairs={{0,6},{1,5},{2,4},{3,7},{4,2},{5,1},{6,0},{7,3},{8,14},{9,13},{10,... | collective-permute-start | bytes 393224 | tf_op jit(solution)/shard_map/ppermute | solution.py:341
  (142 other events, 1214.3 us)
